TPU v7x, 128 devices: a whole 4x4x4 slice. The times are simulated.
128 devices in a mesh: dp: 16 (over y, x), tensor: 8 (over z, core).
Axes of the slice: x: 4, y: 4, z: 4, core: 2. Of those that a mesh axis runs over, the one named last changes fastest.
Arguments:
- pre_norm: bfloat16 [4096, 4096], P(('dp', 'tensor')), may hold values from -140 to 140
- out_grad: bfloat16 [4096, 4096], P(('dp', 'tensor')), may hold values from -6 to 6
- routes: int32 [4096, 8], P(('dp', 'tensor')), may hold values from 0 to 63, all different within a row; in each aligned block of 32 rows (0 to 31, 32 to 63, ...) at most 6 rows name the same one
- gate_probs: float32 [4096, 8], P(('dp', 'tensor')), may hold values from 0 to 1, as said below
- norm_gain: float32 [4096], replicated, may hold values from 0.5 to 1.5
- router_weight: bfloat16 [4096, 64], replicated, may hold values from -0.09375 to 0.09375
- w_gate: bfloat16 [128, 4096, 768], P(('dp', 'tensor')), may hold values from -0.09375 to 0.09375
- w_up: bfloat16 [128, 4096, 768], P(('dp', 'tensor')), may hold values from -0.09375 to 0.09375
- w_down: bfloat16 [128, 768, 4096], P(('dp', 'tensor')), may hold values from -0.15625 to 0.15625
- context: bfloat16 [4096, 8192], P('dp', 'tensor'), may hold values from -6 to 6
- out_weight: bfloat16 [4096, 8192], P('dp', 'tensor'), may hold values from -0.0625 to 0.0625
Outputs:
- residual_grad: bfloat16 [4096, 4096], P(('dp', 'tensor'))
- gate_grad: float32 [4096, 8], P(('dp', 'tensor'))
- router_grad: float32 [4096, 64], P('tensor')
- gain_grad: float32 [4096], P('tensor')
- context_grad: bfloat16 [4096, 8192], P('dp', 'tensor')
- weight_grad: bfloat16 [4096, 8192], P('dp', 'tensor')
Inputs may be any that keep to these rules, and one draw needn't show every extreme that they name: `routes`: each row names 8 different experts; among the 32 tokens of one device (aligned blocks) no expert is named more than 6 times, a bound that some block reaches. `gate_probs`: each row is positive and sums to one.
All inputs are finite; a program needn't handle non-finite values.
Results may differ from a plain program's by a relative error of at most 0.019.
Values may be sent and summed in bfloat16 or wider, within the bound.
No kernel may reach another device: no remote copies, remote signals or barrier semaphores. Data moves between devices by JAX's collectives and lax.ppermute only.
A program may use at most 192 MiB of HBM per device.

v0:
```python
import jax
import jax.numpy as jnp
from jax import lax
from jax.sharding import PartitionSpec as P


def expert_rows(token_in, grad_in, gate_mat, up_mat, down_mat):
    leading = token_in.shape[:-1]
    features = token_in.shape[-1]
    token_rows = token_in.reshape(-1, features)
    grad_rows = grad_in.reshape(-1, features)
    gate_pre = jnp.dot(token_rows, gate_mat, preferred_element_type=jnp.float32)
    up_pre = jnp.dot(token_rows, up_mat, preferred_element_type=jnp.float32)
    upstream = lax.dot_general(
        grad_rows, down_mat, (((1,), (1,)), ((), ())), preferred_element_type=jnp.float32
    )
    gate_sig = jax.nn.sigmoid(gate_pre)
    activation = gate_pre * gate_sig * up_pre
    partial_value = jnp.sum(activation * upstream, axis=-1).astype(jnp.bfloat16)
    grad_up = (upstream * gate_pre * gate_sig).astype(jnp.bfloat16)
    grad_gate = (upstream * up_pre * gate_sig * (1.0 + gate_pre * (1.0 - gate_sig))).astype(
        jnp.bfloat16
    )
    back_rows = lax.dot_general(
        grad_gate, gate_mat, (((1,), (1,)), ((), ())), preferred_element_type=jnp.float32
    )
    back_rows = back_rows + lax.dot_general(
        grad_up, up_mat, (((1,), (1,)), ((), ())), preferred_element_type=jnp.float32
    )
    return (
        back_rows.astype(jnp.bfloat16).reshape(leading + (features,)),
        partial_value.reshape(leading),
    )


def shards(
    pre_norm,
    out_grad,
    routes,
    gate_probs,
    norm_gain,
    router_weight,
    w_gate,
    w_up,
    w_down,
    context,
    out_weight,
):
    devices = lax.axis_size(("dp", "tensor"))
    tok_rows, features = pre_norm.shape
    chosen_count = routes.shape[1]
    experts = router_weight.shape[1]
    halves = devices // experts
    capacity = tok_rows * chosen_count * 3 // (2 * experts)
    slot_count = tok_rows * chosen_count
    hidden = pre_norm.astype(jnp.float32)
    inverse = lax.rsqrt(jnp.mean(hidden * hidden, axis=-1, keepdims=True) + 1e-06)
    normed = (hidden * inverse * norm_gain).astype(jnp.bfloat16)
    flat_route = routes.reshape(slot_count)
    matches = (flat_route[:, None] == jnp.arange(experts, dtype=jnp.int32)[None, :]).astype(
        jnp.int32
    )
    before = jnp.cumsum(matches, axis=0) - matches
    position = jnp.sum(before * matches, axis=1)
    target = flat_route * capacity + position
    placing = (jnp.arange(experts * capacity, dtype=jnp.int32)[:, None] == target[None, :]).astype(
        jnp.float32
    )
    per_token = (
        placing.reshape(experts * capacity, tok_rows, chosen_count).sum(-1).astype(jnp.bfloat16)
    )
    send_tokens = jnp.dot(per_token, normed, preferred_element_type=jnp.float32).astype(
        jnp.bfloat16
    )
    send_grads = jnp.dot(per_token, out_grad, preferred_element_type=jnp.float32).astype(
        jnp.bfloat16
    )
    send_tokens = jnp.broadcast_to(
        send_tokens.reshape(experts, 1, capacity, features), (experts, halves, capacity, features)
    ).reshape(devices, capacity, features)
    send_grads = jnp.broadcast_to(
        send_grads.reshape(experts, 1, capacity, features), (experts, halves, capacity, features)
    ).reshape(devices, capacity, features)
    gate_mat = w_gate[0]
    up_mat = w_up[0]
    down_mat = w_down[0]
    back_rows, partial_value = expert_rows(
        lax.all_to_all(send_tokens, ("dp", "tensor"), split_axis=0, concat_axis=0, tiled=True),
        lax.all_to_all(send_grads, ("dp", "tensor"), split_axis=0, concat_axis=0, tiled=True),
        gate_mat,
        up_mat,
        down_mat,
    )
    back_term = lax.all_to_all(back_rows, ("dp", "tensor"), split_axis=0, concat_axis=0, tiled=True)
    back_part = lax.all_to_all(
        partial_value, ("dp", "tensor"), split_axis=0, concat_axis=0, tiled=True
    )
    term_sum = (
        back_term.reshape(experts, halves, capacity, features)
        .astype(jnp.float32)
        .sum(1)
        .reshape(experts * capacity, features)
    )
    part_sum = (
        back_part.reshape(experts, halves, capacity)
        .astype(jnp.float32)
        .sum(1)
        .reshape(experts * capacity)
    )
    flat_gate = gate_probs.reshape(slot_count)
    mixing = (
        (placing * flat_gate[None, :]).reshape(experts * capacity, tok_rows, chosen_count).sum(-1)
    )
    expert_grad = lax.dot_general(
        mixing,
        term_sum,
        (((0,), (0,)), ((), ())),
        precision=lax.Precision.HIGHEST,
        preferred_element_type=jnp.float32,
    )
    gate_grad = jnp.dot(
        part_sum, placing, precision=lax.Precision.HIGHEST, preferred_element_type=jnp.float32
    ).reshape(tok_rows, chosen_count)
    weighted = jnp.sum(gate_probs * gate_grad, axis=-1, keepdims=True)
    logit_grad = (gate_probs * (gate_grad - weighted)).astype(jnp.bfloat16)
    table = matches.reshape(tok_rows, chosen_count, experts).astype(jnp.float32)
    logit_full = jnp.sum(logit_grad.astype(jnp.float32)[:, :, None] * table, axis=1).astype(
        jnp.bfloat16
    )
    router_term = lax.dot_general(
        logit_full, router_weight, (((1,), (1,)), ((), ())), preferred_element_type=jnp.float32
    )
    normed_grad = expert_grad + router_term
    router_part = lax.dot_general(
        normed, logit_full, (((0,), (0,)), ((), ())), preferred_element_type=jnp.float32
    )
    gain_part = jnp.sum(normed_grad * hidden * inverse, axis=0)
    router_all, gain_all = lax.psum((router_part, gain_part), ("dp", "tensor"))
    band_rows = features // lax.axis_size("tensor")
    offset = lax.axis_index("tensor") * band_rows
    router_grad = lax.dynamic_slice_in_dim(router_all, offset, band_rows, 0)
    gain_grad = lax.dynamic_slice_in_dim(gain_all, offset, band_rows, 0)
    scaled = norm_gain * normed_grad
    cubed = inverse * inverse * inverse
    residual_grad = (
        out_grad.astype(jnp.float32)
        + inverse * scaled
        - hidden * cubed * jnp.mean(hidden * scaled, axis=-1, keepdims=True)
    ).astype(jnp.bfloat16)
    gathered = lax.all_gather(residual_grad, "tensor", axis=0, tiled=True)
    columns = gathered
    context_grad = jnp.dot(
        columns,
        lax.all_gather(out_weight, "dp", axis=0, tiled=True),
        preferred_element_type=jnp.float32,
    ).astype(jnp.bfloat16)
    columns = gathered
    weight_grad = lax.psum_scatter(
        lax.dot_general(
            columns, context, (((0,), (0,)), ((), ())), preferred_element_type=jnp.float32
        ).astype(jnp.bfloat16),
        "dp",
        scatter_dimension=0,
        tiled=True,
    )
    return (residual_grad, gate_grad, router_grad, gain_grad, context_grad, weight_grad)


def solution(mesh):
    placed = (
        P(("dp", "tensor"), None),
        P(("dp", "tensor"), None),
        P(("dp", "tensor"), None),
        P(("dp", "tensor"), None),
        P(),
        P(),
        P(("dp", "tensor"), None, None),
        P(("dp", "tensor"), None, None),
        P(("dp", "tensor"), None, None),
        P("dp", "tensor"),
        P("dp", "tensor"),
    )
    return jax.shard_map(
        shards,
        mesh=mesh,
        in_specs=placed,
        out_specs=(
            P(("dp", "tensor"), None),
            P(("dp", "tensor"), None),
            P("tensor", None),
            P("tensor"),
            P("dp", "tensor"),
            P("dp", "tensor"),
        ),
        check_vma=False,
    )
```

profile of v0, /device:TPU:0, one launch (start us, length us, event | category | flops | bytes accessed | tf_op | source)
XLA Modules:
  0.0 722.7 jit_solution(15467889700793272001)
XLA Ops:
  8.0 0.0 copy-start
  8.0 0.8 copy.36
  8.8 0.1 eq.67
  8.9 0.1 eq.63
  9.0 0.6 reduce-window.6
  9.6 0.2 slice_reduce_fusion
  9.9 0.1 fusion.29
  10.0 0.1 reduce_sum.103
  10.1 0.8 copy.40
  10.8 1.1 fusion.11
  12.0 0.3 convert_reduce_fusion.1
  12.3 3.7 convolution_convert_fusion.1
  15.9 5.6 broadcast_in_dim.10
  21.6 6.5 broadcast_in_dim.11
  28.1 11.7 %all-to-all-start.1 = ((bf16[128,6,4096]{2,1,0:T(8,128)(2,1)}), bf16[128,6,4096]{2,1,0:T(8,128)(2,1)}, u32[]{:S(2)}, u32[]{:S(2)}) async-start(bf16[128,6,4096]{2,1,0:T(8,128)(2,1)} %bitcast.63), calls=%async_computation.1 | async-start | bytes 16777216 | tf_op jit(solution)/shard_map/all_to_all | solution.py:88
  39.8 0.0 copy-done.4
  39.8 2.7 convolution_convert_fusion.2
  42.4 5.7 broadcast_in_dim.8
  48.1 91.8 %all-to-all-done.1 = bf16[128,6,4096]{2,1,0:T(8,128)(2,1)} async-done(((bf16[128,6,4096]{2,1,0:T(8,128)(2,1)}), bf16[128,6,4096]{2,1,0:T(8,128)(2,1)}, u32[]{:S(2)}, u32[]{:S(2)}) %all-to-all-start.1) | async-done | bytes 6291488 | tf_op jit(solution)/shard_map/all_to_all | solution.py:88
  139.9 6.5 broadcast_in_dim.9
  146.4 10.2 %all-to-all-start = ((bf16[128,6,4096]{2,1,0:T(8,128)(2,1)}), bf16[128,6,4096]{2,1,0:T(8,128)(2,1)}, u32[]{:S(2)}, u32[]{:S(2)}) async-start(bf16[128,6,4096]{2,1,0:T(8,128)(2,1)} %bitcast.62), calls=%async_computation | async-start | bytes 16777216 | tf_op jit(solution)/shard_map/all_to_all | solution.py:89
  156.6 10.2 %reshape.170 = bf16[768,4096]{1,0:T(8,128)(2,1)} reshape(bf16[128,6,4096]{2,1,0:T(8,128)(2,1)} %all-to-all-done.1) | data formatting | bytes 12582912 | tf_op jit(solution)/shard_map/reshape | solution.py:10
  166.8 9.8 %fusion.2 = f32[768,768]{0,1:T(8,128)S(1)} fusion(bf16[768,4096]{1,0:T(8,128)(2,1)} %reshape.170, bf16[1,4096,768]{2,1,0:T(8,128)(2,1)} %param.17), kind=kOutput, calls=%fused_computation.5 | convolution fusion | flops 4831838208 | bytes 14942208 | tf_op jit(solution)/shard_map/dot_general | solution.py:12
  176.6 0.0 copy-done.2
  176.6 8.7 %fusion.5 = f32[768,768]{0,1:T(8,128)} fusion(bf16[768,4096]{1,0:T(8,128)(2,1)S(1)} %copy-done.2, bf16[1,4096,768]{2,1,0:T(8,128)(2,1)} %param.18), kind=kOutput, calls=%fused_computation.8 | convolution fusion | flops 4831838208 | bytes 14942208 | tf_op jit(solution)/shard_map/dot_general | solution.py:13
  185.2 70.9 %all-to-all-done = bf16[128,6,4096]{2,1,0:T(8,128)(2,1)} async-done(((bf16[128,6,4096]{2,1,0:T(8,128)(2,1)}), bf16[128,6,4096]{2,1,0:T(8,128)(2,1)}, u32[]{:S(2)}, u32[]{:S(2)}) %all-to-all-start) | async-done | bytes 6291488 | tf_op jit(solution)/shard_map/all_to_all | solution.py:89
  256.1 10.3 %reshape.168 = bf16[768,4096]{1,0:T(8,128)(2,1)} reshape(bf16[128,6,4096]{2,1,0:T(8,128)(2,1)} %all-to-all-done) | data formatting | bytes 12582912 | tf_op jit(solution)/shard_map/reshape | solution.py:11
  266.4 10.5 %multiply_reduce_fusion = (bf16[768]{0:T(1024)(128)(2,1)S(1)}, f32[768,768]{0,1:T(8,128)}) fusion(f32[768,768]{0,1:T(8,128)} %fusion.5, f32[768,768]{0,1:T(8,128)S(1)} %fusion.2, bf16[768,4096]{1,0:T(8,128)(2,1)} %reshape.168, bf16[1,768,4096]{2,1,0:T(8,128)(2,1)} %param.19), kind=kOutput, calls=%fused_computation.15 | convolution fusion | flops 4835965952 | bytes 19662336 | tf_op jit(solution)/shard_map/dot_general | solution.py:14
  276.9 0.8 convert_element_type.119
  277.7 11.4 %all-to-all-start.3 = ((bf16[128,1,6]{2,1,0:T(2,128)(2,1)}), bf16[128,1,6]{2,1,0:T(2,128)(2,1)S(1)}, u32[]{:S(2)}, u32[]{:S(2)}) async-start(bf16[128,1,6]{2,1,0:T(2,128)(2,1)} %convert_element_type.119), calls=%async_computation.3 | async-start | bytes 131072 | tf_op jit(solution)/shard_map/all_to_all | solution.py:95
  289.0 12.7 %fusion = f32[768,4096]{1,0:T(8,128)} fusion(bf16[1,4096,768]{2,1,0:T(8,128)(2,1)} %param.17, f32[768,768]{0,1:T(8,128)S(1)} %fusion.2, f32[768,768]{0,1:T(8,128)} %get-tuple-element.13, f32[768,768]{0,1:T(8,128)} %fusion.5), kind=kOutput, calls=%fused_computation.3 | convolution fusion | flops 4837736448 | bytes 25952256 | tf_op jit(solution)/shard_map/dot_general | solution.py:24
  301.8 11.7 %add_convert_fusion = bf16[768,4096]{1,0:T(8,128)(2,1)} fusion(f32[768,4096]{1,0:T(8,128)} %fusion, bf16[1,4096,768]{2,1,0:T(8,128)(2,1)} %param.18, f32[768,768]{0,1:T(8,128)S(1)} %copy-done.9, f32[768,768]{0,1:T(8,128)S(1)} %fusion.2), kind=kOutput, calls=%fused_computation.1 | convolution fusion | flops 4841668608 | bytes 29884416 | tf_op jit(solution)/shard_map/dot_general | solution.py:27
  313.5 10.1 %reshape.171 = bf16[128,6,4096]{2,1,0:T(8,128)(2,1)} reshape(bf16[768,4096]{1,0:T(8,128)(2,1)} %add_convert_fusion) | data formatting | bytes 12582912 | tf_op jit(solution)/shard_map/reshape | solution.py:31
  323.6 0.0 all-to-all-done.3
  323.6 10.1 %all-to-all-start.2 = ((bf16[128,6,4096]{2,1,0:T(8,128)(2,1)}), bf16[128,6,4096]{2,1,0:T(8,128)(2,1)}, u32[]{:S(2)}, u32[]{:S(2)}) async-start(bf16[128,6,4096]{2,1,0:T(8,128)(2,1)} %reshape.171), calls=%async_computation.2 | async-start | bytes 16777216 | tf_op jit(solution)/shard_map/all_to_all | solution.py:94
  333.7 0.3 all-gather.3.cloned.1.call-start
  334.0 0.1 convert_element_type.118
  334.1 0.1 reduce_sum.108
  334.2 0.1 reshape.176
  334.3 1.9 fusion.21
  336.3 0.1 copy.44
  336.4 0.1 copy.42
  336.4 0.2 multiply_reduce_fusion.1
  336.6 97.3 %all-to-all-done.2 = bf16[128,6,4096]{2,1,0:T(8,128)(2,1)} async-done(((bf16[128,6,4096]{2,1,0:T(8,128)(2,1)}), bf16[128,6,4096]{2,1,0:T(8,128)(2,1)}, u32[]{:S(2)}, u32[]{:S(2)}) %all-to-all-start.2) | async-done | bytes 6291488 | tf_op jit(solution)/shard_map/all_to_all | solution.py:94
  433.9 9.6 %convert_reduce_fusion = f32[64,6,4096]{2,1,0:T(8,128)} fusion(bf16[128,6,4096]{2,1,0:T(8,128)(2,1)} %all-to-all-done.2), kind=kLoop, calls=%fused_computation | loop fusion | flops 4718592 | bytes 12582912 | tf_op jit(solution)/shard_map/reduce_sum | solution.py:101
  443.4 7.8 %reshape.172 = f32[384,4096]{1,0:T(8,128)} reshape(f32[64,6,4096]{2,1,0:T(8,128)} %convert_reduce_fusion) | data formatting | bytes 12582912 | tf_op jit(solution)/shard_map/reshape | solution.py:102
  451.2 5.7 fusion.38
  457.0 0.4 fusion.19
  457.4 0.9 fusion.16
  458.3 0.0 all-gather.3.cloned.1.call-update
  458.3 0.0 all-reduce.2.cloned.1.call-start
  458.4 1.4 fusion.24
  459.7 0.0 all-reduce.2.cloned.1.call-update
  459.8 0.0 all-gather.5.cloned.1.call-start
  459.8 0.7 all-gather.5.cloned.1.call-update
  460.5 0.0 reduce-scatter.2.cloned.1.call-start
  460.6 24.2 %all-gather.3.cloned.1.call-done = bf16[256,4096]{1,0:T(8,128)(2,1)} async-done(((bf16[32,4096]{1,0:T(8,128)(2,1)}), bf16[256,4096]{1,0:T(8,128)(2,1)}) %all-gather.3.cloned.1.call-update) | async-done | bytes 2097168 | tf_op jit(solution)/shard_map/all_gather | solution.py:150
  484.8 7.2 convolution_convert_fusion
  492.0 0.0 reduce-scatter.2.cloned.1.call-update
  492.0 148.1 %all-reduce.2.cloned.1.call-done = f32[4096,64]{0,1:T(8,128)} async-done(((f32[4096,64]{0,1:T(8,128)}), f32[4096,64]{0,1:T(8,128)}) %all-reduce.2.cloned.1.call-update) | async-done | bytes 1048592 | tf_op jit(solution)/shard_map/psum | solution.py:138
  640.1 1.6 constant_dynamic-slice_fusion
  641.6 66.8 %psum.15 = f32[4096]{0:T(1024)S(1)} all-reduce(f32[4096]{0:T(1024)S(1)} %get-tuple-element.6), channel_id=1, replica_groups=mesh['dp'=16,'tensor'=8] {'dp','tensor'}, use_global_device_ids=true, to_apply=%region_14.15 | all-reduce | flops 4096 | bytes 32768 | tf_op jit(solution)/shard_map/psum | solution.py:138
  708.4 0.7 dynamic_slice.7
  709.1 6.5 convolution_convert_fusion.3
  (28 shorter events, 0.2 us)
Async XLA Ops:
  8.0 476.8 %copy-start = (bf16[256,1024]{1,0:T(8,128)(2,1)S(1)}, bf16[256,1024]{1,0:T(8,128)(2,1)}, u32[]{:S(2)}) copy-start(bf16[256,1024]{1,0:T(8,128)(2,1)} %param.20) | copy-start | bytes 1572868
  28.1 11.7 %copy-start.4 = (bf16[32,4096]{1,0:T(8,128)(2,1)S(1)}, bf16[32,4096]{1,0:T(8,128)(2,1)}, u32[]{:S(2)}) copy-start(bf16[32,4096]{1,0:T(8,128)(2,1)} %param.12) | copy-start | bytes 786436
  28.1 111.8 %all-to-all-start.1 = ((bf16[128,6,4096]{2,1,0:T(8,128)(2,1)}), bf16[128,6,4096]{2,1,0:T(8,128)(2,1)}, u32[]{:S(2)}, u32[]{:S(2)}) async-start(bf16[128,6,4096]{2,1,0:T(8,128)(2,1)} %bitcast.63), calls=%async_computation.1 | async-start | bytes 16777216 | tf_op jit(solution)/shard_map/all_to_all | solution.py:88
  146.4 109.7 %all-to-all-start = ((bf16[128,6,4096]{2,1,0:T(8,128)(2,1)}), bf16[128,6,4096]{2,1,0:T(8,128)(2,1)}, u32[]{:S(2)}, u32[]{:S(2)}) async-start(bf16[128,6,4096]{2,1,0:T(8,128)(2,1)} %bitcast.62), calls=%async_computation | async-start | bytes 16777216 | tf_op jit(solution)/shard_map/all_to_all | solution.py:89
  166.8 9.8 %copy-start.2 = (bf16[768,4096]{1,0:T(8,128)(2,1)S(1)}, bf16[768,4096]{1,0:T(8,128)(2,1)}, u32[]{:S(2)}) copy-start(bf16[768,4096]{1,0:T(8,128)(2,1)} %reshape.170) | copy-start | bytes 18874372
  277.7 46.0 %all-to-all-start.3 = ((bf16[128,1,6]{2,1,0:T(2,128)(2,1)}), bf16[128,1,6]{2,1,0:T(2,128)(2,1)S(1)}, u32[]{:S(2)}, u32[]{:S(2)}) async-start(bf16[128,1,6]{2,1,0:T(2,128)(2,1)} %convert_element_type.119), calls=%async_computation.3 | async-start | bytes 131072 | tf_op jit(solution)/shard_map/all_to_all | solution.py:95
  289.0 12.8 %copy-start.9 = (f32[768,768]{0,1:T(8,128)S(1)}, f32[768,768]{0,1:T(8,128)}, u32[]{:S(2)}) copy-start(f32[768,768]{0,1:T(8,128)} %get-tuple-element.13) | copy-start | bytes 7077892
  323.6 12.7 %copy-start.7 = (f32[32,8]{0,1:T(8,128)S(1)}, f32[32,8]{0,1:T(8,128)}, u32[]{:S(2)}) copy-start(f32[32,8]{0,1:T(8,128)} %param.14) | copy-start | bytes 3076
  323.6 110.2 %all-to-all-start.2 = ((bf16[128,6,4096]{2,1,0:T(8,128)(2,1)}), bf16[128,6,4096]{2,1,0:T(8,128)(2,1)}, u32[]{:S(2)}, u32[]{:S(2)}) async-start(bf16[128,6,4096]{2,1,0:T(8,128)(2,1)} %reshape.171), calls=%async_computation.2 | async-start | bytes 16777216 | tf_op jit(solution)/shard_map/all_to_all | solution.py:94
  333.7 151.0 %all-gather.3.cloned.1.call-start = ((), (), s32[]{:S(2)}) async-start(), calls=%async_computation.6 | async-start | bytes 2359296 | tf_op jit(solution)/shard_map/all_gather | solution.py:150
  336.3 107.1 %copy-start.8 = (f32[1,32,8]{1,2,0:T(8,128)}, f32[1,32,8]{1,2,0:T(8,128)S(1)}, u32[]{:S(2)}) copy-start(f32[1,32,8]{1,2,0:T(8,128)S(1)} %copy.44) | copy-start | bytes 3076
  451.2 5.7 copy-start.1
  451.2 5.7 copy-start.5
  451.2 5.7 copy-start.6
  458.3 181.7 %all-reduce.2.cloned.1.call-start = ((), (), s32[]{:S(2)}) async-start(), calls=%async_computation.5 | async-start | bytes 2097152 | tf_op jit(solution)/shard_map/psum | solution.py:138
  459.8 249.3 %all-gather.5.cloned.1.call-start = ((), (), s32[]{:S(2)}) async-start(), calls=%async_computation.7 | async-start | bytes 8912896 | tf_op jit(solution)/shard_map/all_gather | solution.py:154
  460.5 255.1 %reduce-scatter.2.cloned.1.call-start = ((), (), s32[]{:S(2)}) async-start(), calls=%async_computation.8 | async-start | bytes 8912896 | tf_op jit(solution)/shard_map/reduce_scatter | solution.py:158
  492.0 217.1 %copy-start.3 = (bf16[256,4096]{1,0:T(8,128)(2,1)S(1)}, bf16[256,4096]{1,0:T(8,128)(2,1)}, u32[]{:S(2)}) copy-start(bf16[256,4096]{1,0:T(8,128)(2,1)} %all-gather.3.cloned.1.call-done) | copy-start | bytes 6291460
Sparse Core Ops, SparseCore 0:
  458.5 26.2 all-gather.2
  487.1 71.3 all-gather.4
  562.9 84.8 reduce-scatter.1
Sparse Core Ops, SparseCore 1:
  463.6 176.4 all-reduce.1
where the time goes:
time: 725 us; the launch traced here: 723 us
  waiting for transfers between devices  433 us (60%)
  matrix products  82.8 us (11%)
  local copies, waits for them, and re-layouts  68 us (9%)
  blocking collectives  66.8 us (9%)
  starting transfers between devices  43.7 us (6%)
  between operations  15.4 us (2%)
  other arithmetic  13.1 us (2%)
    psum x1, waiting for transfers between devices, shards(): router_all, gain_all = lax.psum((router_part, gain_part), ('dp', 'tensor'))  148 us
    all_to_all x1, waiting for transfers between devices, shards(): lax.all_to_all(back_rows, ('dp', 'tensor'), split_axis=0, concat_axis=0,...  97.3 us
    all_to_all x1, waiting for transfers between devices, shards(): lax.all_to_all(send_tokens, ('dp', 'tensor'), split_axis=0, concat_axis=0...  91.8 us
    all_to_all x1, waiting for transfers between devices, shards(): lax.all_to_all(send_grads, ('dp', 'tensor'), split_axis=0, concat_axis=0,...  70.9 us
    psum x1, blocking collectives, shards(): router_all, gain_all = lax.psum((router_part, gain_part), ('dp', 'tensor'))  66.8 us
    all_gather x1, waiting for transfers between devices, shards(): gathered = lax.all_gather(residual_grad, 'tensor', axis=0, tiled=True)  24.2 us
  transfers between devices with their start and end apart: 8, of which 5 were waited for; matrix products, arithmetic and copies ran while one was open for 13% of the time, Pallas kernels for 0%

commit v1 on v0

v1 whole, which is shorter than its diff:
```python
import functools

import jax
import jax.numpy as jnp
import numpy as np
from jax import lax
from jax.experimental import pallas as pl
from jax.experimental.pallas import tpu as pltpu
from jax.sharding import Mesh, PartitionSpec as P

CHIP = ("y", "x", "z")
EVERY = ("y", "x", "z", "core")
DP = ("y", "x")
TENSOR = ("z", "core")
SWAP = [(0, 1), (1, 0)]
WIDE = 512
SOME = 8
MIB = 1024 * 1024
bf16 = jnp.bfloat16
f32 = jnp.float32
OVER_ROWS = (((0,), (0,)), ((), ()))
OVER_LAST = (((1,), (1,)), ((), ()))


def swap_cores(value):
    return lax.ppermute(value, "core", SWAP)


def exchange(value, axes):
    return lax.all_to_all(value, axes, split_axis=0, concat_axis=0, tiled=True)


def pair_sum(value, axis):
    size = lax.axis_size(axis)
    for mask in (1, 3)[: size // 2]:
        value = value + lax.ppermute(value, axis, [(i, i ^ mask) for i in range(size)])
    return value


def ring_scatter(first, blocks, axis):
    size = lax.axis_size(axis)
    right = [(i, (i + 1) % size) for i in range(size)]
    left = [(i, (i - 1) % size) for i in range(size)]
    half = first.shape[0] // 2
    from_left = lax.ppermute(first[:half], axis, right)
    from_right = lax.ppermute(first[half:], axis, left)
    mine, after, before = blocks

    def joined(upper, lower, block):
        block = block.astype(f32)
        return jnp.concatenate([block[:half] + upper, block[half:] + lower], axis=0).astype(bf16)

    to_right = joined(from_left.astype(f32), 0.0, after)
    to_left = joined(0.0, from_right.astype(f32), before)
    got_left = lax.ppermute(to_right, axis, right)
    got_right = lax.ppermute(to_left, axis, left)
    return (mine.astype(f32) + got_left.astype(f32) + got_right.astype(f32)).astype(bf16)


def params(grid=0, mib=16):
    return pltpu.CompilerParams(
        vmem_limit_bytes=mib * MIB,
        dimension_semantics=("arbitrary",) * grid if grid else None,
    )


def slot_codes(routes_wide, experts, pieces, tok_rows):
    columns = pieces * tok_rows
    expert = lax.broadcasted_iota(jnp.int32, (experts, columns), 0)
    named = expert == routes_wide[0:1, :]
    for choice in range(1, routes_wide.shape[0]):
        named = named | (expert == routes_wide[choice : choice + 1, :])
    before = lax.broadcasted_iota(jnp.int32, (columns, columns), 0)
    after = lax.broadcasted_iota(jnp.int32, (columns, columns), 1)
    earlier = (before // tok_rows == after // tok_rows) & (before < after)
    rank = jnp.dot(
        jnp.where(named, 1.0, 0.0).astype(bf16),
        jnp.where(earlier, 1.0, 0.0).astype(bf16),
        preferred_element_type=f32,
    )
    piece = (lax.broadcasted_iota(jnp.int32, (experts, columns), 1) // tok_rows).astype(f32)
    return jnp.where(named, piece * 8.0 + rank, -1.0)


def row_codes(shape, capacity, block, dim):
    row = lax.broadcasted_iota(jnp.int32, shape, dim) % block
    return ((row // capacity) * 8 + row % capacity).astype(f32)


def place_kernel(
    capacity, pre_ref, grad_ref, gain_ref, routes_ref, send_ref, code_ref, normed_ref, source
):
    tok_rows, features = pre_ref.shape
    experts, columns = code_ref.shape
    pieces = features // WIDE
    block = pieces * capacity
    hidden = pre_ref[...].astype(f32)
    inverse = lax.rsqrt(jnp.mean(hidden * hidden, axis=-1, keepdims=True) + 1e-06)
    normed = (hidden * inverse * gain_ref[...]).astype(bf16)
    normed_ref[...] = normed
    for piece in range(pieces):
        at = pl.ds(piece * tok_rows, tok_rows)
        source[at, :WIDE] = normed[:, piece * WIDE : (piece + 1) * WIDE]
        source[at, WIDE:] = grad_ref[:, piece * WIDE : (piece + 1) * WIDE]
    code_ref[...] = slot_codes(routes_ref[...], experts, pieces, tok_rows)
    some = 8
    rows = some * block

    def step(group, carry):
        first = pl.multiple_of(group * some, some)
        code = code_ref[pl.ds(first, some), :]
        want = row_codes((some, block, columns), capacity, block, 1)
        hit = jnp.where(code[:, None, :] == want, 1.0, 0.0).astype(bf16).reshape(rows, columns)
        moved = jnp.dot(hit, source[...], preferred_element_type=f32).astype(bf16)
        send_ref[pl.ds(first, some), :block, :] = moved[:, :WIDE].reshape(some, block, WIDE)
        send_ref[pl.ds(first, some), block:, :] = moved[:, WIDE:].reshape(some, block, WIDE)
        return carry

    lax.fori_loop(0, experts // some, step, 0)


def place(pre_norm, out_grad, norm_gain, routes_wide, experts, capacity):
    tok_rows, features = pre_norm.shape
    pieces = features // WIDE
    block = pieces * capacity
    return pl.pallas_call(
        functools.partial(place_kernel, capacity),
        out_shape=(
            jax.ShapeDtypeStruct((experts, 2 * block, WIDE), bf16),
            jax.ShapeDtypeStruct((experts, pieces * tok_rows), f32),
            jax.ShapeDtypeStruct((tok_rows, features), bf16),
        ),
        scratch_shapes=[pltpu.VMEM((pieces * tok_rows, 2 * WIDE), bf16)],
        compiler_params=params(0, 24),
        name="place",
    )(pre_norm, out_grad, norm_gain, routes_wide)


def order_matrix(capacity, block):
    span = SOME * block
    to = lax.broadcasted_iota(jnp.int32, (span, span), 0)
    at = lax.broadcasted_iota(jnp.int32, (span, span), 1)
    moved = (at % block) // capacity * (SOME * capacity) + at // block * capacity + at % capacity
    return jnp.where(moved == to, 1.0, 0.0).astype(bf16)


def spread_kernel(capacity, got_ref, order_ref, rows_ref):
    some, block, _ = got_ref.shape
    pieces = block // capacity
    span = some * capacity
    source = got_ref[...].reshape(some * block, WIDE)
    moved = jnp.dot(order_ref[...], source, preferred_element_type=f32).astype(bf16)
    for piece in range(pieces):
        rows_ref[:, piece * WIDE : (piece + 1) * WIDE] = moved[piece * span : (piece + 1) * span]


def spread(got, kind, order, capacity):
    sources, double, _ = got.shape
    block = double // 2
    features = block // capacity * WIDE
    span = SOME * capacity
    return pl.pallas_call(
        functools.partial(spread_kernel, capacity),
        grid=(sources // SOME,),
        in_specs=[
            pl.BlockSpec((SOME, block, WIDE), lambda i: (i, kind, 0)),
            pl.BlockSpec(order.shape, lambda i: (0, 0)),
        ],
        out_specs=pl.BlockSpec((span, features), lambda i: (i, 0)),
        out_shape=jax.ShapeDtypeStruct((sources * capacity, features), bf16),
        compiler_params=params(1),
        name="spread",
    )(got, order)


def forward_kernel(own_ref, other_ref, gate_ref, up_ref, gate_pre_ref, up_pre_ref):
    count = own_ref.shape[0]
    units = gate_ref.shape[2]
    tile = 256
    for mat, out in ((gate_ref, gate_pre_ref), (up_ref, up_pre_ref)):
        for n in range(units // tile):
            at = slice(n * tile, (n + 1) * tile)
            out[:count, at] = jnp.dot(own_ref[...], mat[0, :, at], preferred_element_type=f32)
            out[count:, at] = jnp.dot(other_ref[...], mat[0, :, at], preferred_element_type=f32)


def forward(own, other, w_gate, w_up):
    count, features = own.shape
    units = w_gate.shape[2]
    inside = pl.BlockSpec(memory_space=pltpu.VMEM)
    return pl.pallas_call(
        forward_kernel,
        in_specs=[inside] * 4,
        out_specs=(inside, inside),
        out_shape=(jax.ShapeDtypeStruct((2 * count, units), f32),) * 2,
        compiler_params=params(),
        cost_estimate=pl.CostEstimate(
            flops=8 * count * features * units, bytes_accessed=24_000_000, transcendentals=0
        ),
        name="forward",
    )(own, other, w_gate, w_up)


def hidden_kernel(
    own_ref, other_ref, down_ref, gate_pre_ref, up_pre_ref, gg_ref, gu_ref, part_ref
):
    count = own_ref.shape[0]
    units = down_ref.shape[1]
    tile = 256
    for half, rows in enumerate((own_ref, other_ref)):
        here = slice(half * count, (half + 1) * count)
        part = jnp.zeros((count, 1), f32)
        for n in range(units // tile):
            at = slice(n * tile, (n + 1) * tile)
            upstream = lax.dot_general(
                rows[...], down_ref[0, at, :], OVER_LAST, preferred_element_type=f32
            )
            gate_pre = gate_pre_ref[here, at]
            up_pre = up_pre_ref[here, at]
            sig = jax.nn.sigmoid(gate_pre)
            grad_up = upstream * (gate_pre * sig)
            part = part + jnp.sum(grad_up * up_pre, axis=-1, keepdims=True)
            gu_ref[here, at] = grad_up.astype(bf16)
            gg_ref[here, at] = (
                upstream * up_pre * sig * (1.0 + gate_pre * (1.0 - sig))
            ).astype(bf16)
        part_ref[here, :] = jnp.broadcast_to(part.astype(bf16).astype(f32), (count, 128))


def hidden_grads(own, other, w_down, gate_pre, up_pre):
    count, features = own.shape
    units = w_down.shape[1]
    inside = pl.BlockSpec(memory_space=pltpu.VMEM)
    return pl.pallas_call(
        hidden_kernel,
        in_specs=[inside] * 5,
        out_specs=(inside, inside, inside),
        out_shape=(
            jax.ShapeDtypeStruct((2 * count, units), bf16),
            jax.ShapeDtypeStruct((2 * count, units), bf16),
            jax.ShapeDtypeStruct((2 * count, 128), f32),
        ),
        compiler_params=params(),
        cost_estimate=pl.CostEstimate(
            flops=4 * count * features * units, bytes_accessed=24_000_000, transcendentals=0
        ),
        name="hidden_grads",
    )(own, other, w_down, gate_pre, up_pre)


def term_kernel(gg_ref, gu_ref, gate_ref, up_ref, term_ref):
    features = gate_ref.shape[1]
    tile = 512
    for n in range(features // tile):
        at = slice(n * tile, (n + 1) * tile)
        term = lax.dot_general(
            gg_ref[...], gate_ref[0, at, :], OVER_LAST, preferred_element_type=f32
        )
        term = term + lax.dot_general(
            gu_ref[...], up_ref[0, at, :], OVER_LAST, preferred_element_type=f32
        )
        term_ref[:, at] = term.astype(bf16)


def terms(grad_gate, grad_up, w_gate, w_up, half):
    count = grad_gate.shape[0] // 2
    units = grad_gate.shape[1]
    features = w_gate.shape[1]
    inside = pl.BlockSpec(memory_space=pltpu.VMEM)
    return pl.pallas_call(
        term_kernel,
        in_specs=[inside] * 4,
        out_specs=inside,
        out_shape=jax.ShapeDtypeStruct((count, features), bf16),
        compiler_params=params(),
        cost_estimate=pl.CostEstimate(
            flops=4 * count * features * units, bytes_accessed=17_000_000, transcendentals=0
        ),
        name="terms",
    )(
        grad_gate[half * count : (half + 1) * count],
        grad_up[half * count : (half + 1) * count],
        w_gate,
        w_up,
    )


def pack_kernel(capacity, own_ref, other_ref, order_ref, send_ref, held):
    span, features = own_ref.shape
    pieces = features // WIDE
    for piece in range(pieces):
        at = slice(piece * WIDE, (piece + 1) * WIDE)
        held[pl.ds(piece * span, span), :] = (
            own_ref[:, at].astype(f32) + other_ref[:, at].astype(f32)
        ).astype(bf16)
    moved = lax.dot_general(order_ref[...], held[...], OVER_ROWS, preferred_element_type=f32)
    send_ref[...] = moved.astype(bf16).reshape(send_ref.shape)


def pack(own, other, order, capacity):
    count, features = own.shape
    block = features // WIDE * capacity
    span = SOME * capacity
    return pl.pallas_call(
        functools.partial(pack_kernel, capacity),
        grid=(count // span,),
        in_specs=[
            pl.BlockSpec((span, features), lambda i: (i, 0)),
            pl.BlockSpec((span, features), lambda i: (i, 0)),
            pl.BlockSpec(order.shape, lambda i: (0, 0)),
        ],
        out_specs=pl.BlockSpec((SOME, block, WIDE), lambda i: (i, 0, 0)),
        out_shape=jax.ShapeDtypeStruct((count // capacity, block, WIDE), bf16),
        scratch_shapes=[pltpu.VMEM((SOME * block, WIDE), bf16)],
        compiler_params=params(1),
        name="pack",
    )(own, other, order)


def mix_kernel(capacity, code_ref, gate_ref, mix_ref):
    some, columns = code_ref.shape
    rows = mix_ref.shape[1]
    block = rows // some
    want = row_codes((some, block, columns), capacity, block, 1)
    mixing = jnp.where(code_ref[...][:, None, :] == want, gate_ref[...][:, None, :], 0.0)
    mixing = mixing.reshape(rows, columns)
    high = mixing.astype(bf16)
    low = (mixing - high.astype(f32)).astype(bf16)
    mix_ref[:columns, :] = high.T
    mix_ref[columns:, :] = low.T


def mixings(code, gate_wide, capacity, block):
    experts, columns = code.shape
    some = 8
    return pl.pallas_call(
        functools.partial(mix_kernel, capacity),
        grid=(experts // some,),
        in_specs=[
            pl.BlockSpec((some, columns), lambda i: (i, 0)),
            pl.BlockSpec((some, columns), lambda i: (i, 0)),
        ],
        out_specs=pl.BlockSpec((2 * columns, some * block), lambda i: (0, i)),
        out_shape=jax.ShapeDtypeStruct((2 * columns, experts * block), bf16),
        compiler_params=params(1),
        name="mixings",
    )(code, gate_wide)


def finish_kernel(
    mix_ref, back_ref, pre_ref, grad_ref, gain_ref, logit_ref, router_ref,
    residual_ref, pieces_ref, gain_out_ref,
):
    tok_rows, features = pre_ref.shape
    columns = mix_ref.shape[0] // 2
    pieces = features // WIDE
    both = jnp.dot(mix_ref[...], back_ref[...], preferred_element_type=f32)
    expert_grad = both[:columns] + both[columns:]
    hidden = pre_ref[...].astype(f32)
    inverse = lax.rsqrt(jnp.mean(hidden * hidden, axis=-1, keepdims=True) + 1e-06)
    router_term = jnp.dot(logit_ref[...], router_ref[...], preferred_element_type=f32)
    moment = jnp.zeros((tok_rows, 1), f32)
    normed_grads = []
    for piece in range(pieces):
        at = slice(piece * WIDE, (piece + 1) * WIDE)
        normed_grad = (
            expert_grad[piece * tok_rows : (piece + 1) * tok_rows] + router_term[:, at]
        )
        normed_grads.append(normed_grad)
        gain_out_ref[:, at] = jnp.sum(
            normed_grad * hidden[:, at] * inverse, axis=0, keepdims=True
        )
        moment = moment + jnp.sum(
            hidden[:, at] * gain_ref[:, at] * normed_grad, axis=-1, keepdims=True
        )
    factor = inverse * inverse * inverse * (moment / features)
    for piece in range(pieces):
        at = slice(piece * WIDE, (piece + 1) * WIDE)
        residual = (
            grad_ref[:, at].astype(f32)
            + inverse * gain_ref[:, at] * normed_grads[piece]
            - hidden[:, at] * factor
        ).astype(bf16)
        residual_ref[:, at] = residual
        pieces_ref[pl.ds(piece * tok_rows, tok_rows), :] = residual


def finish(mix, back, pre_norm, out_grad, norm_gain, logit_full, router_wide):
    tok_rows, features = pre_norm.shape
    return pl.pallas_call(
        finish_kernel,
        out_shape=(
            jax.ShapeDtypeStruct((tok_rows, features), bf16),
            jax.ShapeDtypeStruct((tok_rows * features // WIDE, WIDE), bf16),
            jax.ShapeDtypeStruct((1, features), f32),
        ),
        compiler_params=params(0, 24),
        name="finish",
    )(mix, back, pre_norm, out_grad, norm_gain, logit_full, router_wide)


def shards(
    pre_norm,
    out_grad,
    routes,
    gate_probs,
    norm_gain,
    router_weight,
    w_gate,
    w_up,
    w_down,
    context,
    out_weight,
):
    tok_rows, features = pre_norm.shape
    top = routes.shape[1]
    experts = router_weight.shape[1]
    capacity = tok_rows * top * 3 // (2 * experts)
    pieces = features // WIDE
    block = pieces * capacity
    gain = norm_gain.reshape(1, features)

    routes_wide = jnp.tile(routes.T, (1, pieces))
    send, code, normed = place(pre_norm, out_grad, gain, routes_wide, experts, capacity)

    got = exchange(send, CHIP)

    order = order_matrix(capacity, block)
    named = routes[:, :, None] == jnp.arange(experts, dtype=jnp.int32)[None, None, :]
    gate_of = jnp.sum(jnp.where(named, gate_probs[:, :, None], 0.0), axis=1)
    mix = mixings(code, jnp.tile(gate_of.T, (1, pieces)), capacity, block)
    router_wide = router_weight.T
    got, order, mix, router_wide, out_weight, context = lax.optimization_barrier(
        (got, order, mix, router_wide, out_weight, context)
    )

    weight_band = lax.all_gather(out_weight, "x", axis=0, tiled=True)
    context_band = lax.all_gather(context, "y", axis=0, tiled=True)

    own_tokens = spread(got, 0, order, capacity)
    other_tokens = swap_cores(own_tokens)
    own_grads = spread(got, 1, order, capacity)
    other_grads = swap_cores(own_grads)
    gate_pre, up_pre = forward(own_tokens, other_tokens, w_gate, w_up)
    grad_gate, grad_up, part = hidden_grads(own_grads, other_grads, w_down, gate_pre, up_pre)
    count = part.shape[0] // 2
    part = part[:count] + swap_cores(part[count:])
    part = jnp.pad(part.reshape(experts, capacity, 128), ((0, 0), (0, 8 - capacity), (0, 0)))
    part = exchange(part, CHIP)[:, :capacity, 0]

    other_term = terms(grad_gate, grad_up, w_gate, w_up, 1)
    grad_gate, other_term = lax.optimization_barrier((grad_gate, other_term))
    own_term = terms(grad_gate, grad_up, w_gate, w_up, 0)
    send_back = pack(own_term, swap_cores(other_term), order, capacity)
    send_back, weight_band, context_band = lax.optimization_barrier(
        (send_back, weight_band, context_band)
    )
    got_back = exchange(send_back, CHIP).reshape(experts * block, WIDE)

    slot = code[:, :tok_rows].T
    at_slot = jnp.arange(capacity, dtype=jnp.int32).astype(f32)
    grad_of = jnp.sum(
        jnp.where(slot[:, :, None] == at_slot[None, None, :], part[None], 0.0), axis=2
    )
    gate_grad = jnp.sum(jnp.where(named, grad_of[:, None, :], 0.0), axis=2)
    weighted = jnp.sum(gate_of * grad_of, axis=-1, keepdims=True)
    logit_full = (gate_of * (grad_of - weighted)).astype(bf16)
    router_part = lax.dot_general(normed, logit_full, OVER_ROWS, preferred_element_type=f32)
    router_sum = lax.psum_scatter(router_part, TENSOR, scatter_dimension=0, tiled=True)
    got_back, router_sum = lax.optimization_barrier((got_back, router_sum))

    residual_grad, residual, gain_part = finish(
        mix, got_back, pre_norm, out_grad, gain, logit_full, router_wide
    )

    sides = lax.axis_size("y")
    shared = lax.axis_size(TENSOR)
    band = features // shared
    swapped = exchange(residual.reshape(sides, -1, WIDE), "y")
    gathered = lax.all_gather(swapped, TENSOR, axis=0, tiled=False)

    gain_all = gain_part.reshape(features // 128, 128)
    gain_all = pair_sum(pair_sum(gain_all, "core"), "z")
    per = band // 128
    mine = lax.dynamic_slice_in_dim(gain_all, lax.axis_index(TENSOR) * per, per, 0)
    small = jnp.concatenate([router_sum.reshape(-1, 128), mine], axis=0)
    small = pair_sum(pair_sum(small, "x"), "y")
    router_grad = small[:-per].reshape(band, experts)
    gain_grad = small[-per:].reshape(band)
    gathered, small = lax.optimization_barrier((gathered, small))

    square = gathered.reshape(shared, sides, pieces // sides, tok_rows, WIDE)
    square = square.transpose(1, 0, 3, 2, 4).reshape(sides, shared * tok_rows, features // sides)
    row, column = lax.axis_index("y"), lax.axis_index("x")

    def context_block(step):
        rows = lax.dynamic_index_in_dim(square, lax.rem(row + step, sides), 0, keepdims=False)
        return jnp.dot(rows, weight_band, preferred_element_type=f32).astype(bf16)

    opposite = context_block(2)
    context_grad = ring_scatter(
        opposite, (context_block(0), context_block(1), context_block(3)), "y"
    )
    weight_part = lax.dot_general(
        square.reshape(sides * shared * tok_rows, features // sides),
        context_band,
        OVER_ROWS,
        preferred_element_type=f32,
    ).astype(bf16)
    weight_part = weight_part.reshape(sides, -1, weight_part.shape[1])

    def weight_block(step):
        return lax.dynamic_index_in_dim(
            weight_part, lax.rem(column + step, sides), 0, keepdims=False
        )

    weight_grad = ring_scatter(
        weight_block(2), (weight_block(0), weight_block(1), weight_block(3)), "x"
    )
    return (residual_grad, gate_grad, router_grad, gain_grad, context_grad, weight_grad)


def solution(mesh):
    devices = np.asarray(mesh.devices)
    fine = Mesh(devices.reshape(4, 4, 4, 2), EVERY)
    rows = P(EVERY, None)
    cube = P(EVERY, None, None)
    split = P(DP, TENSOR)
    return jax.shard_map(
        shards,
        mesh=fine,
        in_specs=(rows, rows, rows, rows, P(), P(), cube, cube, cube, split, split),
        out_specs=(rows, rows, P(TENSOR, None), P(TENSOR), split, split),
        check_vma=False,
    )
```

time: 725 us -> 377 us (0.52)
  waiting for transfers between devices: 433 us -> 159 us
  matrix products: 82.8 us -> 9.79 us
  Pallas kernels: 0 us -> 64.7 us
  blocking collectives: 66.8 us -> 10.3 us
  local copies, waits for them, and re-layouts: 68 us -> 48.7 us
  starting transfers between devices: 43.7 us -> 55 us
    all_to_all x4 -> x3, waiting for transfers between devices: 260 us -> 78.9 us  [exchange(): return lax.all_to_all(value, axes, split_axis=0, concat_axis=0, tiled=True)]
    psum x1 -> x0, waiting for transfers between devices: 148 us -> none  [shards(): router_all, gain_all = lax.psum((router_part, gain_part), ('dp', 'tensor'))]
    dot_general x13 -> x6, matrix products: 82.8 us -> 9.79 us  [the longest x4 5.06 us: context_block(): return jnp.dot(rows, weight_band, preferred_element_type=f32).astype(bf16)]
    psum x1 -> x0, blocking collectives: 66.8 us -> none  [shards(): router_all, gain_all = lax.psum((router_part, gain_part), ('dp', 'tensor'))]
    pallas_call x0 -> x10, Pallas kernels: none -> 64.7 us  [the longest x2 14.8 us: spread(): pl.pallas_call(functools.partial(spread_kernel, capacity), grid=(sources...]
    reduce_scatter x1, waiting for transfers between devices: 0.01 us -> 51.1 us  [shards(): lax.psum_scatter(router_part, TENSOR, scatter_dimension=0, tiled=True)]
    reshape x5, local copies, waits for them, and re-layouts: 38.5 us -> 6.08 us  [the longest x1 2.75 us: shards(): square.transpose(1, 0, 3, 2, 4)]
    ppermute x0 -> x19, waiting for transfers between devices: none -> 29.3 us  [the longest x7 24.7 us: pair_sum(): lax.ppermute(value, axis, [(i, i ^ mask) for i in range(size)])]
  transfers between devices with their start and end apart: 8 -> 26, of which waited for: 5 -> 12; matrix products, arithmetic and copies ran while one was open for 13% -> 7% of each run, Pallas kernels for 0% -> 13%
where the time goes in v1:
time: 377 us; the launch traced here: 371 us
  waiting for transfers between devices  159 us (42%)
  Pallas kernels  64.7 us (17%)
  starting transfers between devices  55 us (15%)
  local copies, waits for them, and re-layouts  48.7 us (13%)
  between operations  16.2 us (4%)
  blocking collectives  10.3 us (3%)
  matrix products  9.79 us (3%)
  other arithmetic  7.2 us (2%)
    all_to_all x3, waiting for transfers between devices, exchange(): return lax.all_to_all(value, axes, split_axis=0, concat_axis=0, tiled=True)  78.9 us
    reduce_scatter x1, waiting for transfers between devices, shards(): lax.psum_scatter(router_part, TENSOR, scatter_dimension=0, tiled=True)  51.1 us
    all_to_all x3, starting transfers between devices, exchange(): return lax.all_to_all(value, axes, split_axis=0, concat_axis=0, tiled=True)  32.7 us
    unnamed x67, local copies, waits for them, and re-layouts  29.4 us
    ppermute x7, waiting for transfers between devices, pair_sum(): lax.ppermute(value, axis, [(i, i ^ mask) for i in range(size)])  24.7 us
    pallas_call x2, Pallas kernels, spread(): pl.pallas_call(functools.partial(spread_kernel, capacity), grid=(sources...  14.8 us
    pallas_call x1, Pallas kernels, forward(): pl.pallas_call(forward_kernel, in_specs=[inside] * 4, out_specs=(inside,...  12.7 us
    pallas_call x2, Pallas kernels, terms(): pl.pallas_call(term_kernel, in_specs=[inside] * 4, out_specs=inside, out_...  12.2 us
  transfers between devices with their start and end apart: 26, of which 12 were waited for; matrix products, arithmetic and copies ran while one was open for 7% of the time, Pallas kernels for 13%

profile of v1, /device:TPU:0, one launch (start us, length us, event | category | flops | bytes accessed | tf_op | source)
XLA Modules:
  0.0 371.3 jit_solution(15996115786609795163)
XLA Ops:
  8.8 0.9 copy-done.3
  9.7 0.9 copy-done.5
  11.4 3.3 place.1
  14.7 2.7 copy-done.1
  18.1 11.9 %all-to-all-start = ((bf16[64,96,512]{2,1,0:T(8,128)(2,1)}), bf16[64,96,512]{2,1,0:T(8,128)(2,1)}, u32[]{:S(2)}, u32[]{:S(2)}) async-start(bf16[64,96,512]{2,1,0:T(8,128)(2,1)} %copy-done.1), calls=%async_computation | async-start | bytes 12582912 | tf_op jit(solution)/shard_map/all_to_all | solution.py:30
  30.7 2.0 mixings.1.mix_ref
  32.9 78.9 %all-to-all-done.got_ref = bf16[64,96,512]{2,1,0:T(8,128)(2,1)} async-done(((bf16[64,96,512]{2,1,0:T(8,128)(2,1)}), bf16[64,96,512]{2,1,0:T(8,128)(2,1)}, u32[]{:S(2)}, u32[]{:S(2)}) %all-to-all-start) | async-done | bytes 6291488 | tf_op jit(solution)/shard_map/all_to_all | solution.py:30
  111.8 7.4 %spread.3.own_ref = bf16[384,4096]{1,0:T(8,128)(2,1)} custom-call(bf16[64,96,512]{2,1,0:T(8,128)(2,1)} %all-to-all-done.got_ref, bf16[384,384]{1,0:T(8,128)(2,1)S(1)} %select_convert_fusion.order_ref), custom_call_target="tpu_custom_call" | custom-call | tf_op jit(solution)/shard_map/spread/pallas_call | solution.py:162
  119.2 7.3 %spread.2.own_ref = bf16[384,4096]{1,0:T(8,128)(2,1)} custom-call(bf16[64,96,512]{2,1,0:T(8,128)(2,1)} %all-to-all-done.got_ref, bf16[384,384]{1,0:T(8,128)(2,1)S(1)} %select_convert_fusion.order_ref), custom_call_target="tpu_custom_call" | custom-call | tf_op jit(solution)/shard_map/spread/pallas_call | solution.py:162
  127.4 2.8 copy-done.15
  130.1 2.8 copy-done.18
  132.9 12.7 %forward.1 = (f32[768,768]{1,0:T(8,128)S(1)}, f32[768,768]{1,0:T(8,128)S(1)}) custom-call(bf16[384,4096]{1,0:T(8,128)(2,1)} %spread.3.own_ref, bf16[384,4096]{1,0:T(8,128)(2,1)} %collective-permute-done.1.other_ref, bf16[1,4096,768]{2,1,0:T(8,128)(2,1)S(1)} %copy-done.15, bf16[1,4096,768]{2,1,0:T(8,128)(2,1)S(1)} %copy-done.18), custom_call_target="tpu_custom_call" | custom-call | flops 9663676416 | bytes 24000000 | tf_op jit(solution)/shard_map/forward/pallas_call | solution.py:191
  145.7 2.8 copy-done.14
  148.5 8.9 %hidden_grads.1 = (bf16[768,768]{1,0:T(8,128)(2,1)S(1)}, bf16[768,768]{1,0:T(8,128)(2,1)S(1)}, f32[768,128]{1,0:T(8,128)S(1)}) custom-call(bf16[384,4096]{1,0:T(8,128)(2,1)} %spread.2.own_ref, bf16[384,4096]{1,0:T(8,128)(2,1)} %collective-permute-done.other_ref, bf16[1,768,4096]{2,1,0:T(8,128)(2,1)S(1)} %copy-done.14, ...), custom_call_target="tpu_custom_call" | custom-call | flops 4831838208 | bytes 24000000 | tf_op jit(solution)/shard_map/hidden_grads/pallas_call | solution.py:234
  157.5 1.0 fusion.39
  158.5 7.1 %terms.2 = bf16[384,4096]{1,0:T(8,128)(2,1)} custom-call(bf16[384,768]{1,0:T(8,128)(2,1)S(1)} %slice.100.gg_ref, bf16[384,768]{1,0:T(8,128)(2,1)S(1)} %get-tuple-element.87.gu_ref, bf16[1,4096,768]{2,1,0:T(8,128)(2,1)S(1)} %copy-done.16, bf16[1,4096,768]{2,1,0:T(8,128)(2,1)S(1)} %copy-done.19), custom_call_target="tpu_custom_call" | custom-call | flops 4831838208 | bytes 17000000 | tf_op jit(solution)/shard_map/terms/pallas_call | solution.py:270
  165.7 0.9 slice.106
  167.2 1.9 slice.102.gg_ref
  169.1 2.4 collective-permute-done.3
  171.6 1.6 slice_add_fusion
  173.2 1.7 reshape.79
  174.9 1.7 pad.4
  176.6 10.4 %all-to-all-start.2 = ((f32[64,8,128]{2,1,0:T(8,128)}), f32[64,8,128]{2,1,0:T(8,128)}, u32[]{:S(2)}, u32[]{:S(2)}) async-start(f32[64,8,128]{2,1,0:T(8,128)} %pad.4), calls=%async_computation.2 | async-start | bytes 524288 | tf_op jit(solution)/shard_map/all_to_all | solution.py:30
  186.9 1.1 copy-done.7
  188.0 1.1 copy-done.8
  189.1 2.8 copy-done.17
  191.9 2.8 copy-done.20
  194.7 5.1 %terms.3.own_ref = bf16[384,4096]{1,0:T(8,128)(2,1)S(1)} custom-call(bf16[384,768]{1,0:T(8,128)(2,1)S(1)} %copy-done.7, bf16[384,768]{1,0:T(8,128)(2,1)S(1)} %copy-done.8, bf16[1,4096,768]{2,1,0:T(8,128)(2,1)S(1)} %copy-done.17, bf16[1,4096,768]{2,1,0:T(8,128)(2,1)S(1)} %copy-done.20), custom_call_target="tpu_custom_call" | custom-call | flops 4831838208 | bytes 17000000 | tf_op jit(solution)/shard_map/terms/pallas_call | solution.py:270
  199.8 6.1 %pack.1 = bf16[64,48,512]{2,1,0:T(8,128)(2,1)S(1)} custom-call(bf16[384,4096]{1,0:T(8,128)(2,1)S(1)} %terms.3.own_ref, bf16[384,4096]{1,0:T(8,128)(2,1)} %collective-permute-done.2.other_ref, bf16[384,384]{1,0:T(8,128)(2,1)S(1)} %select_convert_fusion.order_ref), custom_call_target="tpu_custom_call" | custom-call | tf_op jit(solution)/shard_map/pack/pallas_call | solution.py:304
  205.9 1.7 copy-done
  207.7 10.5 %all-to-all-start.1 = ((bf16[64,48,512]{2,1,0:T(8,128)(2,1)}), bf16[64,48,512]{2,1,0:T(8,128)(2,1)}, u32[]{:S(2)}, u32[]{:S(2)}) async-start(bf16[64,48,512]{2,1,0:T(8,128)(2,1)} %copy-done), calls=%async_computation.1 | async-start | bytes 6291456 | tf_op jit(solution)/shard_map/all_to_all | solution.py:30
  218.3 1.1 copy.53
  219.7 2.3 fusion.41
  222.1 51.1 %reduce-scatter.2.cloned.1.call-done = f32[512,64]{0,1:T(8,128)} async-done(((f32[4096,64]{0,1:T(8,128)}), f32[512,64]{0,1:T(8,128)}) %reduce-scatter.2.cloned.1.call-update) | async-done | bytes 131088 | tf_op jit(solution)/shard_map/reduce_scatter | solution.py:469
  273.2 0.9 copy-done.6
  274.2 1.0 copy-done.9
  275.2 4.7 %finish.1 = (bf16[32,4096]{1,0:T(8,128)(2,1)}, bf16[256,512]{1,0:T(8,128)(2,1)S(1)}, f32[1,4096]{1,0:T(1,128)S(1)}) custom-call(bf16[512,3072]{1,0:T(8,128)(2,1)S(1)} %mixings.1.mix_ref, bf16[3072,512]{1,0:T(8,128)(2,1)} %bitcast.5.back_ref, bf16[32,4096]{1,0:T(8,128)(2,1)S(1)} %copy-done.4, bf16[32,4096]{1,0:T(8,128)(2,1)S(1)} %copy-done.6, ...), custom_call_target="tpu_custom_call" | custom-call | tf_op jit(solution)/shard_map/finish/pallas_call | solution.py:390
  279.9 10.3 %all_to_all.20 = bf16[4,64,512]{2,1,0:T(8,128)(2,1)} all-to-all(bf16[4,64,512]{2,1,0:T(8,128)(2,1)S(1)} %bitcast.64), channel_id=1, replica_groups=mesh['y'=4,'x'=4,'z'=4,'core'=2] {'y'}, dimensions={0} | all-to-all | bytes 524288 | tf_op jit(solution)/shard_map/all_to_all | solution.py:30
  290.3 1.2 collective-permute-done.4
  291.5 3.7 %collective-permute-done.5 = f32[32,128]{1,0:T(8,128)S(1)} collective-permute-done((f32[32,128]{1,0:T(8,128)S(1)}, f32[32,128]{1,0:T(8,128)S(1)}, u32[]{:S(2)}, u32[]{:S(2)}) %collective-permute-start.5) | collective-permute-done | bytes 16416 | tf_op jit(solution)/shard_map/ppermute | solution.py:36
  295.2 1.5 collective-permute-start.6
  296.7 1.0 copy.54
  297.8 2.3 collective-permute-done.6
  300.4 5.0 %collective-permute-done.7 = f32[260,128]{1,0:T(8,128)S(1)} collective-permute-done((f32[260,128]{1,0:T(8,128)S(1)}, f32[260,128]{1,0:T(8,128)S(1)}, u32[]{:S(2)}, u32[]{:S(2)}) %collective-permute-start.7) | collective-permute-done | bytes 133152 | tf_op jit(solution)/shard_map/ppermute | solution.py:36
  305.5 4.0 %collective-permute-start.8 = (f32[260,128]{1,0:T(8,128)S(1)}, f32[260,128]{1,0:T(8,128)S(1)}, u32[]{:S(2)}, u32[]{:S(2)}) collective-permute-start(f32[260,128]{1,0:T(8,128)S(1)} %fusion.38), channel_id=1, source_target_pairs={{0,24},{8,16},{16,8},{24,0},{1,25},{9,17},{17,9},{25,1},{2,26},{10... | collective-permute-start | bytes 399368 | tf_op jit(solution)/shard_map/ppermute | solution.py:36
  309.4 3.0 collective-permute-done.8
  313.1 4.4 %collective-permute-done.9 = f32[260,128]{1,0:T(8,128)S(1)} collective-permute-done((f32[260,128]{1,0:T(8,128)S(1)}, f32[260,128]{1,0:T(8,128)S(1)}, u32[]{:S(2)}, u32[]{:S(2)}) %collective-permute-start.9) | collective-permute-done | bytes 133152 | tf_op jit(solution)/shard_map/ppermute | solution.py:36
  317.5 1.2 collective-permute-start.10
  318.8 5.1 %collective-permute-done.10 = f32[260,128]{1,0:T(8,128)S(1)} collective-permute-done((f32[260,128]{1,0:T(8,128)S(1)}, f32[260,128]{1,0:T(8,128)S(1)}, u32[]{:S(2)}, u32[]{:S(2)}) %collective-permute-start.10) | collective-permute-done | bytes 133152 | tf_op jit(solution)/shard_map/ppermute | solution.py:36
  323.9 3.8 %copy.55 = bf16[4,8,32,2,512]{4,3,2,1,0:T(2,128)(2,1)S(1)} copy(bf16[4,8,32,2,512]{4,2,3,0,1:T(8,128)(2,1)} %bitcast.73) | data formatting | bytes 4194304 | tf_op jit(solution)/shard_map/transpose | solution.py:493
  327.7 2.7 reshape.86
  331.0 1.0 copy-done.30
  332.0 2.4 convolution_convert_fusion
  334.6 3.3 collective-permute-start.17
  339.6 3.3 collective-permute-start.13
  343.8 0.9 pad_maximum_fusion.2
  344.7 0.9 collective-permute-start.16
  346.4 2.4 collective-permute-start.18
  349.7 0.8 pad_maximum_fusion.1
  350.5 3.2 collective-permute-start.14
  355.3 1.0 reshape.82
  357.7 1.1 fusion.5
  358.7 1.6 collective-permute-done.12
  360.8 2.9 fusion.3
  (129 shorter events, 14.5 us)
Async XLA Ops:
  8.8 0.9 copy-start.3
  9.7 0.9 copy-start.5
  10.7 0.7 copy-start.12
  14.7 2.7 copy-start.1
  17.4 0.7 copy-start.11
  18.1 11.9 %copy-start.26 = (s32[32,8]{0,1:T(8,128)S(1)}, s32[32,8]{0,1:T(8,128)}, u32[]{:S(2)}) copy-start(s32[32,8]{0,1:T(8,128)} %param.13) | copy-start | bytes 3076
  18.1 12.0 %copy-start.27 = (f32[32,8]{0,1:T(8,128)S(1)}, f32[32,8]{0,1:T(8,128)}, u32[]{:S(2)}) copy-start(f32[32,8]{0,1:T(8,128)} %param.14) | copy-start | bytes 3076
  18.1 93.7 %all-to-all-start = ((bf16[64,96,512]{2,1,0:T(8,128)(2,1)}), bf16[64,96,512]{2,1,0:T(8,128)(2,1)}, u32[]{:S(2)}, u32[]{:S(2)}) async-start(bf16[64,96,512]{2,1,0:T(8,128)(2,1)} %copy-done.1), calls=%async_computation | async-start | bytes 12582912 | tf_op jit(solution)/shard_map/all_to_all | solution.py:30
  30.0 177.7 %all-gather.5.cloned.1.call-start = ((), (), s32[]{:S(2)}) async-start(), calls=%async_computation.5 | async-start | bytes 2621440 | tf_op jit(solution)/shard_map/all_gather | solution.py:437
  30.1 0.6 copy-start.24
  119.2 8.1 %collective-permute-start.1 = (bf16[384,4096]{1,0:T(8,128)(2,1)}, bf16[384,4096]{1,0:T(8,128)(2,1)}, u32[]{:S(2)}, u32[]{:S(2)}) collective-permute-start(bf16[384,4096]{1,0:T(8,128)(2,1)} %spread.3.own_ref), channel_id=1, source_target_pairs={{0,1},{1,0},{2,3},{3,2},{4,5},{5,4},{6,7},{7,6},{8,9},{9,8},{10,11... | collective-permute-start | bytes 9437192 | tf_op jit(solution)/shard_map/ppermute | solution.py:26
  126.6 19.1 %collective-permute-start = (bf16[384,4096]{1,0:T(8,128)(2,1)}, bf16[384,4096]{1,0:T(8,128)(2,1)}, u32[]{:S(2)}, u32[]{:S(2)}) collective-permute-start(bf16[384,4096]{1,0:T(8,128)(2,1)} %spread.2.own_ref), channel_id=1, source_target_pairs={{0,1},{1,0},{2,3},{3,2},{4,5},{5,4},{6,7},{7,6},{8,9},{9,8},{10,11... | collective-permute-start | bytes 9437192 | tf_op jit(solution)/shard_map/ppermute | solution.py:26
  127.1 80.6 %all-gather.7.cloned.1.call-start = ((), (), s32[]{:S(2)}) async-start(), calls=%async_computation.6 | async-start | bytes 2621440 | tf_op jit(solution)/shard_map/all_gather | solution.py:438
  127.4 2.8 copy-start.15
  130.1 2.8 copy-start.18
  145.7 2.8 copy-start.14
  148.5 10.0 %copy-start.16 = (bf16[1,4096,768]{2,1,0:T(8,128)(2,1)S(1)}, bf16[1,4096,768]{2,1,0:T(8,128)(2,1)}, u32[]{:S(2)}) copy-start(bf16[1,4096,768]{2,1,0:T(8,128)(2,1)} %gate_ref.5) | copy-start | bytes 18874372
  148.5 10.0 %copy-start.19 = (bf16[1,4096,768]{2,1,0:T(8,128)(2,1)S(1)}, bf16[1,4096,768]{2,1,0:T(8,128)(2,1)}, u32[]{:S(2)}) copy-start(bf16[1,4096,768]{2,1,0:T(8,128)(2,1)} %up_ref.5) | copy-start | bytes 18874372
  157.4 8.3 %copy-start.2 = (bf16[768,768]{1,0:T(8,128)(2,1)}, bf16[768,768]{1,0:T(8,128)(2,1)S(1)}, u32[]{:S(2)}) copy-start(bf16[768,768]{1,0:T(8,128)(2,1)S(1)} %get-tuple-element.40) | copy-start | bytes 3538948
  157.4 8.2 %copy-start.10 = (f32[768,128]{1,0:T(8,128)}, f32[768,128]{1,0:T(8,128)S(1)}, u32[]{:S(2)}) copy-start(f32[768,128]{1,0:T(8,128)S(1)} %get-tuple-element.46) | copy-start | bytes 1179652
  165.7 34.1 %collective-permute-start.2 = (bf16[384,4096]{1,0:T(8,128)(2,1)}, bf16[384,4096]{1,0:T(8,128)(2,1)}, u32[]{:S(2)}, u32[]{:S(2)}) collective-permute-start(bf16[384,4096]{1,0:T(8,128)(2,1)} %terms.2), channel_id=1, source_target_pairs={{0,1},{1,0},{2,3},{3,2},{4,5},{5,4},{6,7},{7,6},{8,9},{9,8},{10,11... | collective-permute-start | bytes 9437192 | tf_op jit(solution)/shard_map/ppermute | solution.py:26
  166.6 5.0 %collective-permute-start.3 = (f32[384,128]{1,0:T(8,128)S(1)}, f32[384,128]{1,0:T(8,128)S(1)}, u32[]{:S(2)}, u32[]{:S(2)}) collective-permute-start(f32[384,128]{1,0:T(8,128)S(1)} %slice.106), channel_id=1, source_target_pairs={{0,1},{1,0},{2,3},{3,2},{4,5},{5,4},{6,7},{7,6},{8,9},{9,8},{10,11... | collective-permute-start | bytes 589832 | tf_op jit(solution)/shard_map/ppermute | solution.py:26
  176.6 31.1 %all-to-all-start.2 = ((f32[64,8,128]{2,1,0:T(8,128)}), f32[64,8,128]{2,1,0:T(8,128)}, u32[]{:S(2)}, u32[]{:S(2)}) async-start(f32[64,8,128]{2,1,0:T(8,128)} %pad.4), calls=%async_computation.2 | async-start | bytes 524288 | tf_op jit(solution)/shard_map/all_to_all | solution.py:30
  186.9 1.1 copy-start.7
  188.0 1.1 copy-start.8
  189.1 2.8 copy-start.17
  191.9 2.8 copy-start.20
  205.9 1.8 copy-start
  207.7 65.5 %all-to-all-start.1 = ((bf16[64,48,512]{2,1,0:T(8,128)(2,1)}), bf16[64,48,512]{2,1,0:T(8,128)(2,1)}, u32[]{:S(2)}, u32[]{:S(2)}) async-start(bf16[64,48,512]{2,1,0:T(8,128)(2,1)} %copy-done), calls=%async_computation.1 | async-start | bytes 6291456 | tf_op jit(solution)/shard_map/all_to_all | solution.py:30
  218.2 55.0 %copy-start.4 = (bf16[32,4096]{1,0:T(8,128)(2,1)S(1)}, bf16[32,4096]{1,0:T(8,128)(2,1)}, u32[]{:S(2)}) copy-start(bf16[32,4096]{1,0:T(8,128)(2,1)} %pre_ref.3) | copy-start | bytes 786436
  218.2 55.0 %copy-start.13 = (f32[4096]{0:T(1024)S(1)}, f32[4096]{0:T(1024)}, u32[]{:S(2)}) copy-start(f32[4096]{0:T(1024)} %param.15) | copy-start | bytes 49156
  218.2 55.0 %reduce-scatter.2.cloned.1.call-start = ((), (), s32[]{:S(2)}) async-start(), calls=%async_computation.7 | async-start | bytes 1179648 | tf_op jit(solution)/shard_map/reduce_scatter | solution.py:469
  219.5 53.7 %copy-start.22 = (f32[32,64]{1,0:T(8,128)}, f32[32,64]{1,0:T(8,128)S(1)}, u32[]{:S(2)}) copy-start(f32[32,64]{1,0:T(8,128)S(1)} %select_reduce_fusion.2) | copy-start | bytes 24580
  222.1 101.8 %all-gather.9.cloned.1.call-start = ((), (), s32[]{:S(2)}) async-start(), calls=%async_computation.8 | async-start | bytes 2359296 | tf_op jit(solution)/shard_map/all_gather | solution.py:480
  273.2 1.0 copy-start.6
  274.2 1.0 copy-start.9
  290.2 1.3 collective-permute-start.4
  291.5 3.7 %collective-permute-start.5 = (f32[32,128]{1,0:T(8,128)S(1)}, f32[32,128]{1,0:T(8,128)S(1)}, u32[]{:S(2)}, u32[]{:S(2)}) collective-permute-start(f32[32,128]{1,0:T(8,128)S(1)} %add.127), channel_id=1, source_target_pairs={{0,2},{2,0},{4,6},{6,4},{1,3},{3,1},{5,7},{7,5},{8,10},{10,8},{12,... | collective-permute-start | bytes 49160 | tf_op jit(solution)/shard_map/ppermute | solution.py:36
  295.2 4.9 %collective-permute-start.6 = (f32[32,128]{1,0:T(8,128)S(1)}, f32[32,128]{1,0:T(8,128)S(1)}, u32[]{:S(2)}, u32[]{:S(2)}) collective-permute-start(f32[32,128]{1,0:T(8,128)S(1)} %add.128), channel_id=1, source_target_pairs={{0,6},{2,4},{4,2},{6,0},{1,7},{3,5},{5,3},{7,1},{8,14},{10,12},{12... | collective-permute-start | bytes 49160 | tf_op jit(solution)/shard_map/ppermute | solution.py:36
  300.2 5.3 %collective-permute-start.7 = (f32[260,128]{1,0:T(8,128)S(1)}, f32[260,128]{1,0:T(8,128)S(1)}, u32[]{:S(2)}, u32[]{:S(2)}) collective-permute-start(f32[260,128]{1,0:T(8,128)S(1)} %pad_maximum_fusion.4), channel_id=1, source_target_pairs={{0,8},{8,0},{16,24},{24,16},{1,9},{9,1},{17,25},{25,17},{2,10},{10... | collective-permute-start | bytes 399368 | tf_op jit(solution)/shard_map/ppermute | solution.py:36
  305.5 7.0 %collective-permute-start.8 = (f32[260,128]{1,0:T(8,128)S(1)}, f32[260,128]{1,0:T(8,128)S(1)}, u32[]{:S(2)}, u32[]{:S(2)}) collective-permute-start(f32[260,128]{1,0:T(8,128)S(1)} %fusion.38), channel_id=1, source_target_pairs={{0,24},{8,16},{16,8},{24,0},{1,25},{9,17},{17,9},{25,1},{2,26},{10... | collective-permute-start | bytes 399368 | tf_op jit(solution)/shard_map/ppermute | solution.py:36
  312.4 5.1 %collective-permute-start.9 = (f32[260,128]{1,0:T(8,128)S(1)}, f32[260,128]{1,0:T(8,128)S(1)}, u32[]{:S(2)}, u32[]{:S(2)}) collective-permute-start(f32[260,128]{1,0:T(8,128)S(1)} %add.133), channel_id=1, source_target_pairs={{0,32},{32,0},{64,96},{96,64},{1,33},{33,1},{65,97},{97,65},{2,34}... | collective-permute-start | bytes 399368 | tf_op jit(solution)/shard_map/ppermute | solution.py:36
  317.5 6.3 %collective-permute-start.10 = (f32[260,128]{1,0:T(8,128)S(1)}, f32[260,128]{1,0:T(8,128)S(1)}, u32[]{:S(2)}, u32[]{:S(2)}) collective-permute-start(f32[260,128]{1,0:T(8,128)S(1)} %add.134), channel_id=1, source_target_pairs={{0,96},{32,64},{64,32},{96,0},{1,97},{33,65},{65,33},{97,1},{2,98}... | collective-permute-start | bytes 399368 | tf_op jit(solution)/shard_map/ppermute | solution.py:36
  330.4 1.6 copy-start.30
  332.0 5.9 %copy-start.28 = (bf16[1024,1024]{1,0:T(8,128)(2,1)S(1)}, bf16[1024,1024]{1,0:T(8,128)(2,1)}, u32[]{:S(2)}) copy-start(bf16[1024,1024]{1,0:T(8,128)(2,1)} %all-gather.5.cloned.1.call-done) | copy-start | bytes 6291460
  334.5 3.5 copy-start.21
  334.6 9.0 %collective-permute-start.15 = (bf16[128,1024]{1,0:T(8,128)(2,1)S(1)}, bf16[128,1024]{1,0:T(8,128)(2,1)S(1)}, u32[]{:S(2)}, u32[]{:S(2)}) collective-permute-start(bf16[128,1024]{1,0:T(8,128)(2,1)S(1)} %get-tuple-element.82), channel_id=1, source_target_pairs={{0,8},{8,16},{16,24},{24,0},{1,9},{9,17},{17,25},{25,1},{2,10},{10... | collective-permute-start | bytes 786440 | tf_op jit(solution)/shard_map/ppermute | solution.py:45
  334.6 9.0 %collective-permute-start.17 = (bf16[128,1024]{1,0:T(8,128)(2,1)S(1)}, bf16[128,1024]{1,0:T(8,128)(2,1)S(1)}, u32[]{:S(2)}, u32[]{:S(2)}) collective-permute-start(bf16[128,1024]{1,0:T(8,128)(2,1)S(1)} %get-tuple-element.84), channel_id=1, source_target_pairs={{0,24},{8,0},{16,8},{24,16},{1,25},{9,1},{17,9},{25,17},{2,26},{10... | collective-permute-start | bytes 786440 | tf_op jit(solution)/shard_map/ppermute | solution.py:46
  339.4 9.3 %collective-permute-start.11 = (bf16[128,1024]{1,0:T(8,128)(2,1)S(1)}, bf16[128,1024]{1,0:T(8,128)(2,1)S(1)}, u32[]{:S(2)}, u32[]{:S(2)}) collective-permute-start(bf16[128,1024]{1,0:T(8,128)(2,1)S(1)} %get-tuple-element.88), channel_id=1, source_target_pairs={{0,32},{32,64},{64,96},{96,0},{1,33},{33,65},{65,97},{97,1},{2,34}... | collective-permute-start | bytes 786440 | tf_op jit(solution)/shard_map/ppermute | solution.py:45
  339.6 10.1 %collective-permute-start.13 = (bf16[128,1024]{1,0:T(8,128)(2,1)S(1)}, bf16[128,1024]{1,0:T(8,128)(2,1)S(1)}, u32[]{:S(2)}, u32[]{:S(2)}) collective-permute-start(bf16[128,1024]{1,0:T(8,128)(2,1)S(1)} %get-tuple-element.89), channel_id=1, source_target_pairs={{0,96},{32,0},{64,32},{96,64},{1,97},{33,1},{65,33},{97,65},{2,98}... | collective-permute-start | bytes 786440 | tf_op jit(solution)/shard_map/ppermute | solution.py:46
  344.7 13.0 %collective-permute-start.16 = (bf16[256,1024]{1,0:T(8,128)(2,1)}, bf16[256,1024]{1,0:T(8,128)(2,1)S(1)}, u32[]{:S(2)}, u32[]{:S(2)}) collective-permute-start(bf16[256,1024]{1,0:T(8,128)(2,1)} %pad_maximum_fusion.2), channel_id=1, source_target_pairs={{0,8},{8,16},{16,24},{24,0},{1,9},{9,17},{17,25},{25,1},{2,10},{10... | collective-permute-start | bytes 1572872 | tf_op jit(solution)/shard_map/ppermute | solution.py:55
  346.4 7.4 %copy-start.23 = (f32[32,64]{1,0:T(8,128)S(1)}, f32[32,64]{1,0:T(8,128)}, u32[]{:S(2)}) copy-start(f32[32,64]{1,0:T(8,128)} %copy-done.22) | copy-start | bytes 24580
  346.4 7.4 %copy-start.25 = (s32[32,8]{1,0:T(8,128)S(1)}, s32[32,8]{1,0:T(8,128)}, u32[]{:S(2)}) copy-start(s32[32,8]{1,0:T(8,128)} %copy-done.24) | copy-start | bytes 3076
  346.4 11.3 %collective-permute-start.18 = (bf16[256,1024]{1,0:T(8,128)(2,1)}, bf16[256,1024]{1,0:T(8,128)(2,1)S(1)}, u32[]{:S(2)}, u32[]{:S(2)}) collective-permute-start(bf16[256,1024]{1,0:T(8,128)(2,1)} %pad_maximum_fusion.3), channel_id=1, source_target_pairs={{0,24},{8,0},{16,8},{24,16},{1,25},{9,1},{17,9},{25,17},{2,26},{10... | collective-permute-start | bytes 1572872 | tf_op jit(solution)/shard_map/ppermute | solution.py:56
  349.6 10.7 %collective-permute-start.12 = (bf16[256,1024]{1,0:T(8,128)(2,1)}, bf16[256,1024]{1,0:T(8,128)(2,1)}, u32[]{:S(2)}, u32[]{:S(2)}) collective-permute-start(bf16[256,1024]{1,0:T(8,128)(2,1)} %pad_maximum_fusion), channel_id=1, source_target_pairs={{0,32},{32,64},{64,96},{96,0},{1,33},{33,65},{65,97},{97,1},{2,34}... | collective-permute-start | bytes 1572872 | tf_op jit(solution)/shard_map/ppermute | solution.py:55
  350.5 10.2 %collective-permute-start.14 = (bf16[256,1024]{1,0:T(8,128)(2,1)}, bf16[256,1024]{1,0:T(8,128)(2,1)}, u32[]{:S(2)}, u32[]{:S(2)}) collective-permute-start(bf16[256,1024]{1,0:T(8,128)(2,1)} %pad_maximum_fusion.1), channel_id=1, source_target_pairs={{0,96},{32,0},{64,32},{96,64},{1,97},{33,1},{65,33},{97,65},{2,98}... | collective-permute-start | bytes 1572872 | tf_op jit(solution)/shard_map/ppermute | solution.py:56
  357.1 3.7 %copy-start.29 = (bf16[1024,1024]{1,0:T(8,128)(2,1)S(1)}, bf16[1024,1024]{1,0:T(8,128)(2,1)}, u32[]{:S(2)}) copy-start(bf16[1024,1024]{1,0:T(8,128)(2,1)} %all-gather.5.cloned.1.call-done) | copy-start | bytes 6291460
Sparse Core Ops, SparseCore 0:
  127.2 31.7 all-gather.4
  165.8 34.8 all-gather.6
Sparse Core Ops, SparseCore 1:
  222.1 51.0 reduce-scatter.1
  290.3 23.3 all-gather.8

commit v2 on v1

v2 whole, which is shorter than its diff:
```python
import functools

import jax
import jax.numpy as jnp
import numpy as np
from jax import lax
from jax.experimental import pallas as pl
from jax.experimental.pallas import tpu as pltpu
from jax.sharding import Mesh, PartitionSpec as P

CHIP = ("y", "x", "z")
EVERY = ("y", "x", "z", "core")
DP = ("y", "x")
TENSOR = ("z", "core")
SWAP = [(0, 1), (1, 0)]
WIDE = 512
SOME = 8
MIB = 1024 * 1024
bf16 = jnp.bfloat16
f32 = jnp.float32
OVER_ROWS = (((0,), (0,)), ((), ()))
OVER_LAST = (((1,), (1,)), ((), ()))


def swap_cores(value):
    return lax.ppermute(value, "core", SWAP)


def exchange(value, axes):
    return lax.all_to_all(value, axes, split_axis=0, concat_axis=0, tiled=True)


def cross_sum(value, axis):
    size = lax.axis_size(axis)
    value = value.astype(bf16)
    one, two, three = [
        lax.ppermute(value, axis, [(i, i ^ mask) for i in range(size)]) for mask in (1, 2, 3)
    ]
    return (value.astype(f32) + two.astype(f32)) + (one.astype(f32) + three.astype(f32))


def shift(value, axis, step):
    size = lax.axis_size(axis)
    return lax.ppermute(value, axis, [(i, (i + step) % size) for i in range(size)])


def pass_on_kernel(*refs):
    ins, outs = refs[: len(refs) * 2 // 3], refs[len(refs) * 2 // 3 :]
    for at, out in enumerate(outs):
        here, came = ins[2 * at], ins[2 * at + 1]
        half = here.shape[0]
        first = (at % 2) * half
        came = came[first : first + half, :]
        out[...] = (here[...].astype(f32) + came.astype(f32)).astype(bf16)


def close_kernel(*refs):
    ins, outs = refs[:-2], refs[-2:]
    for at, out in enumerate(outs):
        upper, lower, from_left, from_right, last_left, last_right = ins[6 * at : 6 * at + 6]
        half = upper.shape[0]
        out[:half, :] = (
            upper[...].astype(f32) + from_right[:half, :].astype(f32) + last_left[...].astype(f32)
        ).astype(bf16)
        out[half:, :] = (
            lower[...].astype(f32) + from_left[half:, :].astype(f32) + last_right[...].astype(f32)
        ).astype(bf16)


def whole_call(kernel, name, shapes, *arrays):
    whole = pl.BlockSpec(memory_space=pltpu.VMEM)
    return pl.pallas_call(
        kernel,
        in_specs=[whole] * len(arrays),
        out_specs=tuple(whole for _ in shapes),
        out_shape=tuple(jax.ShapeDtypeStruct(shape, bf16) for shape in shapes),
        compiler_params=params(0, 16),
        name=name,
    )(*arrays)


def ring_scatter(square, rings, small):
    places = [lax.axis_index(axis).astype(jnp.int32).reshape(1) for _, _, axis in rings]
    firsts = [
        kernel(place, square, band, (((2, 0), (1, 1)), ((3, 0), (2, 1))))
        for place, (kernel, band, _) in zip(places, rings)
    ]
    firsts, small = lax.optimization_barrier((firsts, small))
    sent = [
        (shift(to_right, axis, 1), shift(to_left, axis, -1))
        for (to_right, to_left), (_, _, axis) in zip(firsts, rings)
    ]
    rests = [
        kernel(place, square, band, (((1, 0),), ((3, 1),), ((0, 0),), ((0, 1),)))
        for place, (kernel, band, _) in zip(places, rings)
    ]
    sent, rests = lax.optimization_barrier((sent, rests))
    half, width = rests[0][0].shape
    passed = whole_call(
        pass_on_kernel,
        "pass_on",
        [(half, width)] * 4,
        *[
            v
            for came, rest in zip(sent, rests)
            for v in (rest[0], *outside(came[0]), rest[1], *outside(came[1]))
        ],
    )
    last = []
    for at, (_, _, axis) in enumerate(rings):
        last.append((shift(passed[2 * at], axis, 1), shift(passed[2 * at + 1], axis, -1)))
    sums = whole_call(
        close_kernel,
        "close",
        [(2 * half, width)] * 2,
        *[
            v
            for came, rest, end in zip(sent, rests, last)
            for v in (rest[2], rest[3], *outside(*came, *end))
        ],
    )
    return (*sums, small)


def gather_kernel(place_ref, *refs):
    *pieces, out_ref, sems = refs
    sides, tok_rows, _ = pieces[0].shape
    y, z, core = place_ref[0], place_ref[1], place_ref[2]
    copies = []
    for at, piece in enumerate(pieces):
        side, turn = at // sides, at % sides
        here = lax.rem(z - turn + sides, sides) * 2 + (core if side == 0 else 1 - core)
        rows = pl.ds(pl.multiple_of(here * tok_rows, tok_rows), tok_rows)
        for back in range(sides):
            copies.append(
                pltpu.make_async_copy(
                    piece.at[back],
                    out_ref.at[lax.rem(y - back + sides, sides), rows],
                    sems.at[at * sides + back],
                )
            )
    for copy in copies:
        copy.start()
    for copy in copies:
        copy.wait()


def gather_square(bands, small):
    sides, tok_rows, width = bands.shape
    y, z, core = lax.axis_index("y"), lax.axis_index("z"), lax.axis_index("core")

    def block(value, index):
        return lax.dynamic_index_in_dim(value, index, 0, keepdims=False)

    own = block(bands, y)
    piece = [own] + [
        shift(block(bands, lax.rem(y + step, sides)), "y", step) for step in range(1, sides)
    ]
    small = small.reshape(sides, 2, *small.shape[1:])
    mine = lax.dynamic_index_in_dim(small, core, 1, keepdims=False)
    theirs = lax.dynamic_index_in_dim(small, 1 - core, 1, keepdims=False)
    small = mine + swap_cores(theirs.astype(bf16)).astype(f32)
    piece = jnp.stack(piece)
    piece, small = lax.optimization_barrier((piece, small))
    passed = small.astype(bf16)
    came = [
        shift(block(passed, lax.rem(z + step, sides)), "z", step) for step in range(1, sides)
    ]
    near = [piece] + [shift(piece, "z", step) for step in (1, 3, 2)]
    far = [swap_cores(p) for p in near]
    small = block(small, z) + sum(c.astype(f32) for c in came)
    small = cross_sum(small, "x")
    near, far, small = lax.optimization_barrier((near, far, small))
    small = cross_sum(small, "y")
    near = [near[0], near[1], near[3], near[2]]
    far = [far[0], far[1], far[3], far[2]]
    whole = pl.BlockSpec(memory_space=pltpu.VMEM)
    square = pl.pallas_call(
        gather_kernel,
        in_specs=[pl.BlockSpec(memory_space=pltpu.SMEM)]
        + [pl.BlockSpec(memory_space=pl.ANY)] * (2 * sides),
        out_specs=whole,
        out_shape=jax.ShapeDtypeStruct((sides, 2 * sides * tok_rows, width), bf16),
        scratch_shapes=[pltpu.SemaphoreType.DMA((2 * sides * sides,))],
        compiler_params=params(0, 16),
        name="gather_square",
    )(jnp.stack([y, z, core]).astype(jnp.int32), *near, *far)
    return square, small


def context_kernel(wanted, place_ref, square_ref, band_ref, *out_refs):
    sides, tokens, _ = square_ref.shape
    half = tokens // 2
    for blocks, out_ref in zip(wanted, out_refs):
        for at, (step, part) in enumerate(blocks):
            block = lax.rem(place_ref[0] + step, sides)
            rows = square_ref[pl.ds(block, 1), part * half : (part + 1) * half, :][0]
            out_ref[at * half : (at + 1) * half, :] = jnp.dot(
                rows, band_ref[...], preferred_element_type=f32
            ).astype(bf16)


def weight_kernel(wanted, place_ref, square_ref, band_ref, *out_refs):
    sides, tokens, depth = square_ref.shape
    half = depth // sides // 2
    for blocks, out_ref in zip(wanted, out_refs):
        for at, (step, part) in enumerate(blocks):
            block = lax.rem(place_ref[0] + step, sides)
            columns = pl.ds(pl.multiple_of((2 * block + part) * half, half), half)
            out_ref[at * half : (at + 1) * half, :] = lax.dot_general(
                square_ref[:, :, columns].reshape(sides * tokens, half),
                band_ref[...],
                OVER_ROWS,
                preferred_element_type=f32,
            ).astype(bf16)


def projection(kernel, name, place, square, band, wanted):
    width = band.shape[1]
    half = square.shape[1] // 2
    count = sum(len(blocks) for blocks in wanted)
    whole = pl.BlockSpec(memory_space=pltpu.VMEM)
    return pl.pallas_call(
        functools.partial(kernel, wanted),
        in_specs=[pl.BlockSpec(memory_space=pltpu.SMEM), whole, whole],
        out_specs=tuple(whole for _ in wanted),
        out_shape=tuple(
            jax.ShapeDtypeStruct((half * len(blocks), width), bf16) for blocks in wanted
        ),
        compiler_params=params(0, 16),
        cost_estimate=pl.CostEstimate(
            flops=2 * half * count * band.shape[0] * width,
            bytes_accessed=5_000_000,
            transcendentals=0,
        ),
        name=name,
    )(place, square, *kept(band))


def kept(*arrays):
    return [pltpu.with_memory_space_constraint(a, pltpu.VMEM) for a in arrays]


def outside(*arrays):
    return [pltpu.with_memory_space_constraint(a, pltpu.HBM) for a in arrays]


def params(grid=0, mib=16):
    return pltpu.CompilerParams(
        vmem_limit_bytes=mib * MIB,
        dimension_semantics=("arbitrary",) * grid if grid else None,
    )


def slot_codes(routes_wide, experts, pieces, tok_rows):
    columns = pieces * tok_rows
    expert = lax.broadcasted_iota(jnp.int32, (experts, columns), 0)
    named = expert == routes_wide[0:1, :]
    for choice in range(1, routes_wide.shape[0]):
        named = named | (expert == routes_wide[choice : choice + 1, :])
    before = lax.broadcasted_iota(jnp.int32, (columns, columns), 0)
    after = lax.broadcasted_iota(jnp.int32, (columns, columns), 1)
    earlier = (before // tok_rows == after // tok_rows) & (before < after)
    rank = jnp.dot(
        jnp.where(named, 1.0, 0.0).astype(bf16),
        jnp.where(earlier, 1.0, 0.0).astype(bf16),
        preferred_element_type=f32,
    )
    piece = (lax.broadcasted_iota(jnp.int32, (experts, columns), 1) // tok_rows).astype(f32)
    return jnp.where(named, piece * 8.0 + rank, -1.0)


def row_codes(shape, capacity, block, dim):
    row = lax.broadcasted_iota(jnp.int32, shape, dim) % block
    return ((row // capacity) * 8 + row % capacity).astype(f32)


def place_kernel(
    capacity, pre_ref, grad_ref, gain_ref, routes_ref, send_ref, code_ref, normed_ref, source
):
    tok_rows, features = pre_ref.shape
    experts, columns = code_ref.shape
    pieces = features // WIDE
    block = pieces * capacity
    group = pl.program_id(0)
    some = send_ref.shape[0]
    rows = some * block

    @pl.when(group == 0)
    def prepare():
        hidden = pre_ref[...].astype(f32)
        inverse = lax.rsqrt(jnp.mean(hidden * hidden, axis=-1, keepdims=True) + 1e-06)
        normed = (hidden * inverse * gain_ref[...]).astype(bf16)
        normed_ref[...] = normed
        for piece in range(pieces):
            at = pl.ds(piece * tok_rows, tok_rows)
            source[at, :WIDE] = normed[:, piece * WIDE : (piece + 1) * WIDE]
            source[at, WIDE:] = grad_ref[:, piece * WIDE : (piece + 1) * WIDE]
        code_ref[...] = slot_codes(routes_ref[...], experts, pieces, tok_rows)

    code = code_ref[pl.ds(pl.multiple_of(group * some, some), some), :]
    want = row_codes((some, block, columns), capacity, block, 1)
    hit = jnp.where(code[:, None, :] == want, 1.0, 0.0).astype(bf16).reshape(rows, columns)
    moved = jnp.dot(hit, source[...], preferred_element_type=f32).astype(bf16)
    send_ref[:, :block, :] = moved[:, :WIDE].reshape(some, block, WIDE)
    send_ref[:, block:, :] = moved[:, WIDE:].reshape(some, block, WIDE)


def place(pre_norm, out_grad, norm_gain, routes_wide, experts, capacity):
    tok_rows, features = pre_norm.shape
    pieces = features // WIDE
    block = pieces * capacity
    some = 8
    columns = pieces * tok_rows

    def whole(*shape):
        return pl.BlockSpec(shape, lambda i: (0,) * len(shape))

    return pl.pallas_call(
        functools.partial(place_kernel, capacity),
        grid=(experts // some,),
        in_specs=[
            whole(tok_rows, features),
            whole(tok_rows, features),
            whole(1, features),
            whole(*routes_wide.shape),
        ],
        out_specs=(
            pl.BlockSpec((some, 2 * block, WIDE), lambda i: (i, 0, 0)),
            whole(experts, columns),
            whole(tok_rows, features),
        ),
        out_shape=(
            pltpu.HBM((experts, 2 * block, WIDE), bf16),
            jax.ShapeDtypeStruct((experts, columns), f32),
            jax.ShapeDtypeStruct((tok_rows, features), bf16),
        ),
        scratch_shapes=[pltpu.VMEM((columns, 2 * WIDE), bf16)],
        compiler_params=params(1, 16),
        name="place",
    )(*outside(pre_norm, out_grad, norm_gain), routes_wide)


def order_matrix(capacity, block):
    at = np.arange(SOME * block)
    moved = (at % block) // capacity * (SOME * capacity) + at // block * capacity + at % capacity
    return jnp.asarray(moved[None, :] == at[:, None], bf16)


def spread_kernel(capacity, got_ref, order_ref, rows_ref):
    some, block, _ = got_ref.shape
    pieces = block // capacity
    span = SOME * capacity
    for group in range(some // SOME):
        source = got_ref[group * SOME : (group + 1) * SOME].reshape(SOME * block, WIDE)
        moved = jnp.dot(order_ref[...], source, preferred_element_type=f32).astype(bf16)
        for piece in range(pieces):
            rows_ref[group * span : (group + 1) * span, piece * WIDE : (piece + 1) * WIDE] = moved[
                piece * span : (piece + 1) * span
            ]


def spread(got, kind, order, capacity):
    sources, double, _ = got.shape
    block = double // 2
    features = block // capacity * WIDE
    some = 2 * SOME
    return pl.pallas_call(
        functools.partial(spread_kernel, capacity),
        grid=(sources // some,),
        in_specs=[
            pl.BlockSpec((some, block, WIDE), lambda i: (i, kind, 0)),
            pl.BlockSpec(order.shape, lambda i: (0, 0)),
        ],
        out_specs=pl.BlockSpec((some * capacity, features), lambda i: (i, 0)),
        out_shape=jax.ShapeDtypeStruct((sources * capacity, features), bf16),
        compiler_params=params(1),
        name="spread",
    )(got, order)


def forward_kernel(own_ref, other_ref, gate_ref, up_ref, gate_pre_ref, up_pre_ref):
    count = own_ref.shape[0]
    units = gate_ref.shape[2]
    tile = 256
    for mat, out in ((gate_ref, gate_pre_ref), (up_ref, up_pre_ref)):
        for n in range(units // tile):
            at = slice(n * tile, (n + 1) * tile)
            out[:count, at] = jnp.dot(own_ref[...], mat[0, :, at], preferred_element_type=f32)
            out[count:, at] = jnp.dot(other_ref[...], mat[0, :, at], preferred_element_type=f32)


def forward(own, other, w_gate, w_up):
    count, features = own.shape
    units = w_gate.shape[2]
    inside = pl.BlockSpec(memory_space=pltpu.VMEM)
    return pl.pallas_call(
        forward_kernel,
        in_specs=[inside] * 4,
        out_specs=(inside, inside),
        out_shape=(jax.ShapeDtypeStruct((2 * count, units), f32),) * 2,
        compiler_params=params(0, 10),
        cost_estimate=pl.CostEstimate(
            flops=8 * count * features * units, bytes_accessed=24_000_000, transcendentals=0
        ),
        name="forward",
    )(own, other, *kept(w_gate, w_up))


def hidden_kernel(
    capacity, own_ref, other_ref, down_ref, gate_pre_ref, up_pre_ref, gg_ref, gu_ref, *part_refs
):
    count = own_ref.shape[0]
    units = down_ref.shape[1]
    tile = 256
    for half, rows in enumerate((own_ref, other_ref)):
        here = slice(half * count, (half + 1) * count)
        part = jnp.zeros((count, 1), f32)
        for n in range(units // tile):
            at = slice(n * tile, (n + 1) * tile)
            upstream = lax.dot_general(
                rows[...], down_ref[0, at, :], OVER_LAST, preferred_element_type=f32
            )
            gate_pre = gate_pre_ref[here, at]
            up_pre = up_pre_ref[here, at]
            sig = jax.nn.sigmoid(gate_pre)
            grad_up = upstream * (gate_pre * sig)
            part = part + jnp.sum(grad_up * up_pre, axis=-1, keepdims=True)
            gu_ref[here, at] = grad_up.astype(bf16)
            gg_ref[here, at] = (
                upstream * up_pre * sig * (1.0 + gate_pre * (1.0 - sig))
            ).astype(bf16)
        part_rows = part_refs[half].shape[0]
        rows_of = lax.broadcasted_iota(jnp.int32, (part_rows, count), 0)
        slots_of = lax.broadcasted_iota(jnp.int32, (part_rows, count), 1)
        same = (rows_of // 8 == slots_of // capacity) & (rows_of % 8 == slots_of % capacity)
        part_refs[half][...] = jnp.dot(
            jnp.where(same, 1.0, 0.0).astype(bf16),
            jnp.broadcast_to(part.astype(bf16), (count, 128)),
            preferred_element_type=f32,
        )


def hidden_grads(own, other, w_down, gate_pre, up_pre, capacity):
    count, features = own.shape
    units = w_down.shape[1]
    inside = pl.BlockSpec(memory_space=pltpu.VMEM)
    return pl.pallas_call(
        functools.partial(hidden_kernel, capacity),
        in_specs=[inside] * 5,
        out_specs=(inside,) * 4,
        out_shape=(
            jax.ShapeDtypeStruct((2 * count, units), bf16),
            jax.ShapeDtypeStruct((2 * count, units), bf16),
            jax.ShapeDtypeStruct((count // capacity * 8, 128), f32),
            jax.ShapeDtypeStruct((count // capacity * 8, 128), f32),
        ),
        compiler_params=params(0, 10),
        cost_estimate=pl.CostEstimate(
            flops=4 * count * features * units, bytes_accessed=24_000_000, transcendentals=0
        ),
        name="hidden_grads",
    )(own, other, *kept(w_down), gate_pre, up_pre)


def term_kernel(half, gg_ref, gu_ref, gate_ref, up_ref, term_ref):
    count = term_ref.shape[0]
    here = slice(half * count, (half + 1) * count)
    features = gate_ref.shape[1]
    tile = 512
    for n in range(features // tile):
        at = slice(n * tile, (n + 1) * tile)
        term = lax.dot_general(
            gg_ref[here, :], gate_ref[0, at, :], OVER_LAST, preferred_element_type=f32
        )
        term = term + lax.dot_general(
            gu_ref[here, :], up_ref[0, at, :], OVER_LAST, preferred_element_type=f32
        )
        term_ref[:, at] = term.astype(bf16)


def terms(grad_gate, grad_up, w_gate, w_up, half):
    count = grad_gate.shape[0] // 2
    units = grad_gate.shape[1]
    features = w_gate.shape[1]
    inside = pl.BlockSpec(memory_space=pltpu.VMEM)
    return pl.pallas_call(
        functools.partial(term_kernel, half),
        in_specs=[inside] * 4,
        out_specs=inside,
        out_shape=jax.ShapeDtypeStruct((count, features), bf16),
        compiler_params=params(0, 10),
        cost_estimate=pl.CostEstimate(
            flops=4 * count * features * units, bytes_accessed=17_000_000, transcendentals=0
        ),
        name="terms",
    )(grad_gate, grad_up, *kept(w_gate, w_up))


def pack_kernel(capacity, own_ref, other_ref, order_ref, send_ref, held):
    rows, features = own_ref.shape
    pieces = features // WIDE
    span = SOME * capacity
    for group in range(rows // span):
        here = slice(group * span, (group + 1) * span)
        for piece in range(pieces):
            at = slice(piece * WIDE, (piece + 1) * WIDE)
            held[group, pl.ds(piece * span, span), :] = (
                own_ref[here, at].astype(f32) + other_ref[here, at].astype(f32)
            ).astype(bf16)
        moved = lax.dot_general(
            order_ref[...], held[group], OVER_ROWS, preferred_element_type=f32
        )
        send_ref[group * SOME : (group + 1) * SOME] = moved.astype(bf16).reshape(
            SOME, -1, WIDE
        )


def pack(own, other, order, capacity):
    count, features = own.shape
    block = features // WIDE * capacity
    groups = 2
    span = groups * SOME * capacity
    return pl.pallas_call(
        functools.partial(pack_kernel, capacity),
        grid=(count // span,),
        in_specs=[
            pl.BlockSpec((span, features), lambda i: (i, 0)),
            pl.BlockSpec((span, features), lambda i: (i, 0)),
            pl.BlockSpec(order.shape, lambda i: (0, 0)),
        ],
        out_specs=pl.BlockSpec((groups * SOME, block, WIDE), lambda i: (i, 0, 0)),
        out_shape=pltpu.HBM((count // capacity, block, WIDE), bf16),
        scratch_shapes=[pltpu.VMEM((groups, SOME * block, WIDE), bf16)],
        compiler_params=params(1),
        name="pack",
    )(own, other, order)


def mix_kernel(capacity, code_ref, gate_ref, mix_ref):
    some, columns = code_ref.shape
    rows = mix_ref.shape[1]
    block = rows // some
    want = row_codes((some, block, columns), capacity, block, 1)
    mixing = jnp.where(code_ref[...][:, None, :] == want, gate_ref[...][:, None, :], 0.0)
    mixing = mixing.reshape(rows, columns)
    high = mixing.astype(bf16)
    low = (mixing - high.astype(f32)).astype(bf16)
    mix_ref[:columns, :] = high.T
    mix_ref[columns:, :] = low.T


def mixings(code, gate_wide, capacity, block):
    experts, columns = code.shape
    some = 8
    return pl.pallas_call(
        functools.partial(mix_kernel, capacity),
        grid=(experts // some,),
        in_specs=[
            pl.BlockSpec((some, columns), lambda i: (i, 0)),
            pl.BlockSpec((some, columns), lambda i: (i, 0)),
        ],
        out_specs=pl.BlockSpec((2 * columns, some * block), lambda i: (0, i)),
        out_shape=jax.ShapeDtypeStruct((2 * columns, experts * block), bf16),
        compiler_params=params(1),
        name="mixings",
    )(code, gate_wide)


def finish_kernel(
    mix_ref, back_ref, pre_ref, grad_ref, gain_ref, logit_ref, router_ref, normed_ref,
    residual_ref, bands_ref, small_ref,
):
    tok_rows, features = pre_ref.shape
    columns = mix_ref.shape[0] // 2
    pieces = features // WIDE
    both = jnp.dot(mix_ref[...], back_ref[...], preferred_element_type=f32)
    expert_grad = both[:columns] + both[columns:]
    hidden = pre_ref[...].astype(f32)
    inverse = lax.rsqrt(jnp.mean(hidden * hidden, axis=-1, keepdims=True) + 1e-06)
    router_term = jnp.dot(logit_ref[...], router_ref[...], preferred_element_type=f32)
    experts = logit_ref.shape[1]
    router_part = lax.dot_general(
        logit_ref[...], normed_ref[...], OVER_ROWS, preferred_element_type=f32
    )
    spare = small_ref.shape[1] - experts
    per_band = bands_ref.shape[2] // WIDE
    moment = jnp.zeros((tok_rows, 1), f32)
    normed_grads = []
    for piece in range(pieces):
        at = slice(piece * WIDE, (piece + 1) * WIDE)
        normed_grad = (
            expert_grad[piece * tok_rows : (piece + 1) * tok_rows] + router_term[:, at]
        )
        normed_grads.append(normed_grad)
        small_ref[piece, :experts, :] = router_part[:, at]
        small_ref[piece, experts:, :] = jnp.broadcast_to(
            jnp.sum(normed_grad * hidden[:, at] * inverse, axis=0, keepdims=True), (spare, WIDE)
        )
        moment = moment + jnp.sum(
            hidden[:, at] * gain_ref[:, at] * normed_grad, axis=-1, keepdims=True
        )
    factor = inverse * inverse * inverse * (moment / features)
    for piece in range(pieces):
        at = slice(piece * WIDE, (piece + 1) * WIDE)
        residual = (
            grad_ref[:, at].astype(f32)
            + inverse * gain_ref[:, at] * normed_grads[piece]
            - hidden[:, at] * factor
        ).astype(bf16)
        residual_ref[:, at] = residual
        inner = piece % per_band * WIDE
        bands_ref[piece // per_band, :, inner : inner + WIDE] = residual


def finish(mix, back, pre_norm, out_grad, norm_gain, logit_full, router_wide, normed, bands):
    tok_rows, features = pre_norm.shape
    experts = logit_full.shape[1]
    return pl.pallas_call(
        finish_kernel,
        out_shape=(
            jax.ShapeDtypeStruct((tok_rows, features), bf16),
            jax.ShapeDtypeStruct((bands, tok_rows, features // bands), bf16),
            jax.ShapeDtypeStruct((features // WIDE, experts + 8, WIDE), f32),
        ),
        compiler_params=params(0, 24),
        name="finish",
    )(
        mix,
        *outside(back, pre_norm, out_grad, norm_gain),
        logit_full,
        router_wide,
        *outside(normed),
    )


def shards(
    pre_norm,
    out_grad,
    routes,
    gate_probs,
    norm_gain,
    router_weight,
    w_gate,
    w_up,
    w_down,
    context,
    out_weight,
):
    tok_rows, features = pre_norm.shape
    top = routes.shape[1]
    experts = router_weight.shape[1]
    capacity = tok_rows * top * 3 // (2 * experts)
    pieces = features // WIDE
    block = pieces * capacity
    gain = norm_gain.reshape(1, features)

    routes_wide = jnp.tile(routes.T, (1, pieces))
    send, code, normed = place(pre_norm, out_grad, gain, routes_wide, experts, capacity)

    got = exchange(send, CHIP)

    order = order_matrix(capacity, block)
    got, code, normed, out_weight, context, routes, gate_probs = lax.optimization_barrier(
        (got, code, normed, out_weight, context, routes, gate_probs)
    )

    weight_band = lax.all_gather(out_weight, "x", axis=0, tiled=True)
    context_band = lax.all_gather(context, "y", axis=0, tiled=True)

    own_tokens = spread(got, 0, order, capacity)
    other_tokens = swap_cores(own_tokens)
    own_grads = spread(got, 1, order, capacity)
    other_grads = swap_cores(own_grads)
    gate_pre, up_pre = forward(own_tokens, other_tokens, w_gate, w_up)
    grad_gate, grad_up, own_part, other_part = hidden_grads(
        own_grads, other_grads, w_down, gate_pre, up_pre, capacity
    )
    grad_gate, weight_band = lax.optimization_barrier((grad_gate, weight_band))
    other_part = swap_cores(other_part)
    other_term = terms(grad_gate, grad_up, w_gate, w_up, 1)
    other_term = swap_cores(other_term)
    own_term = terms(grad_gate, grad_up, w_gate, w_up, 0)
    own_term, context_band = lax.optimization_barrier((own_term, context_band))
    send_back = pack(own_term, other_term, order, capacity)
    send_back, own_part, other_part = lax.optimization_barrier(
        (send_back, own_part, other_part)
    )
    part = (own_part + other_part).reshape(experts, 8, 128)
    part = exchange(part, CHIP)[:, :capacity, 0]
    send_back, part, code, routes, gate_probs, router_weight = lax.optimization_barrier(
        (send_back, part, code, routes, gate_probs, router_weight)
    )
    got_back = exchange(send_back, CHIP).reshape(experts * block, WIDE)

    named = routes[:, :, None] == jnp.arange(experts, dtype=jnp.int32)[None, None, :]
    gate_of = jnp.sum(jnp.where(named, gate_probs[:, :, None], 0.0), axis=1)
    mix = mixings(code, jnp.tile(gate_of.T, (1, pieces)), capacity, block)
    router_wide = router_weight.T

    slot = code[:, :tok_rows].T
    at_slot = jnp.arange(capacity, dtype=jnp.int32).astype(f32)
    grad_of = jnp.sum(
        jnp.where(slot[:, :, None] == at_slot[None, None, :], part[None], 0.0), axis=2
    )
    gate_grad = jnp.sum(jnp.where(named, grad_of[:, None, :], 0.0), axis=2)
    weighted = jnp.sum(gate_of * grad_of, axis=-1, keepdims=True)
    logit_full = (gate_of * (grad_of - weighted)).astype(bf16)
    got_back, logit_full, mix, router_wide = lax.optimization_barrier(
        (got_back, logit_full, mix, router_wide)
    )

    residual_grad, bands, small = finish(
        mix, got_back, pre_norm, out_grad, gain, logit_full, router_wide, normed, lax.axis_size("y")
    )

    square, small = gather_square(bands, small)
    context_grad, weight_grad, small = ring_scatter(
        square,
        (
            (functools.partial(projection, context_kernel, "context_part"), weight_band, "y"),
            (functools.partial(projection, weight_kernel, "weight_part"), context_band, "x"),
        ),
        small,
    )
    router_grad = small[:experts].T
    gain_grad = small[experts]
    return (residual_grad, gate_grad, router_grad, gain_grad, context_grad, weight_grad)


def solution(mesh):
    devices = np.asarray(mesh.devices)
    fine = Mesh(devices.reshape(4, 4, 4, 2), EVERY)
    rows = P(EVERY, None)
    cube = P(EVERY, None, None)
    split = P(DP, TENSOR)
    return jax.shard_map(
        shards,
        mesh=fine,
        in_specs=(rows, rows, rows, rows, P(), P(), cube, cube, cube, split, split),
        out_specs=(rows, rows, P(TENSOR, None), P(TENSOR), split, split),
        check_vma=False,
    )
```

time: 377 us -> 332 us (0.88)
  waiting for transfers between devices: 159 us -> 60 us
  blocking collectives: 10.3 us -> 102 us
  local copies, waits for them, and re-layouts: 48.7 us -> 29.1 us
  starting transfers between devices: 55 us -> 42 us
  Pallas kernels: 64.7 us -> 74.6 us
  matrix products: 9.79 us -> 0 us
    all_to_all x1 -> x2, blocking collectives: 10.3 us -> 102 us  [exchange(): return lax.all_to_all(value, axes, split_axis=0, concat_axis=0, tiled=True)]
    reduce_scatter x1 -> x0, waiting for transfers between devices: 51.1 us -> none  [shards(): lax.psum_scatter(router_part, TENSOR, scatter_dimension=0, tiled=True)]
    all_to_all x3 -> x1, waiting for transfers between devices: 78.9 us -> 36.4 us  [exchange(): return lax.all_to_all(value, axes, split_axis=0, concat_axis=0, tiled=True)]
    all_to_all x3 -> x1, starting transfers between devices: 32.7 us -> 5.73 us  [exchange(): return lax.all_to_all(value, axes, split_axis=0, concat_axis=0, tiled=True)]
    pallas_call x4 -> x11, Pallas kernels: 24.4 us -> 43.1 us  [the longest x2 11.8 us: terms(): pl.pallas_call(functools.partial(term_kernel, half), in_specs=[inside] *...]
    ppermute x15 -> x23, starting transfers between devices: 20.9 us -> 33.8 us  [the longest x17 25.1 us: shift(): lax.ppermute(value, axis, [(i, (i + step) % size) for i in range(size)])]
    dot_general x6 -> x0, matrix products: 9.79 us -> none  [the longest x4 5.06 us: context_block(): return jnp.dot(rows, weight_band, preferred_element_type=f32).astype(bf16)]
    pallas_call x2, Pallas kernels: 14.8 us -> 6.26 us  [spread(): pl.pallas_call(functools.partial(spread_kernel, capacity), grid=(sources...]
  transfers between devices with their start and end apart: 26 -> 35, of which waited for: 12 -> 12; matrix products, arithmetic and copies ran while one was open for 7% -> 2% of each run, Pallas kernels for 13% -> 18%
where the time goes in v2:
time: 332 us; the launch traced here: 328 us
  blocking collectives  102 us (31%)
  Pallas kernels  74.6 us (22%)
  waiting for transfers between devices  60 us (18%)
  starting transfers between devices  42 us (13%)
  local copies, waits for them, and re-layouts  29.1 us (9%)
  between operations  14.7 us (4%)
  other arithmetic  5.39 us (2%)
    all_to_all x2, blocking collectives, exchange(): return lax.all_to_all(value, axes, split_axis=0, concat_axis=0, tiled=True)  102 us
    all_to_all x1, waiting for transfers between devices, exchange(): return lax.all_to_all(value, axes, split_axis=0, concat_axis=0, tiled=True)  36.4 us
    unnamed x68, local copies, waits for them, and re-layouts  26.6 us
    ppermute x17, starting transfers between devices, shift(): lax.ppermute(value, axis, [(i, (i + step) % size) for i in range(size)])  25.1 us
    ppermute x17, waiting for transfers between devices, shift(): lax.ppermute(value, axis, [(i, (i + step) % size) for i in range(size)])  13.5 us
    pallas_call x1, Pallas kernels, forward(): pl.pallas_call(forward_kernel, in_specs=[inside] * 4, out_specs=(inside,...  12.9 us
    pallas_call x2, Pallas kernels, terms(): pl.pallas_call(functools.partial(term_kernel, half), in_specs=[inside] *...  11.8 us
    pallas_call x1, Pallas kernels, hidden_grads(): pl.pallas_call(functools.partial(hidden_kernel, capacity), in_specs=[insi...  10.5 us
  transfers between devices with their start and end apart: 35, of which 12 were waited for; matrix products, arithmetic and copies ran while one was open for 2% of the time, Pallas kernels for 18%

profile of v2, /device:TPU:0, one launch (start us, length us, event | category | flops | bytes accessed | tf_op | source)
XLA Modules:
  0.0 328.1 jit_solution(2882528081760496812)
XLA Ops:
  8.0 6.9 %place.1 = (bf16[64,96,512]{2,1,0:T(8,128)(2,1)}, f32[64,256]{1,0:T(8,128)S(1)}, bf16[32,4096]{1,0:T(8,128)(2,1)S(1)}) custom-call(bf16[32,4096]{1,0:T(8,128)(2,1)} %pre_ref.3, bf16[32,4096]{1,0:T(8,128)(2,1)} %grad_ref.3, f32[1,4096]{1,0:T(1,128)} %bitcast.49, s32[8,256]{1,0:T(8,128)S(1)} %tile.9.routes_ref), custom_call_target="tpu_custom_call" | custom-call | tf_op jit(solution)/shard_map/place/pallas_call | solution.py:319
  14.9 86.3 %all_to_all.15.got_ref = bf16[64,96,512]{2,1,0:T(8,128)(2,1)} all-to-all(bf16[64,96,512]{2,1,0:T(8,128)(2,1)} %get-tuple-element.88), channel_id=1, replica_groups=mesh['y'=4,'x'=4,'z'=4,'core'=2] {'y','x','z'}, dimensions={0} | all-to-all | bytes 12582912 | tf_op jit(solution)/shard_map/all_to_all | solution.py:30
  101.3 2.8 copy-done
  104.1 3.7 %spread.3.own_ref = bf16[384,4096]{1,0:T(8,128)(2,1)} custom-call(bf16[64,96,512]{2,1,0:T(8,128)(2,1)S(1)} %copy-done, bf16[384,384]{1,0:T(8,128)(2,1)S(1)} %copy-done.13), custom_call_target="tpu_custom_call" | custom-call | tf_op jit(solution)/shard_map/spread/pallas_call | solution.py:368
  107.8 2.5 spread.2.own_ref
  110.3 0.8 collective-permute-start
  111.1 2.7 collective-permute-done.1.other_ref
  113.8 2.9 copy-done.1
  116.6 2.9 copy-done.3
  119.5 12.9 %forward.1 = (f32[768,768]{1,0:T(8,128)S(1)}, f32[768,768]{1,0:T(8,128)S(1)}) custom-call(bf16[384,4096]{1,0:T(8,128)(2,1)} %spread.3.own_ref, bf16[384,4096]{1,0:T(8,128)(2,1)} %collective-permute-done.1.other_ref, bf16[1,4096,768]{2,1,0:T(8,128)(2,1)S(1)} %copy-done.1, bf16[1,4096,768]{2,1,0:T(8,128)(2,1)S(1)} %copy-done.3), custom_call_target="tpu_custom_call" | custom-call | flops 9663676416 | bytes 24000000 | tf_op jit(solution)/shard_map/forward/pallas_call | solution.py:397
  132.5 1.9 copy-done.12
  134.3 10.5 %hidden_grads.1 = (bf16[768,768]{1,0:T(8,128)(2,1)S(1)}, bf16[768,768]{1,0:T(8,128)(2,1)S(1)}, f32[512,128]{1,0:T(8,128)S(1)}, f32[512,128]{1,0:T(8,128)}) custom-call(bf16[384,4096]{1,0:T(8,128)(2,1)S(1)} %copy-done.12, bf16[384,4096]{1,0:T(8,128)(2,1)} %collective-permute-done.other_ref, bf16[1,768,4096]{2,1,0:T(8,128)(2,1)S(1)} %copy-done.19, ...), custom_call_target="tpu_custom_call" | custom-call | flops 4831838208 | bytes 24000000 | tf_op jit(solution)/shard_map/hidden_grads/pallas_call | solution.py:448
  144.8 0.7 copy-done.17
  145.6 3.7 %copy-done.2 = bf16[1,4096,768]{2,1,0:T(8,128)(2,1)S(1)} copy-done((bf16[1,4096,768]{2,1,0:T(8,128)(2,1)S(1)}, bf16[1,4096,768]{2,1,0:T(8,128)(2,1)}, u32[]{:S(2)}) %copy-start.2) | copy-done | bytes 6291480
  149.2 2.9 copy-done.4
  152.1 6.7 %terms.3 = bf16[384,4096]{1,0:T(8,128)(2,1)} custom-call(bf16[768,768]{1,0:T(8,128)(2,1)S(1)} %get-tuple-element.96.gg_ref, bf16[768,768]{1,0:T(8,128)(2,1)S(1)} %get-tuple-element.97.gu_ref, bf16[1,4096,768]{2,1,0:T(8,128)(2,1)S(1)} %copy-done.2, bf16[1,4096,768]{2,1,0:T(8,128)(2,1)S(1)} %copy-done.4), custom_call_target="tpu_custom_call" | custom-call | flops 4831838208 | bytes 17000000 | tf_op jit(solution)/shard_map/terms/pallas_call | solution.py:487
  159.3 1.3 copy-done.8
  160.6 1.3 copy-done.10
  161.9 5.1 %terms.2.own_ref = bf16[384,4096]{1,0:T(8,128)(2,1)S(1)} custom-call(bf16[768,768]{1,0:T(8,128)(2,1)S(1)} %copy-done.8, bf16[768,768]{1,0:T(8,128)(2,1)S(1)} %copy-done.10, bf16[1,4096,768]{2,1,0:T(8,128)(2,1)S(1)} %copy-done.2, bf16[1,4096,768]{2,1,0:T(8,128)(2,1)S(1)} %copy-done.4), custom_call_target="tpu_custom_call" | custom-call | flops 4831838208 | bytes 17000000 | tf_op jit(solution)/shard_map/terms/pallas_call | solution.py:487
  167.0 5.4 %pack.1 = bf16[64,48,512]{2,1,0:T(8,128)(2,1)} custom-call(bf16[384,4096]{1,0:T(8,128)(2,1)S(1)} %terms.2.own_ref, bf16[384,4096]{1,0:T(8,128)(2,1)} %collective-permute-done.2.other_ref, bf16[384,384]{1,0:T(8,128)(2,1)S(1)} %copy-done.13), custom_call_target="tpu_custom_call" | custom-call | tf_op jit(solution)/shard_map/pack/pallas_call | solution.py:524
  172.4 1.0 add_bitcast_fusion
  173.4 16.2 %all_to_all.16 = f32[64,8,128]{2,1,0:T(8,128)S(1)} all-to-all(f32[64,8,128]{2,1,0:T(8,128)S(1)} %add_bitcast_fusion), channel_id=1, replica_groups=mesh['y'=4,'x'=4,'z'=4,'core'=2] {'y','x','z'}, dimensions={0} | all-to-all | bytes 524288 | tf_op jit(solution)/shard_map/all_to_all | solution.py:30
  189.7 5.7 %all-to-all-start.2 = ((bf16[64,48,512]{2,1,0:T(8,128)(2,1)}), bf16[64,48,512]{2,1,0:T(8,128)(2,1)}, u32[]{:S(2)}, u32[]{:S(2)}) async-start(bf16[64,48,512]{2,1,0:T(8,128)(2,1)} %pack.1), calls=%async_computation.2 | async-start | bytes 6291456 | tf_op jit(solution)/shard_map/all_to_all | solution.py:30
  195.8 0.8 select_reduce_fusion
  196.7 2.0 mixings.1.mix_ref
  198.9 36.4 %all-to-all-done.2 = bf16[64,48,512]{2,1,0:T(8,128)(2,1)} async-done(((bf16[64,48,512]{2,1,0:T(8,128)(2,1)}), bf16[64,48,512]{2,1,0:T(8,128)(2,1)}, u32[]{:S(2)}, u32[]{:S(2)}) %all-to-all-start.2) | async-done | bytes 3145760 | tf_op jit(solution)/shard_map/all_to_all | solution.py:30
  235.3 1.0 copy-done.15
  236.4 4.9 %finish.1 = (bf16[32,4096]{1,0:T(8,128)(2,1)}, bf16[4,32,1024]{2,1,0:T(8,128)(2,1)S(1)}, f32[8,72,512]{2,1,0:T(8,128)S(1)}) custom-call(bf16[512,3072]{1,0:T(8,128)(2,1)S(1)} %mixings.1.mix_ref, bf16[3072,512]{1,0:T(8,128)(2,1)} %bitcast.4.back_ref, bf16[32,4096]{1,0:T(8,128)(2,1)} %pre_ref.3, bf16[32,4096]{1,0:T(8,128)(2,1)} %grad_ref.3, ...), custom_call_target="tpu_custom_call" | custom-call | tf_op jit(solution)/shard_map/finish/pallas_call | solution.py:619
  241.3 1.1 copy-done.14
  243.0 3.5 %collective-permute-start.5 = (bf16[32,1024]{1,0:T(8,128)(2,1)S(1)}, bf16[32,1024]{1,0:T(8,128)(2,1)S(1)}, u32[]{:S(2)}, u32[]{:S(2)}) collective-permute-start(bf16[32,1024]{1,0:T(8,128)(2,1)S(1)} %get-tuple-element.183), channel_id=1, source_target_pairs={{0,64},{32,96},{64,0},{96,32},{1,65},{33,97},{65,1},{97,33},{2,66}... | collective-permute-start | bytes 196616 | tf_op jit(solution)/shard_map/ppermute | solution.py:44
  246.5 2.2 collective-permute-done.4
  248.8 1.6 collective-permute-done.5
  250.8 1.2 bitcast_add_fusion
  252.0 0.9 copy-done.20
  253.0 1.1 collective-permute-start.15
  254.0 1.1 collective-permute-start.16
  255.2 2.3 collective-permute-start.17
  257.5 3.2 collective-permute-start.9
  261.9 1.0 fusion.1
  262.9 2.5 collective-permute-start.18
  265.7 3.3 collective-permute-done.18
  269.0 0.8 collective-permute-done.19
  269.8 1.8 collective-permute-start.20
  272.3 3.2 collective-permute-done.20
  275.5 1.0 add_add_fusion.1
  276.5 1.5 collective-permute-start.21
  278.0 1.9 collective-permute-start.22
  279.9 0.8 collective-permute-start.23
  280.7 3.9 %gather_square.1.square_ref = bf16[4,256,1024]{2,1,0:T(8,128)(2,1)S(1)} custom-call(s32[3]{0:T(128)S(1)} %pad_add_fusion.place_ref, bf16[4,32,1024]{2,1,0:T(8,128)(2,1)S(1)} %pad_maximum_fusion.refs_0_, bf16[4,32,1024]{2,1,0:T(8,128)(2,1)S(1)} %collective-permute-done.8.refs_1_, bf16[4,32,1024]{2,1,0:T(8,128)(2,1)S(1)} %collective-permute-done.10.refs_2_, ...), custom_call_target="tpu_custom_call" | custom-call | tf_op jit(solution)/shard_map/gather_square/pallas_call | solution.py:178
  284.6 1.3 context_part.2
  286.1 1.4 weight_part.2
  287.6 0.7 collective-permute-start.24
  288.3 2.6 collective-permute-start.25
  290.9 3.4 %collective-permute-start.27 = (bf16[256,1024]{1,0:T(8,128)(2,1)S(1)}, bf16[256,1024]{1,0:T(8,128)(2,1)S(1)}, u32[]{:S(2)}, u32[]{:S(2)}) collective-permute-start(bf16[256,1024]{1,0:T(8,128)(2,1)S(1)} %get-tuple-element.143), channel_id=1, source_target_pairs={{0,24},{8,0},{16,8},{24,16},{1,25},{9,1},{17,9},{25,17},{2,26},{10... | collective-permute-start | bytes 1572872 | tf_op jit(solution)/shard_map/ppermute | solution.py:44
  294.3 1.3 weight_part.3
  295.6 1.3 context_part.3
  296.9 3.5 %collective-permute-done.24.refs_1_.refs_2_ = bf16[256,1024]{1,0:T(8,128)(2,1)S(1)} collective-permute-done((bf16[256,1024]{1,0:T(8,128)(2,1)S(1)}, bf16[256,1024]{1,0:T(8,128)(2,1)S(1)}, u32[]{:S(2)}, u32[]{:S(2)}) %collective-permute-start.24) | collective-permute-done | bytes 524320 | tf_op jit(solution)/shard_map/ppermute | solution.py:44
  300.4 2.7 collective-permute-done.26.refs_5_.refs_8_
  303.1 0.8 copy-done.23
  304.1 1.8 pass_on.1
  305.9 3.2 collective-permute-start.29
  309.1 3.2 collective-permute-start.31
  314.3 2.4 collective-permute-done.30.refs_10_
  318.1 3.0 close.1
  (121 shorter events, 9.4 us)
Async XLA Ops:
  7.2 138.4 %all-gather.3.cloned.1.call-start = ((), (), s32[]{:S(2)}) async-start(), calls=%async_computation.3 | async-start | bytes 2621440 | tf_op jit(solution)/shard_map/all_gather | solution.py:668
  14.9 86.3 %copy-start.16 = (bf16[32,4096]{1,0:T(8,128)(2,1)}, bf16[32,4096]{1,0:T(8,128)(2,1)S(1)}, u32[]{:S(2)}) copy-start(bf16[32,4096]{1,0:T(8,128)(2,1)S(1)} %get-tuple-element.118.normed_ref) | copy-start | bytes 786436
  14.9 86.4 %copy-start.13 = (bf16[384,384]{1,0:T(8,128)(2,1)S(1)}, bf16[384,384]{1,0:T(8,128)(2,1)}, u32[]{:S(2)}) copy-start(bf16[384,384]{1,0:T(8,128)(2,1)} %constant.69.clone.order_ref) | copy-start | bytes 884740
  101.2 65.7 %all-gather.5.cloned.1.call-start = ((), (), s32[]{:S(2)}) async-start(), calls=%async_computation.4 | async-start | bytes 2621440 | tf_op jit(solution)/shard_map/all_gather | solution.py:669
  101.3 2.8 copy-start
  107.8 6.0 %collective-permute-start.1 = (bf16[384,4096]{1,0:T(8,128)(2,1)}, bf16[384,4096]{1,0:T(8,128)(2,1)}, u32[]{:S(2)}, u32[]{:S(2)}) collective-permute-start(bf16[384,4096]{1,0:T(8,128)(2,1)} %spread.3.own_ref), channel_id=1, source_target_pairs={{0,1},{1,0},{2,3},{3,2},{4,5},{5,4},{6,7},{7,6},{8,9},{9,8},{10,11... | collective-permute-start | bytes 9437192 | tf_op jit(solution)/shard_map/ppermute | solution.py:26
  110.3 22.1 %copy-start.11 = (bf16[384,4096]{1,0:T(8,128)(2,1)}, bf16[384,4096]{1,0:T(8,128)(2,1)S(1)}, u32[]{:S(2)}) copy-start(bf16[384,4096]{1,0:T(8,128)(2,1)S(1)} %spread.2.own_ref) | copy-start | bytes 9437188
  110.3 22.1 %collective-permute-start = (bf16[384,4096]{1,0:T(8,128)(2,1)S(1)}, bf16[384,4096]{1,0:T(8,128)(2,1)}, u32[]{:S(2)}, u32[]{:S(2)}) collective-permute-start(bf16[384,4096]{1,0:T(8,128)(2,1)S(1)} %spread.2.own_ref), channel_id=1, source_target_pairs={{0,1},{1,0},{2,3},{3,2},{4,5},{5,4},{6,7},{7,6},{8,9},{9,8},{10,11... | collective-permute-start | bytes 9437192 | tf_op jit(solution)/shard_map/ppermute | solution.py:26
  113.8 2.9 copy-start.1
  116.6 2.9 copy-start.3
  119.5 12.9 %copy-start.19 = (bf16[1,768,4096]{2,1,0:T(8,128)(2,1)S(1)}, bf16[1,768,4096]{2,1,0:T(8,128)(2,1)}, u32[]{:S(2)}) copy-start(bf16[1,768,4096]{2,1,0:T(8,128)(2,1)} %down_ref.1) | copy-start | bytes 18874372
  132.5 1.9 copy-start.12
  145.5 13.3 %copy-start.7 = (bf16[768,768]{1,0:T(8,128)(2,1)}, bf16[768,768]{1,0:T(8,128)(2,1)S(1)}, u32[]{:S(2)}) copy-start(bf16[768,768]{1,0:T(8,128)(2,1)S(1)} %get-tuple-element.96.gg_ref) | copy-start | bytes 3538948
  145.5 13.3 %copy-start.9 = (bf16[768,768]{1,0:T(8,128)(2,1)}, bf16[768,768]{1,0:T(8,128)(2,1)S(1)}, u32[]{:S(2)}) copy-start(bf16[768,768]{1,0:T(8,128)(2,1)S(1)} %get-tuple-element.97.gu_ref) | copy-start | bytes 3538948
  145.6 3.7 %copy-start.2 = (bf16[1,4096,768]{2,1,0:T(8,128)(2,1)S(1)}, bf16[1,4096,768]{2,1,0:T(8,128)(2,1)}, u32[]{:S(2)}) copy-start(bf16[1,4096,768]{2,1,0:T(8,128)(2,1)} %gate_ref.5) | copy-start | bytes 18874372
  149.2 2.9 copy-start.4
  158.8 8.2 %collective-permute-start.2 = (bf16[384,4096]{1,0:T(8,128)(2,1)}, bf16[384,4096]{1,0:T(8,128)(2,1)}, u32[]{:S(2)}, u32[]{:S(2)}) collective-permute-start(bf16[384,4096]{1,0:T(8,128)(2,1)} %terms.3), channel_id=1, source_target_pairs={{0,1},{1,0},{2,3},{3,2},{4,5},{5,4},{6,7},{7,6},{8,9},{9,8},{10,11... | collective-permute-start | bytes 9437192 | tf_op jit(solution)/shard_map/ppermute | solution.py:26
  158.9 13.5 %collective-permute-start.3 = (f32[512,128]{1,0:T(8,128)}, f32[512,128]{1,0:T(8,128)}, u32[]{:S(2)}, u32[]{:S(2)}) collective-permute-start(f32[512,128]{1,0:T(8,128)} %get-tuple-element.101), channel_id=1, source_target_pairs={{0,1},{1,0},{2,3},{3,2},{4,5},{5,4},{6,7},{7,6},{8,9},{9,8},{10,11... | collective-permute-start | bytes 786440 | tf_op jit(solution)/shard_map/ppermute | solution.py:26
  159.3 1.3 copy-start.8
  160.6 1.3 copy-start.10
  167.0 5.4 %copy-start.18 = (f32[512,128]{1,0:T(8,128)S(1)}, f32[512,128]{1,0:T(8,128)}, u32[]{:S(2)}) copy-start(f32[512,128]{1,0:T(8,128)} %copy-done.17) | copy-start | bytes 786436
  189.7 5.9 %copy-start.31 = (s32[32,8]{0,1:T(8,128)S(1)}, s32[32,8]{0,1:T(8,128)}, u32[]{:S(2)}) copy-start(s32[32,8]{0,1:T(8,128)} %param.14) | copy-start | bytes 3076
  189.7 5.9 %copy-start.32 = (f32[32,8]{0,1:T(8,128)S(1)}, f32[32,8]{0,1:T(8,128)}, u32[]{:S(2)}) copy-start(f32[32,8]{0,1:T(8,128)} %param.15) | copy-start | bytes 3076
  189.7 45.6 %all-to-all-start.2 = ((bf16[64,48,512]{2,1,0:T(8,128)(2,1)}), bf16[64,48,512]{2,1,0:T(8,128)(2,1)}, u32[]{:S(2)}, u32[]{:S(2)}) async-start(bf16[64,48,512]{2,1,0:T(8,128)(2,1)} %pack.1), calls=%async_computation.2 | async-start | bytes 6291456 | tf_op jit(solution)/shard_map/all_to_all | solution.py:30
  235.3 1.0 copy-start.15
  241.3 1.1 copy-start.14
  242.4 8.5 %collective-permute-start.7 = (bf16[4,72,512]{2,1,0:T(8,128)(2,1)S(1)}, bf16[4,72,512]{2,1,0:T(8,128)(2,1)S(1)}, u32[]{:S(2)}, u32[]{:S(2)}) collective-permute-start(bf16[4,72,512]{2,1,0:T(8,128)(2,1)S(1)} %fusion), channel_id=1, source_target_pairs={{0,1},{1,0},{2,3},{3,2},{4,5},{5,4},{6,7},{7,6},{8,9},{9,8},{10,11... | collective-permute-start | bytes 884744 | tf_op jit(solution)/shard_map/ppermute | solution.py:26
  242.9 5.9 %collective-permute-start.4 = (bf16[32,1024]{1,0:T(8,128)(2,1)S(1)}, bf16[32,1024]{1,0:T(8,128)(2,1)S(1)}, u32[]{:S(2)}, u32[]{:S(2)}) collective-permute-start(bf16[32,1024]{1,0:T(8,128)(2,1)S(1)} %get-tuple-element.184), channel_id=1, source_target_pairs={{0,32},{32,64},{64,96},{96,0},{1,33},{33,65},{65,97},{97,1},{2,34}... | collective-permute-start | bytes 196616 | tf_op jit(solution)/shard_map/ppermute | solution.py:44
  243.0 7.4 %collective-permute-start.5 = (bf16[32,1024]{1,0:T(8,128)(2,1)S(1)}, bf16[32,1024]{1,0:T(8,128)(2,1)S(1)}, u32[]{:S(2)}, u32[]{:S(2)}) collective-permute-start(bf16[32,1024]{1,0:T(8,128)(2,1)S(1)} %get-tuple-element.183), channel_id=1, source_target_pairs={{0,64},{32,96},{64,0},{96,32},{1,65},{33,97},{65,1},{97,33},{2,66}... | collective-permute-start | bytes 196616 | tf_op jit(solution)/shard_map/ppermute | solution.py:44
  246.5 4.3 %collective-permute-start.6 = (bf16[32,1024]{1,0:T(8,128)(2,1)S(1)}, bf16[32,1024]{1,0:T(8,128)(2,1)S(1)}, u32[]{:S(2)}, u32[]{:S(2)}) collective-permute-start(bf16[32,1024]{1,0:T(8,128)(2,1)S(1)} %get-tuple-element.182), channel_id=1, source_target_pairs={{0,96},{32,0},{64,32},{96,64},{1,97},{33,1},{65,33},{97,65},{2,98}... | collective-permute-start | bytes 196616 | tf_op jit(solution)/shard_map/ppermute | solution.py:44
  252.0 0.9 copy-start.20
  252.9 31.7 %copy-start.5 = (bf16[1024,1024]{1,0:T(8,128)(2,1)S(1)}, bf16[1024,1024]{1,0:T(8,128)(2,1)}, u32[]{:S(2)}) copy-start(bf16[1024,1024]{1,0:T(8,128)(2,1)} %all-gather.3.cloned.1.call-done.band_ref) | copy-start | bytes 6291460
  253.0 7.8 %collective-permute-start.15 = (bf16[72,512]{1,0:T(8,128)(2,1)S(1)}, bf16[72,512]{1,0:T(8,128)(2,1)S(1)}, u32[]{:S(2)}, u32[]{:S(2)}) collective-permute-start(bf16[72,512]{1,0:T(8,128)(2,1)S(1)} %get-tuple-element.178), channel_id=1, source_target_pairs={{0,2},{2,4},{4,6},{6,0},{1,3},{3,5},{5,7},{7,1},{8,10},{10,12},{12... | collective-permute-start | bytes 221192 | tf_op jit(solution)/shard_map/ppermute | solution.py:44
  254.0 7.2 %collective-permute-start.16 = (bf16[72,512]{1,0:T(8,128)(2,1)S(1)}, bf16[72,512]{1,0:T(8,128)(2,1)S(1)}, u32[]{:S(2)}, u32[]{:S(2)}) collective-permute-start(bf16[72,512]{1,0:T(8,128)(2,1)S(1)} %get-tuple-element.180), channel_id=1, source_target_pairs={{0,4},{2,6},{4,0},{6,2},{1,5},{3,7},{5,1},{7,3},{8,12},{10,14},{12... | collective-permute-start | bytes 221192 | tf_op jit(solution)/shard_map/ppermute | solution.py:44
  255.2 6.8 %collective-permute-start.17 = (bf16[72,512]{1,0:T(8,128)(2,1)S(1)}, bf16[72,512]{1,0:T(8,128)(2,1)}, u32[]{:S(2)}, u32[]{:S(2)}) collective-permute-start(bf16[72,512]{1,0:T(8,128)(2,1)S(1)} %get-tuple-element.179), channel_id=1, source_target_pairs={{0,6},{2,0},{4,2},{6,4},{1,7},{3,1},{5,3},{7,5},{8,14},{10,8},{12,... | collective-permute-start | bytes 221192 | tf_op jit(solution)/shard_map/ppermute | solution.py:44
  257.5 14.1 %collective-permute-start.8 = (bf16[4,32,1024]{2,1,0:T(8,128)(2,1)S(1)}, bf16[4,32,1024]{2,1,0:T(8,128)(2,1)S(1)}, u32[]{:S(2)}, u32[]{:S(2)}) collective-permute-start(bf16[4,32,1024]{2,1,0:T(8,128)(2,1)S(1)} %pad_maximum_fusion.refs_0_), channel_id=1, source_target_pairs={{0,2},{2,4},{4,6},{6,0},{1,3},{3,5},{5,7},{7,1},{8,10},{10,12},{12... | collective-permute-start | bytes 786440 | tf_op jit(solution)/shard_map/ppermute | solution.py:44
  257.5 14.1 %collective-permute-start.9 = (bf16[4,32,1024]{2,1,0:T(8,128)(2,1)S(1)}, bf16[4,32,1024]{2,1,0:T(8,128)(2,1)S(1)}, u32[]{:S(2)}, u32[]{:S(2)}) collective-permute-start(bf16[4,32,1024]{2,1,0:T(8,128)(2,1)S(1)} %pad_maximum_fusion.refs_0_), channel_id=1, source_target_pairs={{0,6},{2,0},{4,2},{6,4},{1,7},{3,1},{5,3},{7,5},{8,14},{10,8},{12,... | collective-permute-start | bytes 786440 | tf_op jit(solution)/shard_map/ppermute | solution.py:44
  260.8 11.3 %collective-permute-start.10 = (bf16[4,32,1024]{2,1,0:T(8,128)(2,1)S(1)}, bf16[4,32,1024]{2,1,0:T(8,128)(2,1)S(1)}, u32[]{:S(2)}, u32[]{:S(2)}) collective-permute-start(bf16[4,32,1024]{2,1,0:T(8,128)(2,1)S(1)} %pad_maximum_fusion.refs_0_), channel_id=1, source_target_pairs={{0,4},{2,6},{4,0},{6,2},{1,5},{3,7},{5,1},{7,3},{8,12},{10,14},{12... | collective-permute-start | bytes 786440 | tf_op jit(solution)/shard_map/ppermute | solution.py:44
  262.9 6.0 %collective-permute-start.18 = (bf16[72,512]{1,0:T(8,128)(2,1)S(1)}, bf16[72,512]{1,0:T(8,128)(2,1)}, u32[]{:S(2)}, u32[]{:S(2)}) collective-permute-start(bf16[72,512]{1,0:T(8,128)(2,1)S(1)} %fusion.1), channel_id=1, source_target_pairs={{0,16},{8,24},{16,0},{24,8},{1,17},{9,25},{17,1},{25,9},{2,18},{10... | collective-permute-start | bytes 221192 | tf_op jit(solution)/shard_map/ppermute | solution.py:37
  265.4 4.4 %collective-permute-start.19 = (bf16[72,512]{1,0:T(8,128)(2,1)S(1)}, bf16[72,512]{1,0:T(8,128)(2,1)S(1)}, u32[]{:S(2)}, u32[]{:S(2)}) collective-permute-start(bf16[72,512]{1,0:T(8,128)(2,1)S(1)} %fusion.1), channel_id=1, source_target_pairs={{0,8},{8,0},{16,24},{24,16},{1,9},{9,1},{17,25},{25,17},{2,10},{10... | collective-permute-start | bytes 221192 | tf_op jit(solution)/shard_map/ppermute | solution.py:37
  269.0 7.5 %collective-permute-start.11 = (bf16[4,32,1024]{2,1,0:T(8,128)(2,1)S(1)}, bf16[4,32,1024]{2,1,0:T(8,128)(2,1)S(1)}, u32[]{:S(2)}, u32[]{:S(2)}) collective-permute-start(bf16[4,32,1024]{2,1,0:T(8,128)(2,1)S(1)} %pad_maximum_fusion.refs_0_), channel_id=1, source_target_pairs={{0,1},{1,0},{2,3},{3,2},{4,5},{5,4},{6,7},{7,6},{8,9},{9,8},{10,11... | collective-permute-start | bytes 786440 | tf_op jit(solution)/shard_map/ppermute | solution.py:26
  269.8 2.4 copy-start.29
  269.8 5.7 %collective-permute-start.20 = (bf16[72,512]{1,0:T(8,128)(2,1)S(1)}, bf16[72,512]{1,0:T(8,128)(2,1)}, u32[]{:S(2)}, u32[]{:S(2)}) collective-permute-start(bf16[72,512]{1,0:T(8,128)(2,1)S(1)} %fusion.1), channel_id=1, source_target_pairs={{0,24},{8,16},{16,8},{24,0},{1,25},{9,17},{17,9},{25,1},{2,26},{10... | collective-permute-start | bytes 221192 | tf_op jit(solution)/shard_map/ppermute | solution.py:37
  271.6 4.9 %collective-permute-start.12 = (bf16[4,32,1024]{2,1,0:T(8,128)(2,1)S(1)}, bf16[4,32,1024]{2,1,0:T(8,128)(2,1)}, u32[]{:S(2)}, u32[]{:S(2)}) collective-permute-start(bf16[4,32,1024]{2,1,0:T(8,128)(2,1)S(1)} %collective-permute-done.8.refs_1_), channel_id=1, source_target_pairs={{0,1},{1,0},{2,3},{3,2},{4,5},{5,4},{6,7},{7,6},{8,9},{9,8},{10,11... | collective-permute-start | bytes 786440 | tf_op jit(solution)/shard_map/ppermute | solution.py:26
  271.6 4.9 %collective-permute-start.13 = (bf16[4,32,1024]{2,1,0:T(8,128)(2,1)S(1)}, bf16[4,32,1024]{2,1,0:T(8,128)(2,1)}, u32[]{:S(2)}, u32[]{:S(2)}) collective-permute-start(bf16[4,32,1024]{2,1,0:T(8,128)(2,1)S(1)} %collective-permute-done.9.refs_3_), channel_id=1, source_target_pairs={{0,1},{1,0},{2,3},{3,2},{4,5},{5,4},{6,7},{7,6},{8,9},{9,8},{10,11... | collective-permute-start | bytes 786440 | tf_op jit(solution)/shard_map/ppermute | solution.py:26
  272.1 4.4 %collective-permute-start.14 = (bf16[4,32,1024]{2,1,0:T(8,128)(2,1)S(1)}, bf16[4,32,1024]{2,1,0:T(8,128)(2,1)}, u32[]{:S(2)}, u32[]{:S(2)}) collective-permute-start(bf16[4,32,1024]{2,1,0:T(8,128)(2,1)S(1)} %collective-permute-done.10.refs_2_), channel_id=1, source_target_pairs={{0,1},{1,0},{2,3},{3,2},{4,5},{5,4},{6,7},{7,6},{8,9},{9,8},{10,11... | collective-permute-start | bytes 786440 | tf_op jit(solution)/shard_map/ppermute | solution.py:26
  276.5 11.0 %collective-permute-start.21 = (bf16[72,512]{1,0:T(8,128)(2,1)S(1)}, bf16[72,512]{1,0:T(8,128)(2,1)S(1)}, u32[]{:S(2)}, u32[]{:S(2)}) collective-permute-start(bf16[72,512]{1,0:T(8,128)(2,1)S(1)} %add_add_fusion.1), channel_id=1, source_target_pairs={{0,64},{32,96},{64,0},{96,32},{1,65},{33,97},{65,1},{97,33},{2,66}... | collective-permute-start | bytes 221192 | tf_op jit(solution)/shard_map/ppermute | solution.py:37
  278.0 9.5 %collective-permute-start.22 = (bf16[72,512]{1,0:T(8,128)(2,1)S(1)}, bf16[72,512]{1,0:T(8,128)(2,1)S(1)}, u32[]{:S(2)}, u32[]{:S(2)}) collective-permute-start(bf16[72,512]{1,0:T(8,128)(2,1)S(1)} %add_add_fusion.1), channel_id=1, source_target_pairs={{0,32},{32,0},{64,96},{96,64},{1,33},{33,1},{65,97},{97,65},{2,34}... | collective-permute-start | bytes 221192 | tf_op jit(solution)/shard_map/ppermute | solution.py:37
  279.9 7.7 %collective-permute-start.23 = (bf16[72,512]{1,0:T(8,128)(2,1)S(1)}, bf16[72,512]{1,0:T(8,128)(2,1)S(1)}, u32[]{:S(2)}, u32[]{:S(2)}) collective-permute-start(bf16[72,512]{1,0:T(8,128)(2,1)S(1)} %add_add_fusion.1), channel_id=1, source_target_pairs={{0,96},{32,64},{64,32},{96,0},{1,97},{33,65},{65,33},{97,1},{2,98}... | collective-permute-start | bytes 221192 | tf_op jit(solution)/shard_map/ppermute | solution.py:37
  284.6 1.6 copy-start.6
  287.6 12.8 %collective-permute-start.24 = (bf16[256,1024]{1,0:T(8,128)(2,1)S(1)}, bf16[256,1024]{1,0:T(8,128)(2,1)S(1)}, u32[]{:S(2)}, u32[]{:S(2)}) collective-permute-start(bf16[256,1024]{1,0:T(8,128)(2,1)S(1)} %get-tuple-element.140), channel_id=1, source_target_pairs={{0,32},{32,64},{64,96},{96,0},{1,33},{33,65},{65,97},{97,1},{2,34}... | collective-permute-start | bytes 1572872 | tf_op jit(solution)/shard_map/ppermute | solution.py:44
  288.3 12.1 %collective-permute-start.25 = (bf16[256,1024]{1,0:T(8,128)(2,1)S(1)}, bf16[256,1024]{1,0:T(8,128)(2,1)S(1)}, u32[]{:S(2)}, u32[]{:S(2)}) collective-permute-start(bf16[256,1024]{1,0:T(8,128)(2,1)S(1)} %get-tuple-element.141), channel_id=1, source_target_pairs={{0,96},{32,0},{64,32},{96,64},{1,97},{33,1},{65,33},{97,65},{2,98}... | collective-permute-start | bytes 1572872 | tf_op jit(solution)/shard_map/ppermute | solution.py:44
  290.9 12.2 %collective-permute-start.26 = (bf16[256,1024]{1,0:T(8,128)(2,1)S(1)}, bf16[256,1024]{1,0:T(8,128)(2,1)S(1)}, u32[]{:S(2)}, u32[]{:S(2)}) collective-permute-start(bf16[256,1024]{1,0:T(8,128)(2,1)S(1)} %get-tuple-element.142), channel_id=1, source_target_pairs={{0,8},{8,16},{16,24},{24,0},{1,9},{9,17},{17,25},{25,1},{2,10},{10... | collective-permute-start | bytes 1572872 | tf_op jit(solution)/shard_map/ppermute | solution.py:44
  290.9 12.2 %collective-permute-start.27 = (bf16[256,1024]{1,0:T(8,128)(2,1)S(1)}, bf16[256,1024]{1,0:T(8,128)(2,1)S(1)}, u32[]{:S(2)}, u32[]{:S(2)}) collective-permute-start(bf16[256,1024]{1,0:T(8,128)(2,1)S(1)} %get-tuple-element.143), channel_id=1, source_target_pairs={{0,24},{8,0},{16,8},{24,16},{1,25},{9,1},{17,9},{25,17},{2,26},{10... | collective-permute-start | bytes 1572872 | tf_op jit(solution)/shard_map/ppermute | solution.py:44
  295.6 16.7 %copy-start.30 = (f32[32,8]{1,0:T(8,128)S(1)}, f32[32,8]{1,0:T(8,128)}, u32[]{:S(2)}) copy-start(f32[32,8]{1,0:T(8,128)} %get-tuple-element.176) | copy-start | bytes 3076
  300.4 2.7 copy-start.21
  300.4 2.7 copy-start.22
  303.1 1.0 copy-start.24
  305.8 8.5 %collective-permute-start.28 = (bf16[128,1024]{1,0:T(8,128)(2,1)S(1)}, bf16[128,1024]{1,0:T(8,128)(2,1)S(1)}, u32[]{:S(2)}, u32[]{:S(2)}) collective-permute-start(bf16[128,1024]{1,0:T(8,128)(2,1)S(1)} %get-tuple-element.162), channel_id=1, source_target_pairs={{0,32},{32,64},{64,96},{96,0},{1,33},{33,65},{65,97},{97,1},{2,34}... | collective-permute-start | bytes 786440 | tf_op jit(solution)/shard_map/ppermute | solution.py:44
  305.9 8.4 %collective-permute-start.29 = (bf16[128,1024]{1,0:T(8,128)(2,1)S(1)}, bf16[128,1024]{1,0:T(8,128)(2,1)S(1)}, u32[]{:S(2)}, u32[]{:S(2)}) collective-permute-start(bf16[128,1024]{1,0:T(8,128)(2,1)S(1)} %get-tuple-element.163), channel_id=1, source_target_pairs={{0,96},{32,0},{64,32},{96,64},{1,97},{33,1},{65,33},{97,65},{2,98}... | collective-permute-start | bytes 786440 | tf_op jit(solution)/shard_map/ppermute | solution.py:44
  309.1 7.6 %collective-permute-start.30 = (bf16[128,1024]{1,0:T(8,128)(2,1)S(1)}, bf16[128,1024]{1,0:T(8,128)(2,1)S(1)}, u32[]{:S(2)}, u32[]{:S(2)}) collective-permute-start(bf16[128,1024]{1,0:T(8,128)(2,1)S(1)} %get-tuple-element.166), channel_id=1, source_target_pairs={{0,8},{8,16},{16,24},{24,0},{1,9},{9,17},{17,25},{25,1},{2,10},{10... | collective-permute-start | bytes 786440 | tf_op jit(solution)/shard_map/ppermute | solution.py:44
  309.1 7.6 %collective-permute-start.31 = (bf16[128,1024]{1,0:T(8,128)(2,1)S(1)}, bf16[128,1024]{1,0:T(8,128)(2,1)S(1)}, u32[]{:S(2)}, u32[]{:S(2)}) collective-permute-start(bf16[128,1024]{1,0:T(8,128)(2,1)S(1)} %get-tuple-element.167), channel_id=1, source_target_pairs={{0,24},{8,0},{16,8},{24,16},{1,25},{9,1},{17,9},{25,17},{2,26},{10... | collective-permute-start | bytes 786440 | tf_op jit(solution)/shard_map/ppermute | solution.py:44
  314.3 2.4 copy-start.25
  314.3 2.4 copy-start.26
  (4 other events, 2.9 us)
Sparse Core Ops, SparseCore 0:
  101.3 27.3 all-gather.2
  130.4 30.8 all-gather.4

commit v3 on v2

--- a/solution.py
+++ b/solution.py
@@ -460,47 +460,50 @@
             flops=4 * count * features * units, bytes_accessed=24_000_000, transcendentals=0
         ),
         name="hidden_grads",
-    )(own, other, *kept(w_down), gate_pre, up_pre)
-
-
-def term_kernel(half, gg_ref, gu_ref, gate_ref, up_ref, term_ref):
-    count = term_ref.shape[0]
-    here = slice(half * count, (half + 1) * count)
-    features = gate_ref.shape[1]
+    )(*outside(own, other), *kept(w_down), gate_pre, up_pre)
+
+
+def term_kernel(gg_ref, gu_ref, gate_ref, up_ref, own_ref, other_ref):
+    count, features = own_ref.shape
     tile = 512
     for n in range(features // tile):
         at = slice(n * tile, (n + 1) * tile)
         term = lax.dot_general(
-            gg_ref[here, :], gate_ref[0, at, :], OVER_LAST, preferred_element_type=f32
+            gg_ref[...], gate_ref[0, at, :], OVER_LAST, preferred_element_type=f32
         )
         term = term + lax.dot_general(
-            gu_ref[here, :], up_ref[0, at, :], OVER_LAST, preferred_element_type=f32
-        )
-        term_ref[:, at] = term.astype(bf16)
-
-
-def terms(grad_gate, grad_up, w_gate, w_up, half):
+            gu_ref[...], up_ref[0, at, :], OVER_LAST, preferred_element_type=f32
+        )
+        term = term.astype(bf16)
+        own_ref[:, at] = term[:count]
+        other_ref[:, at] = term[count:]
+
+
+def terms(grad_gate, grad_up, w_gate, w_up):
     count = grad_gate.shape[0] // 2
     units = grad_gate.shape[1]
     features = w_gate.shape[1]
     inside = pl.BlockSpec(memory_space=pltpu.VMEM)
     return pl.pallas_call(
-        functools.partial(term_kernel, half),
+        term_kernel,
         in_specs=[inside] * 4,
-        out_specs=inside,
-        out_shape=jax.ShapeDtypeStruct((count, features), bf16),
+        out_specs=(inside, inside),
+        out_shape=(jax.ShapeDtypeStruct((count, features), bf16),) * 2,
         compiler_params=params(0, 10),
         cost_estimate=pl.CostEstimate(
-            flops=4 * count * features * units, bytes_accessed=17_000_000, transcendentals=0
+            flops=8 * count * features * units, bytes_accessed=17_000_000, transcendentals=0
         ),
         name="terms",
     )(grad_gate, grad_up, *kept(w_gate, w_up))
 
 
-def pack_kernel(capacity, own_ref, other_ref, order_ref, send_ref, held):
+def pack_kernel(
+    capacity, own_ref, other_ref, order_ref, own_part_ref, other_part_ref, chip_ref, send_ref, held
+):
     rows, features = own_ref.shape
     pieces = features // WIDE
     span = SOME * capacity
+    block = pieces * capacity
     for group in range(rows // span):
         here = slice(group * span, (group + 1) * span)
         for piece in range(pieces):
@@ -511,16 +514,28 @@
         moved = lax.dot_general(
             order_ref[...], held[group], OVER_ROWS, preferred_element_type=f32
         )
-        send_ref[group * SOME : (group + 1) * SOME] = moved.astype(bf16).reshape(
-            SOME, -1, WIDE
-        )
-
-
-def pack(own, other, order, capacity):
+        send_ref[group * SOME : (group + 1) * SOME, :block, :] = moved.astype(bf16).reshape(
+            SOME, block, WIDE
+        )
+    part = own_part_ref[...] + other_part_ref[...]
+    high = part.astype(bf16).astype(f32)
+    lane = lax.broadcasted_iota(jnp.int32, part.shape, 1)
+    half = part.shape[1] // 2
+    part = jnp.where(lane < half, high, part - high)
+    part = jnp.where(lane % half == chip_ref[0], part, 0.0)
+    part = part.reshape(send_ref.shape[0], 8, part.shape[1])
+    part = jnp.concatenate(
+        [part, jnp.zeros((*part.shape[:2], WIDE - part.shape[2]), f32)], axis=2
+    )
+    send_ref[:, block:, :] = part.astype(bf16)
+
+
+def pack(own, other, order, capacity, own_part, other_part):
     count, features = own.shape
     block = features // WIDE * capacity
     groups = 2
     span = groups * SOME * capacity
+    chip = lax.axis_index(CHIP).astype(jnp.int32).reshape(1)
     return pl.pallas_call(
         functools.partial(pack_kernel, capacity),
         grid=(count // span,),
@@ -528,13 +543,16 @@
             pl.BlockSpec((span, features), lambda i: (i, 0)),
             pl.BlockSpec((span, features), lambda i: (i, 0)),
             pl.BlockSpec(order.shape, lambda i: (0, 0)),
+            pl.BlockSpec((groups * SOME * 8, 128), lambda i: (i, 0)),
+            pl.BlockSpec((groups * SOME * 8, 128), lambda i: (i, 0)),
+            pl.BlockSpec(memory_space=pltpu.SMEM),
         ],
-        out_specs=pl.BlockSpec((groups * SOME, block, WIDE), lambda i: (i, 0, 0)),
-        out_shape=pltpu.HBM((count // capacity, block, WIDE), bf16),
+        out_specs=pl.BlockSpec((groups * SOME, block + 8, WIDE), lambda i: (i, 0, 0)),
+        out_shape=pltpu.HBM((count // capacity, block + 8, WIDE), bf16),
         scratch_shapes=[pltpu.VMEM((groups, SOME * block, WIDE), bf16)],
         compiler_params=params(1),
         name="pack",
-    )(own, other, order)
+    )(own, other, order, own_part, other_part, chip)
 
 
 def mix_kernel(capacity, code_ref, gate_ref, mix_ref):
@@ -568,20 +586,43 @@
 
 
 def finish_kernel(
-    mix_ref, back_ref, pre_ref, grad_ref, gain_ref, logit_ref, router_ref, normed_ref,
-    residual_ref, bands_ref, small_ref,
+    mix_ref, back_ref, pre_ref, grad_ref, gain_ref, router_ref, normed_ref,
+    code_ref, gate_ref, routes_ref,
+    residual_ref, bands_ref, small_ref, gate_grad_ref,
 ):
     tok_rows, features = pre_ref.shape
     columns = mix_ref.shape[0] // 2
     pieces = features // WIDE
-    both = jnp.dot(mix_ref[...], back_ref[...], preferred_element_type=f32)
+    experts, rows, _ = back_ref.shape
+    block = rows - 8
+    both = jnp.dot(
+        mix_ref[...],
+        back_ref[:, :block, :].reshape(experts * block, WIDE),
+        preferred_element_type=f32,
+    )
+    slot = lax.broadcasted_iota(jnp.int32, (experts, 8, tok_rows), 1).astype(f32)
+    hit = jnp.where(code_ref[:, :tok_rows][:, None, :] == slot, 1.0, 0.0)
+    part = back_ref[:, block:, :128].astype(f32).reshape(experts * 8, 128).astype(bf16)
+    part = lax.dot_general(
+        hit.reshape(experts * 8, tok_rows).astype(bf16), part, OVER_ROWS,
+        preferred_element_type=f32,
+    )
+    grad_of = part[:, :experts] + part[:, experts:]
+    expert = lax.broadcasted_iota(jnp.int32, (tok_rows, experts), 1)
+    for choice in range(routes_ref.shape[1]):
+        named = expert == routes_ref[:, choice : choice + 1]
+        gate_grad_ref[:, choice : choice + 1] = jnp.sum(
+            jnp.where(named, grad_of, 0.0), axis=-1, keepdims=True
+        )
+    gate_of = gate_ref[...]
+    weighted = jnp.sum(gate_of * grad_of, axis=-1, keepdims=True)
+    logit_full = (gate_of * (grad_of - weighted)).astype(bf16)
     expert_grad = both[:columns] + both[columns:]
     hidden = pre_ref[...].astype(f32)
     inverse = lax.rsqrt(jnp.mean(hidden * hidden, axis=-1, keepdims=True) + 1e-06)
-    router_term = jnp.dot(logit_ref[...], router_ref[...], preferred_element_type=f32)
-    experts = logit_ref.shape[1]
+    router_term = jnp.dot(logit_full, router_ref[...], preferred_element_type=f32)
     router_part = lax.dot_general(
-        logit_ref[...], normed_ref[...], OVER_ROWS, preferred_element_type=f32
+        logit_full, normed_ref[...], OVER_ROWS, preferred_element_type=f32
     )
     spare = small_ref.shape[1] - experts
     per_band = bands_ref.shape[2] // WIDE
@@ -613,24 +654,29 @@
         bands_ref[piece // per_band, :, inner : inner + WIDE] = residual
 
 
-def finish(mix, back, pre_norm, out_grad, norm_gain, logit_full, router_wide, normed, bands):
+def finish(
+    mix, back, pre_norm, out_grad, norm_gain, router_wide, normed, code, gate_of, routes, bands
+):
     tok_rows, features = pre_norm.shape
-    experts = logit_full.shape[1]
+    experts = gate_of.shape[1]
     return pl.pallas_call(
         finish_kernel,
         out_shape=(
             jax.ShapeDtypeStruct((tok_rows, features), bf16),
             jax.ShapeDtypeStruct((bands, tok_rows, features // bands), bf16),
             jax.ShapeDtypeStruct((features // WIDE, experts + 8, WIDE), f32),
+            jax.ShapeDtypeStruct(routes.shape, f32),
         ),
         compiler_params=params(0, 24),
         name="finish",
     )(
         mix,
         *outside(back, pre_norm, out_grad, norm_gain),
-        logit_full,
         router_wide,
         *outside(normed),
+        code,
+        gate_of,
+        routes,
     )
 
 
@@ -676,42 +722,29 @@
     grad_gate, grad_up, own_part, other_part = hidden_grads(
         own_grads, other_grads, w_down, gate_pre, up_pre, capacity
     )
-    grad_gate, weight_band = lax.optimization_barrier((grad_gate, weight_band))
     other_part = swap_cores(other_part)
-    other_term = terms(grad_gate, grad_up, w_gate, w_up, 1)
+    own_term, other_term = terms(grad_gate, grad_up, w_gate, w_up)
     other_term = swap_cores(other_term)
-    own_term = terms(grad_gate, grad_up, w_gate, w_up, 0)
-    own_term, context_band = lax.optimization_barrier((own_term, context_band))
-    send_back = pack(own_term, other_term, order, capacity)
-    send_back, own_part, other_part = lax.optimization_barrier(
-        (send_back, own_part, other_part)
-    )
-    part = (own_part + other_part).reshape(experts, 8, 128)
-    part = exchange(part, CHIP)[:, :capacity, 0]
-    send_back, part, code, routes, gate_probs, router_weight = lax.optimization_barrier(
-        (send_back, part, code, routes, gate_probs, router_weight)
-    )
-    got_back = exchange(send_back, CHIP).reshape(experts * block, WIDE)
+    other_term, weight_band, context_band = lax.optimization_barrier(
+        (other_term, weight_band, context_band)
+    )
+    send_back = pack(own_term, other_term, order, capacity, own_part, other_part)
+    send_back, code, routes, gate_probs, router_weight = lax.optimization_barrier(
+        (send_back, code, routes, gate_probs, router_weight)
+    )
+    got_back = exchange(send_back, CHIP)
 
     named = routes[:, :, None] == jnp.arange(experts, dtype=jnp.int32)[None, None, :]
     gate_of = jnp.sum(jnp.where(named, gate_probs[:, :, None], 0.0), axis=1)
     mix = mixings(code, jnp.tile(gate_of.T, (1, pieces)), capacity, block)
     router_wide = router_weight.T
 
-    slot = code[:, :tok_rows].T
-    at_slot = jnp.arange(capacity, dtype=jnp.int32).astype(f32)
-    grad_of = jnp.sum(
-        jnp.where(slot[:, :, None] == at_slot[None, None, :], part[None], 0.0), axis=2
-    )
-    gate_grad = jnp.sum(jnp.where(named, grad_of[:, None, :], 0.0), axis=2)
-    weighted = jnp.sum(gate_of * grad_of, axis=-1, keepdims=True)
-    logit_full = (gate_of * (grad_of - weighted)).astype(bf16)
-    got_back, logit_full, mix, router_wide = lax.optimization_barrier(
-        (got_back, logit_full, mix, router_wide)
-    )
-
-    residual_grad, bands, small = finish(
-        mix, got_back, pre_norm, out_grad, gain, logit_full, router_wide, normed, lax.axis_size("y")
+    got_back, mix, router_wide, gate_of = lax.optimization_barrier(
+        (got_back, mix, router_wide, gate_of)
+    )
+    residual_grad, bands, small, gate_grad = finish(
+        mix, got_back, pre_norm, out_grad, gain, router_wide, normed, code, gate_of, routes,
+        lax.axis_size("y"),
     )
 
     square, small = gather_square(bands, small)

time: 332 us -> 321 us (0.967)
  blocking collectives: 102 us -> 86.3 us
  waiting for transfers between devices: 60 us -> 72.9 us
  local copies, waits for them, and re-layouts: 29.1 us -> 20.5 us
  other arithmetic: 5.39 us -> 1.57 us
    all_to_all x2 -> x1, blocking collectives: 102 us -> 86.3 us  [exchange(): return lax.all_to_all(value, axes, split_axis=0, concat_axis=0, tiled=True)]
    unnamed x68 -> x51, local copies, waits for them, and re-layouts: 26.6 us -> 18.2 us
    all_to_all x1, waiting for transfers between devices: 36.4 us -> 43.5 us  [exchange(): return lax.all_to_all(value, axes, split_axis=0, concat_axis=0, tiled=True)]
    ppermute x9, waiting for transfers between devices: 2.68 us -> 6.85 us  [swap_cores(): return lax.ppermute(value, 'core', SWAP)]
    pallas_call x2 -> x1, Pallas kernels: 11.8 us -> 11.6 us  [terms(): pl.pallas_call(term_kernel, in_specs=[inside] * 4, out_specs=(inside, ins...]
  transfers between devices with their start and end apart: 35 -> 35, of which waited for: 12 -> 14; matrix products, arithmetic and copies ran while one was open for 2% -> 1% of each run, Pallas kernels for 18% -> 17%
where the time goes in v3:
time: 321 us; the launch traced here: 317 us
  blocking collectives  86.3 us (27%)
  Pallas kernels  76.6 us (24%)
  waiting for transfers between devices  72.9 us (23%)
  starting transfers between devices  44.3 us (14%)
  local copies, waits for them, and re-layouts  20.5 us (6%)
  between operations  14.6 us (5%)
    all_to_all x1, blocking collectives, exchange(): return lax.all_to_all(value, axes, split_axis=0, concat_axis=0, tiled=True)  86.3 us
    all_to_all x1, waiting for transfers between devices, exchange(): return lax.all_to_all(value, axes, split_axis=0, concat_axis=0, tiled=True)  43.5 us
    ppermute x17, starting transfers between devices, shift(): lax.ppermute(value, axis, [(i, (i + step) % size) for i in range(size)])  25.5 us
    unnamed x51, local copies, waits for them, and re-layouts  18.2 us
    ppermute x17, waiting for transfers between devices, shift(): lax.ppermute(value, axis, [(i, (i + step) % size) for i in range(size)])  13.2 us
    pallas_call x1, Pallas kernels, forward(): pl.pallas_call(forward_kernel, in_specs=[inside] * 4, out_specs=(inside,...  12.8 us
    pallas_call x1, Pallas kernels, hidden_grads(): pl.pallas_call(functools.partial(hidden_kernel, capacity), in_specs=[insi...  11.8 us
    pallas_call x1, Pallas kernels, terms(): pl.pallas_call(term_kernel, in_specs=[inside] * 4, out_specs=(inside, ins...  11.6 us
  transfers between devices with their start and end apart: 35, of which 14 were waited for; matrix products, arithmetic and copies ran while one was open for 1% of the time, Pallas kernels for 17%

profile of v3, /device:TPU:0, one launch (start us, length us, event | category | flops | bytes accessed | tf_op | source)
XLA Modules:
  0.0 316.8 jit_solution(12979022190062046923)
XLA Ops:
  7.2 0.7 tile.8
  8.0 6.9 %place.1 = (bf16[64,96,512]{2,1,0:T(8,128)(2,1)}, f32[64,256]{1,0:T(8,128)S(1)}, bf16[32,4096]{1,0:T(8,128)(2,1)S(1)}) custom-call(bf16[32,4096]{1,0:T(8,128)(2,1)} %pre_ref.3, bf16[32,4096]{1,0:T(8,128)(2,1)} %grad_ref.3, f32[1,4096]{1,0:T(1,128)} %bitcast.42, s32[8,256]{1,0:T(8,128)S(1)} %tile.9.routes_ref), custom_call_target="tpu_custom_call" | custom-call | tf_op jit(solution)/shard_map/place/pallas_call | solution.py:319
  14.9 86.3 %all_to_all.10.got_ref = bf16[64,96,512]{2,1,0:T(8,128)(2,1)} all-to-all(bf16[64,96,512]{2,1,0:T(8,128)(2,1)} %get-tuple-element.86), channel_id=1, replica_groups=mesh['y'=4,'x'=4,'z'=4,'core'=2] {'y','x','z'}, dimensions={0} | all-to-all | bytes 12582912 | tf_op jit(solution)/shard_map/all_to_all | solution.py:30
  101.3 2.8 copy-done
  104.0 3.7 %spread.3.own_ref = bf16[384,4096]{1,0:T(8,128)(2,1)} custom-call(bf16[64,96,512]{2,1,0:T(8,128)(2,1)S(1)} %copy-done, bf16[384,384]{1,0:T(8,128)(2,1)S(1)} %copy-done.4), custom_call_target="tpu_custom_call" | custom-call | tf_op jit(solution)/shard_map/spread/pallas_call | solution.py:368
  107.8 2.6 spread.2.own_ref
  110.3 0.8 collective-permute-start
  111.1 2.7 collective-permute-done.1.other_ref
  113.8 2.9 copy-done.11
  116.6 2.9 copy-done.13
  119.5 12.8 %forward.1 = (f32[768,768]{1,0:T(8,128)S(1)}, f32[768,768]{1,0:T(8,128)S(1)}) custom-call(bf16[384,4096]{1,0:T(8,128)(2,1)} %spread.3.own_ref, bf16[384,4096]{1,0:T(8,128)(2,1)} %collective-permute-done.1.other_ref, bf16[1,4096,768]{2,1,0:T(8,128)(2,1)S(1)} %copy-done.11, bf16[1,4096,768]{2,1,0:T(8,128)(2,1)S(1)} %copy-done.13), custom_call_target="tpu_custom_call" | custom-call | flops 9663676416 | bytes 24000000 | tf_op jit(solution)/shard_map/forward/pallas_call | solution.py:397
  132.3 2.8 copy-done.10
  135.1 11.8 %hidden_grads.1 = (bf16[768,768]{1,0:T(8,128)(2,1)S(1)}, bf16[768,768]{1,0:T(8,128)(2,1)S(1)}, f32[512,128]{1,0:T(8,128)S(1)}, f32[512,128]{1,0:T(8,128)}) custom-call(bf16[384,4096]{1,0:T(8,128)(2,1)} %copy-done.3, bf16[384,4096]{1,0:T(8,128)(2,1)} %collective-permute-done.other_ref, bf16[1,768,4096]{2,1,0:T(8,128)(2,1)S(1)} %copy-done.10, ...), custom_call_target="tpu_custom_call" | custom-call | flops 4831838208 | bytes 24000000 | tf_op jit(solution)/shard_map/hidden_grads/pallas_call | solution.py:448
  146.8 0.7 copy-done.8
  147.6 11.6 %terms.1 = (bf16[384,4096]{1,0:T(8,128)(2,1)S(1)}, bf16[384,4096]{1,0:T(8,128)(2,1)}) custom-call(bf16[768,768]{1,0:T(8,128)(2,1)S(1)} %get-tuple-element.92.gg_ref, bf16[768,768]{1,0:T(8,128)(2,1)S(1)} %get-tuple-element.93.gu_ref, bf16[1,4096,768]{2,1,0:T(8,128)(2,1)S(1)} %copy-done.12, bf16[1,4096,768]{2,1,0:T(8,128)(2,1)S(1)} %copy-done.14), custom_call_target="tpu_custom_call" | custom-call | flops 9663676416 | bytes 17000000 | tf_op jit(solution)/shard_map/terms/pallas_call | solution.py:487
  159.6 1.7 all-gather.5.cloned.1.call-done.band_ref
  161.3 3.8 %collective-permute-done.2.other_ref = bf16[384,4096]{1,0:T(8,128)(2,1)} collective-permute-done((bf16[384,4096]{1,0:T(8,128)(2,1)}, bf16[384,4096]{1,0:T(8,128)(2,1)}, u32[]{:S(2)}, u32[]{:S(2)}) %collective-permute-start.2) | collective-permute-done | bytes 3145760 | tf_op jit(solution)/shard_map/ppermute | solution.py:26
  165.5 0.9 copy-done.9
  166.5 5.5 %pack.1 = bf16[64,56,512]{2,1,0:T(8,128)(2,1)} custom-call(bf16[384,4096]{1,0:T(8,128)(2,1)S(1)} %get-tuple-element.94.own_ref, bf16[384,4096]{1,0:T(8,128)(2,1)} %collective-permute-done.2.other_ref, bf16[384,384]{1,0:T(8,128)(2,1)S(1)} %copy-done.4, f32[512,128]{1,0:T(8,128)S(1)} %copy-done.9, f32[512,128]{1,0:T(8,128)} %collective-permute-done.3.other_part_ref, ...), custom_call_target="tpu_custom_call" | custom-call | tf_op jit(solution)/shard_map/pack/pallas_call | solution.py:539
  171.9 5.9 %all-to-all-start.1 = ((bf16[64,56,512]{2,1,0:T(8,128)(2,1)}), bf16[64,56,512]{2,1,0:T(8,128)(2,1)}, u32[]{:S(2)}, u32[]{:S(2)}) async-start(bf16[64,56,512]{2,1,0:T(8,128)(2,1)} %pack.1), calls=%async_computation.1 | async-start | bytes 7340032 | tf_op jit(solution)/shard_map/all_to_all | solution.py:30
  178.2 2.0 mixings.1.mix_ref
  180.3 43.5 %all-to-all-done.1.back_ref = bf16[64,56,512]{2,1,0:T(8,128)(2,1)} async-done(((bf16[64,56,512]{2,1,0:T(8,128)(2,1)}), bf16[64,56,512]{2,1,0:T(8,128)(2,1)}, u32[]{:S(2)}, u32[]{:S(2)}) %all-to-all-start.1) | async-done | bytes 3670048 | tf_op jit(solution)/shard_map/all_to_all | solution.py:30
  223.8 1.0 copy-done.6
  224.8 5.8 %finish.1 = (bf16[32,4096]{1,0:T(8,128)(2,1)}, bf16[4,32,1024]{2,1,0:T(8,128)(2,1)S(1)}, f32[8,72,512]{2,1,0:T(8,128)S(1)}, f32[32,8]{1,0:T(8,128)S(1)}) custom-call(bf16[512,3072]{1,0:T(8,128)(2,1)S(1)} %mixings.1.mix_ref, bf16[64,56,512]{2,1,0:T(8,128)(2,1)} %all-to-all-done.1.back_ref, bf16[32,4096]{1,0:T(8,128)(2,1)} %pre_ref.3, ...), custom_call_target="tpu_custom_call" | custom-call | tf_op jit(solution)/shard_map/finish/pallas_call | solution.py:662
  230.7 1.0 copy-done.5
  232.0 2.7 collective-permute-start.5
  234.6 1.0 collective-permute-start.6
  235.6 3.4 %collective-permute-done.4 = bf16[32,1024]{1,0:T(8,128)(2,1)S(1)} collective-permute-done((bf16[32,1024]{1,0:T(8,128)(2,1)S(1)}, bf16[32,1024]{1,0:T(8,128)(2,1)S(1)}, u32[]{:S(2)}, u32[]{:S(2)}) %collective-permute-start.4) | collective-permute-done | bytes 65568 | tf_op jit(solution)/shard_map/ppermute | solution.py:44
  239.7 1.2 bitcast_add_fusion
  240.9 1.6 collective-permute-start.15
  242.5 1.3 collective-permute-start.16
  243.8 2.5 collective-permute-start.17
  246.3 3.2 %collective-permute-start.9 = (bf16[4,32,1024]{2,1,0:T(8,128)(2,1)S(1)}, bf16[4,32,1024]{2,1,0:T(8,128)(2,1)S(1)}, u32[]{:S(2)}, u32[]{:S(2)}) collective-permute-start(bf16[4,32,1024]{2,1,0:T(8,128)(2,1)S(1)} %pad_maximum_fusion.refs_0_), channel_id=1, source_target_pairs={{0,6},{2,0},{4,2},{6,4},{1,7},{3,1},{5,3},{7,5},{8,14},{10,8},{12,... | collective-permute-start | bytes 786440 | tf_op jit(solution)/shard_map/ppermute | solution.py:44
  249.6 5.0 %collective-permute-start.18 = (bf16[72,512]{1,0:T(8,128)(2,1)S(1)}, bf16[72,512]{1,0:T(8,128)(2,1)S(1)}, u32[]{:S(2)}, u32[]{:S(2)}) collective-permute-start(bf16[72,512]{1,0:T(8,128)(2,1)S(1)} %fusion.1), channel_id=1, source_target_pairs={{0,16},{8,24},{16,0},{24,8},{1,17},{9,25},{17,1},{25,9},{2,18},{10... | collective-permute-start | bytes 221192 | tf_op jit(solution)/shard_map/ppermute | solution.py:37
  254.7 2.4 collective-permute-done.18
  257.1 1.9 collective-permute-done.19
  259.0 1.6 collective-permute-start.20
  261.3 3.3 %collective-permute-done.20 = bf16[72,512]{1,0:T(8,128)(2,1)S(1)} collective-permute-done((bf16[72,512]{1,0:T(8,128)(2,1)S(1)}, bf16[72,512]{1,0:T(8,128)(2,1)S(1)}, u32[]{:S(2)}, u32[]{:S(2)}) %collective-permute-start.20) | collective-permute-done | bytes 73760 | tf_op jit(solution)/shard_map/ppermute | solution.py:37
  264.7 2.2 collective-permute-start.21
  266.9 1.2 collective-permute-start.22
  268.0 1.0 collective-permute-start.23
  269.0 4.0 %gather_square.1.square_ref = bf16[4,256,1024]{2,1,0:T(8,128)(2,1)S(1)} custom-call(s32[3]{0:T(128)S(1)} %pad_add_fusion.place_ref, bf16[4,32,1024]{2,1,0:T(8,128)(2,1)S(1)} %pad_maximum_fusion.refs_0_, bf16[4,32,1024]{2,1,0:T(8,128)(2,1)S(1)} %collective-permute-done.8.refs_1_, bf16[4,32,1024]{2,1,0:T(8,128)(2,1)S(1)} %collective-permute-done.10.refs_2_, ...), custom_call_target="tpu_custom_call" | custom-call | tf_op jit(solution)/shard_map/gather_square/pallas_call | solution.py:178
  273.0 1.3 context_part.2
  274.6 1.4 weight_part.2
  276.1 1.5 collective-permute-start.24
  277.5 1.8 collective-permute-start.25
  279.6 3.0 collective-permute-start.27
  282.6 1.3 weight_part.3
  283.9 1.3 context_part.3
  285.2 3.2 %collective-permute-done.24.refs_1_.refs_2_ = bf16[256,1024]{1,0:T(8,128)(2,1)S(1)} collective-permute-done((bf16[256,1024]{1,0:T(8,128)(2,1)S(1)}, bf16[256,1024]{1,0:T(8,128)(2,1)S(1)}, u32[]{:S(2)}, u32[]{:S(2)}) %collective-permute-start.24) | collective-permute-done | bytes 524320 | tf_op jit(solution)/shard_map/ppermute | solution.py:44
  288.4 2.7 collective-permute-done.26.refs_5_.refs_8_
  291.1 0.9 collective-permute-done.27.refs_7_.refs_9_
  292.0 0.8 copy-done.18
  292.8 1.8 pass_on.1
  294.6 3.2 %collective-permute-start.29 = (bf16[128,1024]{1,0:T(8,128)(2,1)S(1)}, bf16[128,1024]{1,0:T(8,128)(2,1)S(1)}, u32[]{:S(2)}, u32[]{:S(2)}) collective-permute-start(bf16[128,1024]{1,0:T(8,128)(2,1)S(1)} %get-tuple-element.159), channel_id=1, source_target_pairs={{0,96},{32,0},{64,32},{96,64},{1,97},{33,1},{65,33},{97,65},{2,98}... | collective-permute-start | bytes 786440 | tf_op jit(solution)/shard_map/ppermute | solution.py:44
  297.8 0.9 collective-permute-start.30
  298.8 2.3 collective-permute-start.31
  301.1 0.7 copy.32
  301.7 0.6 slice.7
  302.3 0.7 slice_bitcast_fusion
  303.0 2.4 collective-permute-done.30.refs_10_
  305.4 0.7 copy-done.21
  306.1 0.7 copy-done.22
  306.8 3.0 close.1
  (95 shorter events, 3.9 us)
Async XLA Ops:
  7.2 152.5 %all-gather.3.cloned.1.call-start = ((), (), s32[]{:S(2)}) async-start(), calls=%async_computation.2 | async-start | bytes 2621440 | tf_op jit(solution)/shard_map/all_gather | solution.py:714
  14.9 86.3 %copy-start.7 = (bf16[32,4096]{1,0:T(8,128)(2,1)}, bf16[32,4096]{1,0:T(8,128)(2,1)S(1)}, u32[]{:S(2)}) copy-start(bf16[32,4096]{1,0:T(8,128)(2,1)S(1)} %get-tuple-element.112.normed_ref) | copy-start | bytes 786436
  14.9 86.4 %copy-start.4 = (bf16[384,384]{1,0:T(8,128)(2,1)S(1)}, bf16[384,384]{1,0:T(8,128)(2,1)}, u32[]{:S(2)}) copy-start(bf16[384,384]{1,0:T(8,128)(2,1)} %constant.71.clone.order_ref) | copy-start | bytes 884740
  101.2 60.1 %all-gather.5.cloned.1.call-start = ((), (), s32[]{:S(2)}) async-start(), calls=%async_computation.3 | async-start | bytes 2621440 | tf_op jit(solution)/shard_map/all_gather | solution.py:715
  101.3 2.8 copy-start
  107.7 6.0 %collective-permute-start.1 = (bf16[384,4096]{1,0:T(8,128)(2,1)}, bf16[384,4096]{1,0:T(8,128)(2,1)}, u32[]{:S(2)}, u32[]{:S(2)}) collective-permute-start(bf16[384,4096]{1,0:T(8,128)(2,1)} %spread.3.own_ref), channel_id=1, source_target_pairs={{0,1},{1,0},{2,3},{3,2},{4,5},{5,4},{6,7},{7,6},{8,9},{9,8},{10,11... | collective-permute-start | bytes 9437192 | tf_op jit(solution)/shard_map/ppermute | solution.py:26
  110.3 21.9 %copy-start.3 = (bf16[384,4096]{1,0:T(8,128)(2,1)}, bf16[384,4096]{1,0:T(8,128)(2,1)S(1)}, u32[]{:S(2)}) copy-start(bf16[384,4096]{1,0:T(8,128)(2,1)S(1)} %spread.2.own_ref) | copy-start | bytes 9437188
  110.3 21.9 %collective-permute-start = (bf16[384,4096]{1,0:T(8,128)(2,1)S(1)}, bf16[384,4096]{1,0:T(8,128)(2,1)}, u32[]{:S(2)}, u32[]{:S(2)}) collective-permute-start(bf16[384,4096]{1,0:T(8,128)(2,1)S(1)} %spread.2.own_ref), channel_id=1, source_target_pairs={{0,1},{1,0},{2,3},{3,2},{4,5},{5,4},{6,7},{7,6},{8,9},{9,8},{10,11... | collective-permute-start | bytes 9437192 | tf_op jit(solution)/shard_map/ppermute | solution.py:26
  113.8 2.9 copy-start.11
  116.6 2.9 copy-start.13
  132.3 2.8 copy-start.10
  135.1 12.5 %copy-start.12 = (bf16[1,4096,768]{2,1,0:T(8,128)(2,1)S(1)}, bf16[1,4096,768]{2,1,0:T(8,128)(2,1)}, u32[]{:S(2)}) copy-start(bf16[1,4096,768]{2,1,0:T(8,128)(2,1)} %gate_ref.3) | copy-start | bytes 18874372
  135.1 12.5 %copy-start.14 = (bf16[1,4096,768]{2,1,0:T(8,128)(2,1)S(1)}, bf16[1,4096,768]{2,1,0:T(8,128)(2,1)}, u32[]{:S(2)}) copy-start(bf16[1,4096,768]{2,1,0:T(8,128)(2,1)} %up_ref.3) | copy-start | bytes 18874372
  146.8 0.7 copy-start.8
  159.1 6.0 %collective-permute-start.2 = (bf16[384,4096]{1,0:T(8,128)(2,1)}, bf16[384,4096]{1,0:T(8,128)(2,1)}, u32[]{:S(2)}, u32[]{:S(2)}) collective-permute-start(bf16[384,4096]{1,0:T(8,128)(2,1)} %get-tuple-element.95), channel_id=1, source_target_pairs={{0,1},{1,0},{2,3},{3,2},{4,5},{5,4},{6,7},{7,6},{8,9},{9,8},{10,11... | collective-permute-start | bytes 9437192 | tf_op jit(solution)/shard_map/ppermute | solution.py:26
  159.2 6.3 %collective-permute-start.3 = (f32[512,128]{1,0:T(8,128)}, f32[512,128]{1,0:T(8,128)}, u32[]{:S(2)}, u32[]{:S(2)}) collective-permute-start(f32[512,128]{1,0:T(8,128)} %get-tuple-element.100), channel_id=1, source_target_pairs={{0,1},{1,0},{2,3},{3,2},{4,5},{5,4},{6,7},{7,6},{8,9},{9,8},{10,11... | collective-permute-start | bytes 786440 | tf_op jit(solution)/shard_map/ppermute | solution.py:26
  165.5 1.0 copy-start.9
  171.9 5.9 %copy-start.23 = (s32[32,8]{0,1:T(8,128)S(1)}, s32[32,8]{0,1:T(8,128)}, u32[]{:S(2)}) copy-start(s32[32,8]{0,1:T(8,128)} %param.14) | copy-start | bytes 3076
  171.9 6.0 %copy-start.24 = (f32[32,8]{0,1:T(8,128)S(1)}, f32[32,8]{0,1:T(8,128)}, u32[]{:S(2)}) copy-start(f32[32,8]{0,1:T(8,128)} %param.15) | copy-start | bytes 3076
  171.9 51.9 %all-to-all-start.1 = ((bf16[64,56,512]{2,1,0:T(8,128)(2,1)}), bf16[64,56,512]{2,1,0:T(8,128)(2,1)}, u32[]{:S(2)}, u32[]{:S(2)}) async-start(bf16[64,56,512]{2,1,0:T(8,128)(2,1)} %pack.1), calls=%async_computation.1 | async-start | bytes 7340032 | tf_op jit(solution)/shard_map/all_to_all | solution.py:30
  223.8 1.0 copy-start.6
  230.7 1.0 copy-start.5
  231.7 7.9 %collective-permute-start.7 = (bf16[4,72,512]{2,1,0:T(8,128)(2,1)S(1)}, bf16[4,72,512]{2,1,0:T(8,128)(2,1)S(1)}, u32[]{:S(2)}, u32[]{:S(2)}) collective-permute-start(bf16[4,72,512]{2,1,0:T(8,128)(2,1)S(1)} %fusion), channel_id=1, source_target_pairs={{0,1},{1,0},{2,3},{3,2},{4,5},{5,4},{6,7},{7,6},{8,9},{9,8},{10,11... | collective-permute-start | bytes 884744 | tf_op jit(solution)/shard_map/ppermute | solution.py:26
  231.9 7.2 %collective-permute-start.4 = (bf16[32,1024]{1,0:T(8,128)(2,1)S(1)}, bf16[32,1024]{1,0:T(8,128)(2,1)S(1)}, u32[]{:S(2)}, u32[]{:S(2)}) collective-permute-start(bf16[32,1024]{1,0:T(8,128)(2,1)S(1)} %get-tuple-element.190), channel_id=1, source_target_pairs={{0,32},{32,64},{64,96},{96,0},{1,33},{33,65},{65,97},{97,1},{2,34}... | collective-permute-start | bytes 196616 | tf_op jit(solution)/shard_map/ppermute | solution.py:44
  232.0 7.1 %collective-permute-start.5 = (bf16[32,1024]{1,0:T(8,128)(2,1)S(1)}, bf16[32,1024]{1,0:T(8,128)(2,1)S(1)}, u32[]{:S(2)}, u32[]{:S(2)}) collective-permute-start(bf16[32,1024]{1,0:T(8,128)(2,1)S(1)} %get-tuple-element.189), channel_id=1, source_target_pairs={{0,64},{32,96},{64,0},{96,32},{1,65},{33,97},{65,1},{97,33},{2,66}... | collective-permute-start | bytes 196616 | tf_op jit(solution)/shard_map/ppermute | solution.py:44
  234.6 5.0 %collective-permute-start.6 = (bf16[32,1024]{1,0:T(8,128)(2,1)S(1)}, bf16[32,1024]{1,0:T(8,128)(2,1)S(1)}, u32[]{:S(2)}, u32[]{:S(2)}) collective-permute-start(bf16[32,1024]{1,0:T(8,128)(2,1)S(1)} %get-tuple-element.188), channel_id=1, source_target_pairs={{0,96},{32,0},{64,32},{96,64},{1,97},{33,1},{65,33},{97,65},{2,98}... | collective-permute-start | bytes 196616 | tf_op jit(solution)/shard_map/ppermute | solution.py:44
  240.8 32.2 %copy-start.1 = (bf16[1024,1024]{1,0:T(8,128)(2,1)S(1)}, bf16[1024,1024]{1,0:T(8,128)(2,1)}, u32[]{:S(2)}) copy-start(bf16[1024,1024]{1,0:T(8,128)(2,1)} %all-gather.3.cloned.1.call-done.band_ref) | copy-start | bytes 6291460
  240.9 8.7 %collective-permute-start.15 = (bf16[72,512]{1,0:T(8,128)(2,1)S(1)}, bf16[72,512]{1,0:T(8,128)(2,1)S(1)}, u32[]{:S(2)}, u32[]{:S(2)}) collective-permute-start(bf16[72,512]{1,0:T(8,128)(2,1)S(1)} %get-tuple-element.184), channel_id=1, source_target_pairs={{0,2},{2,4},{4,6},{6,0},{1,3},{3,5},{5,7},{7,1},{8,10},{10,12},{12... | collective-permute-start | bytes 221192 | tf_op jit(solution)/shard_map/ppermute | solution.py:44
  242.5 7.1 %collective-permute-start.16 = (bf16[72,512]{1,0:T(8,128)(2,1)S(1)}, bf16[72,512]{1,0:T(8,128)(2,1)S(1)}, u32[]{:S(2)}, u32[]{:S(2)}) collective-permute-start(bf16[72,512]{1,0:T(8,128)(2,1)S(1)} %get-tuple-element.186), channel_id=1, source_target_pairs={{0,4},{2,6},{4,0},{6,2},{1,5},{3,7},{5,1},{7,3},{8,12},{10,14},{12... | collective-permute-start | bytes 221192 | tf_op jit(solution)/shard_map/ppermute | solution.py:44
  243.8 5.8 %collective-permute-start.17 = (bf16[72,512]{1,0:T(8,128)(2,1)S(1)}, bf16[72,512]{1,0:T(8,128)(2,1)S(1)}, u32[]{:S(2)}, u32[]{:S(2)}) collective-permute-start(bf16[72,512]{1,0:T(8,128)(2,1)S(1)} %get-tuple-element.185), channel_id=1, source_target_pairs={{0,6},{2,0},{4,2},{6,4},{1,7},{3,1},{5,3},{7,5},{8,14},{10,8},{12,... | collective-permute-start | bytes 221192 | tf_op jit(solution)/shard_map/ppermute | solution.py:44
  246.3 14.2 %collective-permute-start.8 = (bf16[4,32,1024]{2,1,0:T(8,128)(2,1)S(1)}, bf16[4,32,1024]{2,1,0:T(8,128)(2,1)S(1)}, u32[]{:S(2)}, u32[]{:S(2)}) collective-permute-start(bf16[4,32,1024]{2,1,0:T(8,128)(2,1)S(1)} %pad_maximum_fusion.refs_0_), channel_id=1, source_target_pairs={{0,2},{2,4},{4,6},{6,0},{1,3},{3,5},{5,7},{7,1},{8,10},{10,12},{12... | collective-permute-start | bytes 786440 | tf_op jit(solution)/shard_map/ppermute | solution.py:44
  246.3 14.2 %collective-permute-start.9 = (bf16[4,32,1024]{2,1,0:T(8,128)(2,1)S(1)}, bf16[4,32,1024]{2,1,0:T(8,128)(2,1)S(1)}, u32[]{:S(2)}, u32[]{:S(2)}) collective-permute-start(bf16[4,32,1024]{2,1,0:T(8,128)(2,1)S(1)} %pad_maximum_fusion.refs_0_), channel_id=1, source_target_pairs={{0,6},{2,0},{4,2},{6,4},{1,7},{3,1},{5,3},{7,5},{8,14},{10,8},{12,... | collective-permute-start | bytes 786440 | tf_op jit(solution)/shard_map/ppermute | solution.py:44
  249.6 11.5 %collective-permute-start.10 = (bf16[4,32,1024]{2,1,0:T(8,128)(2,1)S(1)}, bf16[4,32,1024]{2,1,0:T(8,128)(2,1)S(1)}, u32[]{:S(2)}, u32[]{:S(2)}) collective-permute-start(bf16[4,32,1024]{2,1,0:T(8,128)(2,1)S(1)} %pad_maximum_fusion.refs_0_), channel_id=1, source_target_pairs={{0,4},{2,6},{4,0},{6,2},{1,5},{3,7},{5,1},{7,3},{8,12},{10,14},{12... | collective-permute-start | bytes 786440 | tf_op jit(solution)/shard_map/ppermute | solution.py:44
  249.6 7.5 %collective-permute-start.18 = (bf16[72,512]{1,0:T(8,128)(2,1)S(1)}, bf16[72,512]{1,0:T(8,128)(2,1)S(1)}, u32[]{:S(2)}, u32[]{:S(2)}) collective-permute-start(bf16[72,512]{1,0:T(8,128)(2,1)S(1)} %fusion.1), channel_id=1, source_target_pairs={{0,16},{8,24},{16,0},{24,8},{1,17},{9,25},{17,1},{25,9},{2,18},{10... | collective-permute-start | bytes 221192 | tf_op jit(solution)/shard_map/ppermute | solution.py:37
  254.7 4.4 %collective-permute-start.19 = (bf16[72,512]{1,0:T(8,128)(2,1)S(1)}, bf16[72,512]{1,0:T(8,128)(2,1)S(1)}, u32[]{:S(2)}, u32[]{:S(2)}) collective-permute-start(bf16[72,512]{1,0:T(8,128)(2,1)S(1)} %fusion.1), channel_id=1, source_target_pairs={{0,8},{8,0},{16,24},{24,16},{1,9},{9,1},{17,25},{25,17},{2,10},{10... | collective-permute-start | bytes 221192 | tf_op jit(solution)/shard_map/ppermute | solution.py:37
  257.1 7.5 %collective-permute-start.11 = (bf16[4,32,1024]{2,1,0:T(8,128)(2,1)S(1)}, bf16[4,32,1024]{2,1,0:T(8,128)(2,1)S(1)}, u32[]{:S(2)}, u32[]{:S(2)}) collective-permute-start(bf16[4,32,1024]{2,1,0:T(8,128)(2,1)S(1)} %pad_maximum_fusion.refs_0_), channel_id=1, source_target_pairs={{0,1},{1,0},{2,3},{3,2},{4,5},{5,4},{6,7},{7,6},{8,9},{9,8},{10,11... | collective-permute-start | bytes 786440 | tf_op jit(solution)/shard_map/ppermute | solution.py:26
  259.0 5.6 %collective-permute-start.20 = (bf16[72,512]{1,0:T(8,128)(2,1)S(1)}, bf16[72,512]{1,0:T(8,128)(2,1)S(1)}, u32[]{:S(2)}, u32[]{:S(2)}) collective-permute-start(bf16[72,512]{1,0:T(8,128)(2,1)S(1)} %fusion.1), channel_id=1, source_target_pairs={{0,24},{8,16},{16,8},{24,0},{1,25},{9,17},{17,9},{25,1},{2,26},{10... | collective-permute-start | bytes 221192 | tf_op jit(solution)/shard_map/ppermute | solution.py:37
  260.6 4.0 %collective-permute-start.12 = (bf16[4,32,1024]{2,1,0:T(8,128)(2,1)S(1)}, bf16[4,32,1024]{2,1,0:T(8,128)(2,1)S(1)}, u32[]{:S(2)}, u32[]{:S(2)}) collective-permute-start(bf16[4,32,1024]{2,1,0:T(8,128)(2,1)S(1)} %collective-permute-done.8.refs_1_), channel_id=1, source_target_pairs={{0,1},{1,0},{2,3},{3,2},{4,5},{5,4},{6,7},{7,6},{8,9},{9,8},{10,11... | collective-permute-start | bytes 786440 | tf_op jit(solution)/shard_map/ppermute | solution.py:26
  260.6 4.1 %collective-permute-start.13 = (bf16[4,32,1024]{2,1,0:T(8,128)(2,1)S(1)}, bf16[4,32,1024]{2,1,0:T(8,128)(2,1)S(1)}, u32[]{:S(2)}, u32[]{:S(2)}) collective-permute-start(bf16[4,32,1024]{2,1,0:T(8,128)(2,1)S(1)} %collective-permute-done.9.refs_3_), channel_id=1, source_target_pairs={{0,1},{1,0},{2,3},{3,2},{4,5},{5,4},{6,7},{7,6},{8,9},{9,8},{10,11... | collective-permute-start | bytes 786440 | tf_op jit(solution)/shard_map/ppermute | solution.py:26
  261.1 3.6 %collective-permute-start.14 = (bf16[4,32,1024]{2,1,0:T(8,128)(2,1)S(1)}, bf16[4,32,1024]{2,1,0:T(8,128)(2,1)S(1)}, u32[]{:S(2)}, u32[]{:S(2)}) collective-permute-start(bf16[4,32,1024]{2,1,0:T(8,128)(2,1)S(1)} %collective-permute-done.10.refs_2_), channel_id=1, source_target_pairs={{0,1},{1,0},{2,3},{3,2},{4,5},{5,4},{6,7},{7,6},{8,9},{9,8},{10,11... | collective-permute-start | bytes 786440 | tf_op jit(solution)/shard_map/ppermute | solution.py:26
  264.7 11.3 %collective-permute-start.21 = (bf16[72,512]{1,0:T(8,128)(2,1)S(1)}, bf16[72,512]{1,0:T(8,128)(2,1)S(1)}, u32[]{:S(2)}, u32[]{:S(2)}) collective-permute-start(bf16[72,512]{1,0:T(8,128)(2,1)S(1)} %add_add_fusion.1), channel_id=1, source_target_pairs={{0,64},{32,96},{64,0},{96,32},{1,65},{33,97},{65,1},{97,33},{2,66}... | collective-permute-start | bytes 221192 | tf_op jit(solution)/shard_map/ppermute | solution.py:37
  266.9 9.1 %collective-permute-start.22 = (bf16[72,512]{1,0:T(8,128)(2,1)S(1)}, bf16[72,512]{1,0:T(8,128)(2,1)S(1)}, u32[]{:S(2)}, u32[]{:S(2)}) collective-permute-start(bf16[72,512]{1,0:T(8,128)(2,1)S(1)} %add_add_fusion.1), channel_id=1, source_target_pairs={{0,32},{32,0},{64,96},{96,64},{1,33},{33,1},{65,97},{97,65},{2,34}... | collective-permute-start | bytes 221192 | tf_op jit(solution)/shard_map/ppermute | solution.py:37
  268.0 8.0 %collective-permute-start.23 = (bf16[72,512]{1,0:T(8,128)(2,1)S(1)}, bf16[72,512]{1,0:T(8,128)(2,1)S(1)}, u32[]{:S(2)}, u32[]{:S(2)}) collective-permute-start(bf16[72,512]{1,0:T(8,128)(2,1)S(1)} %add_add_fusion.1), channel_id=1, source_target_pairs={{0,96},{32,64},{64,32},{96,0},{1,97},{33,65},{65,33},{97,1},{2,98}... | collective-permute-start | bytes 221192 | tf_op jit(solution)/shard_map/ppermute | solution.py:37
  273.0 1.6 copy-start.2
  276.1 12.4 %collective-permute-start.24 = (bf16[256,1024]{1,0:T(8,128)(2,1)S(1)}, bf16[256,1024]{1,0:T(8,128)(2,1)S(1)}, u32[]{:S(2)}, u32[]{:S(2)}) collective-permute-start(bf16[256,1024]{1,0:T(8,128)(2,1)S(1)} %get-tuple-element.136), channel_id=1, source_target_pairs={{0,32},{32,64},{64,96},{96,0},{1,33},{33,65},{65,97},{97,1},{2,34}... | collective-permute-start | bytes 1572872 | tf_op jit(solution)/shard_map/ppermute | solution.py:44
  277.5 10.9 %collective-permute-start.25 = (bf16[256,1024]{1,0:T(8,128)(2,1)S(1)}, bf16[256,1024]{1,0:T(8,128)(2,1)S(1)}, u32[]{:S(2)}, u32[]{:S(2)}) collective-permute-start(bf16[256,1024]{1,0:T(8,128)(2,1)S(1)} %get-tuple-element.137), channel_id=1, source_target_pairs={{0,96},{32,0},{64,32},{96,64},{1,97},{33,1},{65,33},{97,65},{2,98}... | collective-permute-start | bytes 1572872 | tf_op jit(solution)/shard_map/ppermute | solution.py:44
  279.4 11.7 %collective-permute-start.26 = (bf16[256,1024]{1,0:T(8,128)(2,1)S(1)}, bf16[256,1024]{1,0:T(8,128)(2,1)S(1)}, u32[]{:S(2)}, u32[]{:S(2)}) collective-permute-start(bf16[256,1024]{1,0:T(8,128)(2,1)S(1)} %get-tuple-element.138), channel_id=1, source_target_pairs={{0,8},{8,16},{16,24},{24,0},{1,9},{9,17},{17,25},{25,1},{2,10},{10... | collective-permute-start | bytes 1572872 | tf_op jit(solution)/shard_map/ppermute | solution.py:44
  279.6 12.4 %collective-permute-start.27 = (bf16[256,1024]{1,0:T(8,128)(2,1)S(1)}, bf16[256,1024]{1,0:T(8,128)(2,1)S(1)}, u32[]{:S(2)}, u32[]{:S(2)}) collective-permute-start(bf16[256,1024]{1,0:T(8,128)(2,1)S(1)} %get-tuple-element.139), channel_id=1, source_target_pairs={{0,24},{8,0},{16,8},{24,16},{1,25},{9,1},{17,9},{25,17},{2,26},{10... | collective-permute-start | bytes 1572872 | tf_op jit(solution)/shard_map/ppermute | solution.py:44
  288.4 3.6 %copy-start.15 = (bf16[256,1024]{1,0:T(8,128)(2,1)}, bf16[256,1024]{1,0:T(8,128)(2,1)S(1)}, u32[]{:S(2)}) copy-start(bf16[256,1024]{1,0:T(8,128)(2,1)S(1)} %collective-permute-done.24.refs_1_.refs_2_) | copy-start | bytes 1572868
  288.4 3.6 %copy-start.16 = (bf16[256,1024]{1,0:T(8,128)(2,1)}, bf16[256,1024]{1,0:T(8,128)(2,1)S(1)}, u32[]{:S(2)}) copy-start(bf16[256,1024]{1,0:T(8,128)(2,1)S(1)} %collective-permute-done.25.refs_3_) | copy-start | bytes 1572868
  291.1 0.9 copy-start.17
  292.0 0.8 copy-start.18
  294.5 8.5 %collective-permute-start.28 = (bf16[128,1024]{1,0:T(8,128)(2,1)S(1)}, bf16[128,1024]{1,0:T(8,128)(2,1)S(1)}, u32[]{:S(2)}, u32[]{:S(2)}) collective-permute-start(bf16[128,1024]{1,0:T(8,128)(2,1)S(1)} %get-tuple-element.158), channel_id=1, source_target_pairs={{0,32},{32,64},{64,96},{96,0},{1,33},{33,65},{65,97},{97,1},{2,34}... | collective-permute-start | bytes 786440 | tf_op jit(solution)/shard_map/ppermute | solution.py:44
  294.6 8.4 %collective-permute-start.29 = (bf16[128,1024]{1,0:T(8,128)(2,1)S(1)}, bf16[128,1024]{1,0:T(8,128)(2,1)S(1)}, u32[]{:S(2)}, u32[]{:S(2)}) collective-permute-start(bf16[128,1024]{1,0:T(8,128)(2,1)S(1)} %get-tuple-element.159), channel_id=1, source_target_pairs={{0,96},{32,0},{64,32},{96,64},{1,97},{33,1},{65,33},{97,65},{2,98}... | collective-permute-start | bytes 786440 | tf_op jit(solution)/shard_map/ppermute | solution.py:44
  297.8 7.6 %collective-permute-start.30 = (bf16[128,1024]{1,0:T(8,128)(2,1)S(1)}, bf16[128,1024]{1,0:T(8,128)(2,1)S(1)}, u32[]{:S(2)}, u32[]{:S(2)}) collective-permute-start(bf16[128,1024]{1,0:T(8,128)(2,1)S(1)} %get-tuple-element.162), channel_id=1, source_target_pairs={{0,8},{8,16},{16,24},{24,0},{1,9},{9,17},{17,25},{25,1},{2,10},{10... | collective-permute-start | bytes 786440 | tf_op jit(solution)/shard_map/ppermute | solution.py:44
  298.8 6.7 %collective-permute-start.31 = (bf16[128,1024]{1,0:T(8,128)(2,1)S(1)}, bf16[128,1024]{1,0:T(8,128)(2,1)S(1)}, u32[]{:S(2)}, u32[]{:S(2)}) collective-permute-start(bf16[128,1024]{1,0:T(8,128)(2,1)S(1)} %get-tuple-element.163), channel_id=1, source_target_pairs={{0,24},{8,0},{16,8},{24,16},{1,25},{9,1},{17,9},{25,17},{2,26},{10... | collective-permute-start | bytes 786440 | tf_op jit(solution)/shard_map/ppermute | solution.py:44
  303.0 2.4 copy-start.19
  303.0 2.4 copy-start.20
  305.4 0.7 copy-start.21
  306.1 0.7 copy-start.22
Sparse Core Ops, SparseCore 0:
  101.3 27.3 all-gather.2
  130.4 30.8 all-gather.4

commit v4 on v3

--- a/solution.py
+++ b/solution.py
@@ -94,7 +94,6 @@
         kernel(place, square, band, (((1, 0),), ((3, 1),), ((0, 0),), ((0, 1),)))
         for place, (kernel, band, _) in zip(places, rings)
     ]
-    sent, rests = lax.optimization_barrier((sent, rests))
     half, width = rests[0][0].shape
     passed = whole_call(
         pass_on_kernel,

time: 321 us -> 321 us (level)
  no operation moved by 1% of the time
where the time goes in v4:
time: 321 us; the launch traced here: 316 us
  blocking collectives  86.3 us (27%)
  Pallas kernels  76.6 us (24%)
  waiting for transfers between devices  72.9 us (23%)
  starting transfers between devices  44.3 us (14%)
  local copies, waits for them, and re-layouts  19.9 us (6%)
  between operations  14.6 us (5%)
    all_to_all x1, blocking collectives, exchange(): return lax.all_to_all(value, axes, split_axis=0, concat_axis=0, tiled=True)  86.3 us
    all_to_all x1, waiting for transfers between devices, exchange(): return lax.all_to_all(value, axes, split_axis=0, concat_axis=0, tiled=True)  43.5 us
    ppermute x17, starting transfers between devices, shift(): lax.ppermute(value, axis, [(i, (i + step) % size) for i in range(size)])  25.5 us
    unnamed x51, local copies, waits for them, and re-layouts  17.6 us
    ppermute x17, waiting for transfers between devices, shift(): lax.ppermute(value, axis, [(i, (i + step) % size) for i in range(size)])  13.2 us
    pallas_call x1, Pallas kernels, forward(): pl.pallas_call(forward_kernel, in_specs=[inside] * 4, out_specs=(inside,...  12.8 us
    pallas_call x1, Pallas kernels, hidden_grads(): pl.pallas_call(functools.partial(hidden_kernel, capacity), in_specs=[insi...  11.8 us
    pallas_call x1, Pallas kernels, terms(): pl.pallas_call(term_kernel, in_specs=[inside] * 4, out_specs=(inside, ins...  11.6 us
  transfers between devices with their start and end apart: 35, of which 14 were waited for; matrix products, arithmetic and copies ran while one was open for 1% of the time, Pallas kernels for 17%

profile of v4, /device:TPU:0, one launch (start us, length us, event | category | flops | bytes accessed | tf_op | source)
XLA Modules:
  0.0 316.2 jit_solution(2612766810625647741)
XLA Ops:
  7.2 0.7 tile.8
  8.0 6.9 %place.1 = (bf16[64,96,512]{2,1,0:T(8,128)(2,1)}, f32[64,256]{1,0:T(8,128)S(1)}, bf16[32,4096]{1,0:T(8,128)(2,1)S(1)}) custom-call(bf16[32,4096]{1,0:T(8,128)(2,1)} %pre_ref.3, bf16[32,4096]{1,0:T(8,128)(2,1)} %grad_ref.3, f32[1,4096]{1,0:T(1,128)} %bitcast.42, s32[8,256]{1,0:T(8,128)S(1)} %tile.9.routes_ref), custom_call_target="tpu_custom_call" | custom-call | tf_op jit(solution)/shard_map/place/pallas_call | solution.py:318
  14.9 86.3 %all_to_all.10.got_ref = bf16[64,96,512]{2,1,0:T(8,128)(2,1)} all-to-all(bf16[64,96,512]{2,1,0:T(8,128)(2,1)} %get-tuple-element.74), channel_id=1, replica_groups=mesh['y'=4,'x'=4,'z'=4,'core'=2] {'y','x','z'}, dimensions={0} | all-to-all | bytes 12582912 | tf_op jit(solution)/shard_map/all_to_all | solution.py:30
  101.3 2.8 copy-done
  104.0 3.7 %spread.3.own_ref = bf16[384,4096]{1,0:T(8,128)(2,1)} custom-call(bf16[64,96,512]{2,1,0:T(8,128)(2,1)S(1)} %copy-done, bf16[384,384]{1,0:T(8,128)(2,1)S(1)} %copy-done.4), custom_call_target="tpu_custom_call" | custom-call | tf_op jit(solution)/shard_map/spread/pallas_call | solution.py:367
  107.8 2.6 spread.2.own_ref
  110.3 0.8 collective-permute-start
  111.1 2.7 collective-permute-done.1.other_ref
  113.8 2.9 copy-done.11
  116.6 2.9 copy-done.13
  119.5 12.8 %forward.1 = (f32[768,768]{1,0:T(8,128)S(1)}, f32[768,768]{1,0:T(8,128)S(1)}) custom-call(bf16[384,4096]{1,0:T(8,128)(2,1)} %spread.3.own_ref, bf16[384,4096]{1,0:T(8,128)(2,1)} %collective-permute-done.1.other_ref, bf16[1,4096,768]{2,1,0:T(8,128)(2,1)S(1)} %copy-done.11, bf16[1,4096,768]{2,1,0:T(8,128)(2,1)S(1)} %copy-done.13), custom_call_target="tpu_custom_call" | custom-call | flops 9663676416 | bytes 24000000 | tf_op jit(solution)/shard_map/forward/pallas_call | solution.py:396
  132.3 2.8 copy-done.10
  135.1 11.8 %hidden_grads.1 = (bf16[768,768]{1,0:T(8,128)(2,1)S(1)}, bf16[768,768]{1,0:T(8,128)(2,1)S(1)}, f32[512,128]{1,0:T(8,128)S(1)}, f32[512,128]{1,0:T(8,128)}) custom-call(bf16[384,4096]{1,0:T(8,128)(2,1)} %copy-done.3, bf16[384,4096]{1,0:T(8,128)(2,1)} %collective-permute-done.other_ref, bf16[1,768,4096]{2,1,0:T(8,128)(2,1)S(1)} %copy-done.10, ...), custom_call_target="tpu_custom_call" | custom-call | flops 4831838208 | bytes 24000000 | tf_op jit(solution)/shard_map/hidden_grads/pallas_call | solution.py:447
  146.8 0.7 copy-done.8
  147.6 11.6 %terms.1 = (bf16[384,4096]{1,0:T(8,128)(2,1)S(1)}, bf16[384,4096]{1,0:T(8,128)(2,1)}) custom-call(bf16[768,768]{1,0:T(8,128)(2,1)S(1)} %get-tuple-element.80.gg_ref, bf16[768,768]{1,0:T(8,128)(2,1)S(1)} %get-tuple-element.81.gu_ref, bf16[1,4096,768]{2,1,0:T(8,128)(2,1)S(1)} %copy-done.12, bf16[1,4096,768]{2,1,0:T(8,128)(2,1)S(1)} %copy-done.14), custom_call_target="tpu_custom_call" | custom-call | flops 9663676416 | bytes 17000000 | tf_op jit(solution)/shard_map/terms/pallas_call | solution.py:486
  159.6 1.7 all-gather.5.cloned.1.call-done.band_ref
  161.3 3.8 %collective-permute-done.2.other_ref = bf16[384,4096]{1,0:T(8,128)(2,1)} collective-permute-done((bf16[384,4096]{1,0:T(8,128)(2,1)}, bf16[384,4096]{1,0:T(8,128)(2,1)}, u32[]{:S(2)}, u32[]{:S(2)}) %collective-permute-start.2) | collective-permute-done | bytes 3145760 | tf_op jit(solution)/shard_map/ppermute | solution.py:26
  165.5 0.9 copy-done.9
  166.5 5.5 %pack.1 = bf16[64,56,512]{2,1,0:T(8,128)(2,1)} custom-call(bf16[384,4096]{1,0:T(8,128)(2,1)S(1)} %get-tuple-element.82.own_ref, bf16[384,4096]{1,0:T(8,128)(2,1)} %collective-permute-done.2.other_ref, bf16[384,384]{1,0:T(8,128)(2,1)S(1)} %copy-done.4, f32[512,128]{1,0:T(8,128)S(1)} %copy-done.9, f32[512,128]{1,0:T(8,128)} %collective-permute-done.3.other_part_ref, ...), custom_call_target="tpu_custom_call" | custom-call | tf_op jit(solution)/shard_map/pack/pallas_call | solution.py:538
  171.9 5.9 %all-to-all-start.1 = ((bf16[64,56,512]{2,1,0:T(8,128)(2,1)}), bf16[64,56,512]{2,1,0:T(8,128)(2,1)}, u32[]{:S(2)}, u32[]{:S(2)}) async-start(bf16[64,56,512]{2,1,0:T(8,128)(2,1)} %pack.1), calls=%async_computation.1 | async-start | bytes 7340032 | tf_op jit(solution)/shard_map/all_to_all | solution.py:30
  178.2 2.0 mixings.1.mix_ref
  180.3 43.5 %all-to-all-done.1.back_ref = bf16[64,56,512]{2,1,0:T(8,128)(2,1)} async-done(((bf16[64,56,512]{2,1,0:T(8,128)(2,1)}), bf16[64,56,512]{2,1,0:T(8,128)(2,1)}, u32[]{:S(2)}, u32[]{:S(2)}) %all-to-all-start.1) | async-done | bytes 3670048 | tf_op jit(solution)/shard_map/all_to_all | solution.py:30
  223.8 1.0 copy-done.6
  224.8 5.8 %finish.1 = (bf16[32,4096]{1,0:T(8,128)(2,1)}, bf16[4,32,1024]{2,1,0:T(8,128)(2,1)S(1)}, f32[8,72,512]{2,1,0:T(8,128)S(1)}, f32[32,8]{1,0:T(8,128)S(1)}) custom-call(bf16[512,3072]{1,0:T(8,128)(2,1)S(1)} %mixings.1.mix_ref, bf16[64,56,512]{2,1,0:T(8,128)(2,1)} %all-to-all-done.1.back_ref, bf16[32,4096]{1,0:T(8,128)(2,1)} %pre_ref.3, ...), custom_call_target="tpu_custom_call" | custom-call | tf_op jit(solution)/shard_map/finish/pallas_call | solution.py:661
  230.7 1.0 copy-done.5
  232.0 2.7 collective-permute-start.5
  234.6 1.0 collective-permute-start.6
  235.6 3.4 %collective-permute-done.4 = bf16[32,1024]{1,0:T(8,128)(2,1)S(1)} collective-permute-done((bf16[32,1024]{1,0:T(8,128)(2,1)S(1)}, bf16[32,1024]{1,0:T(8,128)(2,1)S(1)}, u32[]{:S(2)}, u32[]{:S(2)}) %collective-permute-start.4) | collective-permute-done | bytes 65568 | tf_op jit(solution)/shard_map/ppermute | solution.py:44
  239.0 0.6 collective-permute-done.6
  239.7 1.2 bitcast_add_fusion
  240.9 1.6 collective-permute-start.15
  242.5 1.3 collective-permute-start.16
  243.8 2.5 collective-permute-start.17
  246.3 3.2 %collective-permute-start.9 = (bf16[4,32,1024]{2,1,0:T(8,128)(2,1)S(1)}, bf16[4,32,1024]{2,1,0:T(8,128)(2,1)S(1)}, u32[]{:S(2)}, u32[]{:S(2)}) collective-permute-start(bf16[4,32,1024]{2,1,0:T(8,128)(2,1)S(1)} %pad_maximum_fusion.refs_0_), channel_id=1, source_target_pairs={{0,6},{2,0},{4,2},{6,4},{1,7},{3,1},{5,3},{7,5},{8,14},{10,8},{12,... | collective-permute-start | bytes 786440 | tf_op jit(solution)/shard_map/ppermute | solution.py:44
  249.6 5.0 %collective-permute-start.18 = (bf16[72,512]{1,0:T(8,128)(2,1)S(1)}, bf16[72,512]{1,0:T(8,128)(2,1)S(1)}, u32[]{:S(2)}, u32[]{:S(2)}) collective-permute-start(bf16[72,512]{1,0:T(8,128)(2,1)S(1)} %fusion.1), channel_id=1, source_target_pairs={{0,16},{8,24},{16,0},{24,8},{1,17},{9,25},{17,1},{25,9},{2,18},{10... | collective-permute-start | bytes 221192 | tf_op jit(solution)/shard_map/ppermute | solution.py:37
  254.7 2.4 collective-permute-done.18
  257.1 1.9 collective-permute-done.19
  259.0 1.6 collective-permute-start.20
  261.3 3.3 %collective-permute-done.20 = bf16[72,512]{1,0:T(8,128)(2,1)S(1)} collective-permute-done((bf16[72,512]{1,0:T(8,128)(2,1)S(1)}, bf16[72,512]{1,0:T(8,128)(2,1)S(1)}, u32[]{:S(2)}, u32[]{:S(2)}) %collective-permute-start.20) | collective-permute-done | bytes 73760 | tf_op jit(solution)/shard_map/ppermute | solution.py:37
  264.7 2.2 collective-permute-start.21
  266.9 1.2 collective-permute-start.22
  268.0 1.0 collective-permute-start.23
  269.0 4.0 %gather_square.1.square_ref = bf16[4,256,1024]{2,1,0:T(8,128)(2,1)S(1)} custom-call(s32[3]{0:T(128)S(1)} %pad_add_fusion.place_ref, bf16[4,32,1024]{2,1,0:T(8,128)(2,1)S(1)} %pad_maximum_fusion.refs_0_, bf16[4,32,1024]{2,1,0:T(8,128)(2,1)S(1)} %collective-permute-done.8.refs_1_, bf16[4,32,1024]{2,1,0:T(8,128)(2,1)S(1)} %collective-permute-done.10.refs_2_, ...), custom_call_target="tpu_custom_call" | custom-call | tf_op jit(solution)/shard_map/gather_square/pallas_call | solution.py:177
  273.0 1.3 context_part.2
  274.6 1.4 weight_part.2
  276.1 1.5 collective-permute-start.24
  277.5 1.8 collective-permute-start.25
  279.6 3.0 collective-permute-start.27
  282.6 1.3 weight_part.3
  283.9 1.3 context_part.3
  285.2 3.2 %collective-permute-done.24.refs_1_.refs_2_ = bf16[256,1024]{1,0:T(8,128)(2,1)S(1)} collective-permute-done((bf16[256,1024]{1,0:T(8,128)(2,1)S(1)}, bf16[256,1024]{1,0:T(8,128)(2,1)S(1)}, u32[]{:S(2)}, u32[]{:S(2)}) %collective-permute-start.24) | collective-permute-done | bytes 524320 | tf_op jit(solution)/shard_map/ppermute | solution.py:44
  288.4 2.7 collective-permute-done.26.refs_5_.refs_8_
  291.1 0.9 collective-permute-done.27.refs_7_.refs_9_
  292.0 0.8 copy-done.18
  292.8 1.8 pass_on.1
  294.6 3.2 %collective-permute-start.29 = (bf16[128,1024]{1,0:T(8,128)(2,1)S(1)}, bf16[128,1024]{1,0:T(8,128)(2,1)S(1)}, u32[]{:S(2)}, u32[]{:S(2)}) collective-permute-start(bf16[128,1024]{1,0:T(8,128)(2,1)S(1)} %get-tuple-element.135), channel_id=1, source_target_pairs={{0,96},{32,0},{64,32},{96,64},{1,97},{33,1},{65,33},{97,65},{2,98}... | collective-permute-start | bytes 786440 | tf_op jit(solution)/shard_map/ppermute | solution.py:44
  297.8 0.9 collective-permute-start.30
  298.8 2.3 collective-permute-start.31
  301.1 0.7 copy.32
  301.7 0.6 slice.7
  302.3 0.7 slice_bitcast_fusion
  303.0 2.4 collective-permute-done.30.refs_10_
  305.4 0.7 copy-done.21
  306.2 3.0 close.1
  (95 shorter events, 3.4 us)
Async XLA Ops:
  7.2 152.5 %all-gather.3.cloned.1.call-start = ((), (), s32[]{:S(2)}) async-start(), calls=%async_computation.2 | async-start | bytes 2621440 | tf_op jit(solution)/shard_map/all_gather | solution.py:713
  14.9 86.3 %copy-start.7 = (bf16[32,4096]{1,0:T(8,128)(2,1)}, bf16[32,4096]{1,0:T(8,128)(2,1)S(1)}, u32[]{:S(2)}) copy-start(bf16[32,4096]{1,0:T(8,128)(2,1)S(1)} %get-tuple-element.100.normed_ref) | copy-start | bytes 786436
  14.9 86.4 %copy-start.4 = (bf16[384,384]{1,0:T(8,128)(2,1)S(1)}, bf16[384,384]{1,0:T(8,128)(2,1)}, u32[]{:S(2)}) copy-start(bf16[384,384]{1,0:T(8,128)(2,1)} %constant.71.clone.order_ref) | copy-start | bytes 884740
  101.2 60.1 %all-gather.5.cloned.1.call-start = ((), (), s32[]{:S(2)}) async-start(), calls=%async_computation.3 | async-start | bytes 2621440 | tf_op jit(solution)/shard_map/all_gather | solution.py:714
  101.3 2.8 copy-start
  107.7 6.0 %collective-permute-start.1 = (bf16[384,4096]{1,0:T(8,128)(2,1)}, bf16[384,4096]{1,0:T(8,128)(2,1)}, u32[]{:S(2)}, u32[]{:S(2)}) collective-permute-start(bf16[384,4096]{1,0:T(8,128)(2,1)} %spread.3.own_ref), channel_id=1, source_target_pairs={{0,1},{1,0},{2,3},{3,2},{4,5},{5,4},{6,7},{7,6},{8,9},{9,8},{10,11... | collective-permute-start | bytes 9437192 | tf_op jit(solution)/shard_map/ppermute | solution.py:26
  110.3 21.9 %copy-start.3 = (bf16[384,4096]{1,0:T(8,128)(2,1)}, bf16[384,4096]{1,0:T(8,128)(2,1)S(1)}, u32[]{:S(2)}) copy-start(bf16[384,4096]{1,0:T(8,128)(2,1)S(1)} %spread.2.own_ref) | copy-start | bytes 9437188
  110.3 21.9 %collective-permute-start = (bf16[384,4096]{1,0:T(8,128)(2,1)S(1)}, bf16[384,4096]{1,0:T(8,128)(2,1)}, u32[]{:S(2)}, u32[]{:S(2)}) collective-permute-start(bf16[384,4096]{1,0:T(8,128)(2,1)S(1)} %spread.2.own_ref), channel_id=1, source_target_pairs={{0,1},{1,0},{2,3},{3,2},{4,5},{5,4},{6,7},{7,6},{8,9},{9,8},{10,11... | collective-permute-start | bytes 9437192 | tf_op jit(solution)/shard_map/ppermute | solution.py:26
  113.8 2.9 copy-start.11
  116.6 2.9 copy-start.13
  132.3 2.8 copy-start.10
  135.1 12.5 %copy-start.12 = (bf16[1,4096,768]{2,1,0:T(8,128)(2,1)S(1)}, bf16[1,4096,768]{2,1,0:T(8,128)(2,1)}, u32[]{:S(2)}) copy-start(bf16[1,4096,768]{2,1,0:T(8,128)(2,1)} %gate_ref.3) | copy-start | bytes 18874372
  135.1 12.5 %copy-start.14 = (bf16[1,4096,768]{2,1,0:T(8,128)(2,1)S(1)}, bf16[1,4096,768]{2,1,0:T(8,128)(2,1)}, u32[]{:S(2)}) copy-start(bf16[1,4096,768]{2,1,0:T(8,128)(2,1)} %up_ref.3) | copy-start | bytes 18874372
  146.8 0.7 copy-start.8
  159.1 6.0 %collective-permute-start.2 = (bf16[384,4096]{1,0:T(8,128)(2,1)}, bf16[384,4096]{1,0:T(8,128)(2,1)}, u32[]{:S(2)}, u32[]{:S(2)}) collective-permute-start(bf16[384,4096]{1,0:T(8,128)(2,1)} %get-tuple-element.83), channel_id=1, source_target_pairs={{0,1},{1,0},{2,3},{3,2},{4,5},{5,4},{6,7},{7,6},{8,9},{9,8},{10,11... | collective-permute-start | bytes 9437192 | tf_op jit(solution)/shard_map/ppermute | solution.py:26
  159.2 6.3 %collective-permute-start.3 = (f32[512,128]{1,0:T(8,128)}, f32[512,128]{1,0:T(8,128)}, u32[]{:S(2)}, u32[]{:S(2)}) collective-permute-start(f32[512,128]{1,0:T(8,128)} %get-tuple-element.88), channel_id=1, source_target_pairs={{0,1},{1,0},{2,3},{3,2},{4,5},{5,4},{6,7},{7,6},{8,9},{9,8},{10,11... | collective-permute-start | bytes 786440 | tf_op jit(solution)/shard_map/ppermute | solution.py:26
  165.5 1.0 copy-start.9
  171.9 5.9 %copy-start.23 = (s32[32,8]{0,1:T(8,128)S(1)}, s32[32,8]{0,1:T(8,128)}, u32[]{:S(2)}) copy-start(s32[32,8]{0,1:T(8,128)} %param.14) | copy-start | bytes 3076
  171.9 6.0 %copy-start.24 = (f32[32,8]{0,1:T(8,128)S(1)}, f32[32,8]{0,1:T(8,128)}, u32[]{:S(2)}) copy-start(f32[32,8]{0,1:T(8,128)} %param.15) | copy-start | bytes 3076
  171.9 51.9 %all-to-all-start.1 = ((bf16[64,56,512]{2,1,0:T(8,128)(2,1)}), bf16[64,56,512]{2,1,0:T(8,128)(2,1)}, u32[]{:S(2)}, u32[]{:S(2)}) async-start(bf16[64,56,512]{2,1,0:T(8,128)(2,1)} %pack.1), calls=%async_computation.1 | async-start | bytes 7340032 | tf_op jit(solution)/shard_map/all_to_all | solution.py:30
  223.8 1.0 copy-start.6
  230.7 1.0 copy-start.5
  231.7 7.9 %collective-permute-start.7 = (bf16[4,72,512]{2,1,0:T(8,128)(2,1)S(1)}, bf16[4,72,512]{2,1,0:T(8,128)(2,1)S(1)}, u32[]{:S(2)}, u32[]{:S(2)}) collective-permute-start(bf16[4,72,512]{2,1,0:T(8,128)(2,1)S(1)} %fusion), channel_id=1, source_target_pairs={{0,1},{1,0},{2,3},{3,2},{4,5},{5,4},{6,7},{7,6},{8,9},{9,8},{10,11... | collective-permute-start | bytes 884744 | tf_op jit(solution)/shard_map/ppermute | solution.py:26
  231.9 7.2 %collective-permute-start.4 = (bf16[32,1024]{1,0:T(8,128)(2,1)S(1)}, bf16[32,1024]{1,0:T(8,128)(2,1)S(1)}, u32[]{:S(2)}, u32[]{:S(2)}) collective-permute-start(bf16[32,1024]{1,0:T(8,128)(2,1)S(1)} %get-tuple-element.166), channel_id=1, source_target_pairs={{0,32},{32,64},{64,96},{96,0},{1,33},{33,65},{65,97},{97,1},{2,34}... | collective-permute-start | bytes 196616 | tf_op jit(solution)/shard_map/ppermute | solution.py:44
  232.0 7.1 %collective-permute-start.5 = (bf16[32,1024]{1,0:T(8,128)(2,1)S(1)}, bf16[32,1024]{1,0:T(8,128)(2,1)S(1)}, u32[]{:S(2)}, u32[]{:S(2)}) collective-permute-start(bf16[32,1024]{1,0:T(8,128)(2,1)S(1)} %get-tuple-element.165), channel_id=1, source_target_pairs={{0,64},{32,96},{64,0},{96,32},{1,65},{33,97},{65,1},{97,33},{2,66}... | collective-permute-start | bytes 196616 | tf_op jit(solution)/shard_map/ppermute | solution.py:44
  234.6 5.0 %collective-permute-start.6 = (bf16[32,1024]{1,0:T(8,128)(2,1)S(1)}, bf16[32,1024]{1,0:T(8,128)(2,1)S(1)}, u32[]{:S(2)}, u32[]{:S(2)}) collective-permute-start(bf16[32,1024]{1,0:T(8,128)(2,1)S(1)} %get-tuple-element.164), channel_id=1, source_target_pairs={{0,96},{32,0},{64,32},{96,64},{1,97},{33,1},{65,33},{97,65},{2,98}... | collective-permute-start | bytes 196616 | tf_op jit(solution)/shard_map/ppermute | solution.py:44
  240.8 32.2 %copy-start.1 = (bf16[1024,1024]{1,0:T(8,128)(2,1)S(1)}, bf16[1024,1024]{1,0:T(8,128)(2,1)}, u32[]{:S(2)}) copy-start(bf16[1024,1024]{1,0:T(8,128)(2,1)} %all-gather.3.cloned.1.call-done.band_ref) | copy-start | bytes 6291460
  240.9 8.7 %collective-permute-start.15 = (bf16[72,512]{1,0:T(8,128)(2,1)S(1)}, bf16[72,512]{1,0:T(8,128)(2,1)S(1)}, u32[]{:S(2)}, u32[]{:S(2)}) collective-permute-start(bf16[72,512]{1,0:T(8,128)(2,1)S(1)} %get-tuple-element.160), channel_id=1, source_target_pairs={{0,2},{2,4},{4,6},{6,0},{1,3},{3,5},{5,7},{7,1},{8,10},{10,12},{12... | collective-permute-start | bytes 221192 | tf_op jit(solution)/shard_map/ppermute | solution.py:44
  242.5 7.1 %collective-permute-start.16 = (bf16[72,512]{1,0:T(8,128)(2,1)S(1)}, bf16[72,512]{1,0:T(8,128)(2,1)S(1)}, u32[]{:S(2)}, u32[]{:S(2)}) collective-permute-start(bf16[72,512]{1,0:T(8,128)(2,1)S(1)} %get-tuple-element.162), channel_id=1, source_target_pairs={{0,4},{2,6},{4,0},{6,2},{1,5},{3,7},{5,1},{7,3},{8,12},{10,14},{12... | collective-permute-start | bytes 221192 | tf_op jit(solution)/shard_map/ppermute | solution.py:44
  243.8 5.8 %collective-permute-start.17 = (bf16[72,512]{1,0:T(8,128)(2,1)S(1)}, bf16[72,512]{1,0:T(8,128)(2,1)S(1)}, u32[]{:S(2)}, u32[]{:S(2)}) collective-permute-start(bf16[72,512]{1,0:T(8,128)(2,1)S(1)} %get-tuple-element.161), channel_id=1, source_target_pairs={{0,6},{2,0},{4,2},{6,4},{1,7},{3,1},{5,3},{7,5},{8,14},{10,8},{12,... | collective-permute-start | bytes 221192 | tf_op jit(solution)/shard_map/ppermute | solution.py:44
  246.3 14.2 %collective-permute-start.8 = (bf16[4,32,1024]{2,1,0:T(8,128)(2,1)S(1)}, bf16[4,32,1024]{2,1,0:T(8,128)(2,1)S(1)}, u32[]{:S(2)}, u32[]{:S(2)}) collective-permute-start(bf16[4,32,1024]{2,1,0:T(8,128)(2,1)S(1)} %pad_maximum_fusion.refs_0_), channel_id=1, source_target_pairs={{0,2},{2,4},{4,6},{6,0},{1,3},{3,5},{5,7},{7,1},{8,10},{10,12},{12... | collective-permute-start | bytes 786440 | tf_op jit(solution)/shard_map/ppermute | solution.py:44
  246.3 14.2 %collective-permute-start.9 = (bf16[4,32,1024]{2,1,0:T(8,128)(2,1)S(1)}, bf16[4,32,1024]{2,1,0:T(8,128)(2,1)S(1)}, u32[]{:S(2)}, u32[]{:S(2)}) collective-permute-start(bf16[4,32,1024]{2,1,0:T(8,128)(2,1)S(1)} %pad_maximum_fusion.refs_0_), channel_id=1, source_target_pairs={{0,6},{2,0},{4,2},{6,4},{1,7},{3,1},{5,3},{7,5},{8,14},{10,8},{12,... | collective-permute-start | bytes 786440 | tf_op jit(solution)/shard_map/ppermute | solution.py:44
  249.6 11.5 %collective-permute-start.10 = (bf16[4,32,1024]{2,1,0:T(8,128)(2,1)S(1)}, bf16[4,32,1024]{2,1,0:T(8,128)(2,1)S(1)}, u32[]{:S(2)}, u32[]{:S(2)}) collective-permute-start(bf16[4,32,1024]{2,1,0:T(8,128)(2,1)S(1)} %pad_maximum_fusion.refs_0_), channel_id=1, source_target_pairs={{0,4},{2,6},{4,0},{6,2},{1,5},{3,7},{5,1},{7,3},{8,12},{10,14},{12... | collective-permute-start | bytes 786440 | tf_op jit(solution)/shard_map/ppermute | solution.py:44
  249.6 7.5 %collective-permute-start.18 = (bf16[72,512]{1,0:T(8,128)(2,1)S(1)}, bf16[72,512]{1,0:T(8,128)(2,1)S(1)}, u32[]{:S(2)}, u32[]{:S(2)}) collective-permute-start(bf16[72,512]{1,0:T(8,128)(2,1)S(1)} %fusion.1), channel_id=1, source_target_pairs={{0,16},{8,24},{16,0},{24,8},{1,17},{9,25},{17,1},{25,9},{2,18},{10... | collective-permute-start | bytes 221192 | tf_op jit(solution)/shard_map/ppermute | solution.py:37
  254.7 4.4 %collective-permute-start.19 = (bf16[72,512]{1,0:T(8,128)(2,1)S(1)}, bf16[72,512]{1,0:T(8,128)(2,1)S(1)}, u32[]{:S(2)}, u32[]{:S(2)}) collective-permute-start(bf16[72,512]{1,0:T(8,128)(2,1)S(1)} %fusion.1), channel_id=1, source_target_pairs={{0,8},{8,0},{16,24},{24,16},{1,9},{9,1},{17,25},{25,17},{2,10},{10... | collective-permute-start | bytes 221192 | tf_op jit(solution)/shard_map/ppermute | solution.py:37
  257.1 7.5 %collective-permute-start.11 = (bf16[4,32,1024]{2,1,0:T(8,128)(2,1)S(1)}, bf16[4,32,1024]{2,1,0:T(8,128)(2,1)S(1)}, u32[]{:S(2)}, u32[]{:S(2)}) collective-permute-start(bf16[4,32,1024]{2,1,0:T(8,128)(2,1)S(1)} %pad_maximum_fusion.refs_0_), channel_id=1, source_target_pairs={{0,1},{1,0},{2,3},{3,2},{4,5},{5,4},{6,7},{7,6},{8,9},{9,8},{10,11... | collective-permute-start | bytes 786440 | tf_op jit(solution)/shard_map/ppermute | solution.py:26
  259.0 5.6 %collective-permute-start.20 = (bf16[72,512]{1,0:T(8,128)(2,1)S(1)}, bf16[72,512]{1,0:T(8,128)(2,1)S(1)}, u32[]{:S(2)}, u32[]{:S(2)}) collective-permute-start(bf16[72,512]{1,0:T(8,128)(2,1)S(1)} %fusion.1), channel_id=1, source_target_pairs={{0,24},{8,16},{16,8},{24,0},{1,25},{9,17},{17,9},{25,1},{2,26},{10... | collective-permute-start | bytes 221192 | tf_op jit(solution)/shard_map/ppermute | solution.py:37
  260.6 4.0 %collective-permute-start.12 = (bf16[4,32,1024]{2,1,0:T(8,128)(2,1)S(1)}, bf16[4,32,1024]{2,1,0:T(8,128)(2,1)S(1)}, u32[]{:S(2)}, u32[]{:S(2)}) collective-permute-start(bf16[4,32,1024]{2,1,0:T(8,128)(2,1)S(1)} %collective-permute-done.8.refs_1_), channel_id=1, source_target_pairs={{0,1},{1,0},{2,3},{3,2},{4,5},{5,4},{6,7},{7,6},{8,9},{9,8},{10,11... | collective-permute-start | bytes 786440 | tf_op jit(solution)/shard_map/ppermute | solution.py:26
  260.6 4.1 %collective-permute-start.13 = (bf16[4,32,1024]{2,1,0:T(8,128)(2,1)S(1)}, bf16[4,32,1024]{2,1,0:T(8,128)(2,1)S(1)}, u32[]{:S(2)}, u32[]{:S(2)}) collective-permute-start(bf16[4,32,1024]{2,1,0:T(8,128)(2,1)S(1)} %collective-permute-done.9.refs_3_), channel_id=1, source_target_pairs={{0,1},{1,0},{2,3},{3,2},{4,5},{5,4},{6,7},{7,6},{8,9},{9,8},{10,11... | collective-permute-start | bytes 786440 | tf_op jit(solution)/shard_map/ppermute | solution.py:26
  261.1 3.6 %collective-permute-start.14 = (bf16[4,32,1024]{2,1,0:T(8,128)(2,1)S(1)}, bf16[4,32,1024]{2,1,0:T(8,128)(2,1)S(1)}, u32[]{:S(2)}, u32[]{:S(2)}) collective-permute-start(bf16[4,32,1024]{2,1,0:T(8,128)(2,1)S(1)} %collective-permute-done.10.refs_2_), channel_id=1, source_target_pairs={{0,1},{1,0},{2,3},{3,2},{4,5},{5,4},{6,7},{7,6},{8,9},{9,8},{10,11... | collective-permute-start | bytes 786440 | tf_op jit(solution)/shard_map/ppermute | solution.py:26
  264.7 11.3 %collective-permute-start.21 = (bf16[72,512]{1,0:T(8,128)(2,1)S(1)}, bf16[72,512]{1,0:T(8,128)(2,1)S(1)}, u32[]{:S(2)}, u32[]{:S(2)}) collective-permute-start(bf16[72,512]{1,0:T(8,128)(2,1)S(1)} %add_add_fusion.1), channel_id=1, source_target_pairs={{0,64},{32,96},{64,0},{96,32},{1,65},{33,97},{65,1},{97,33},{2,66}... | collective-permute-start | bytes 221192 | tf_op jit(solution)/shard_map/ppermute | solution.py:37
  266.9 9.1 %collective-permute-start.22 = (bf16[72,512]{1,0:T(8,128)(2,1)S(1)}, bf16[72,512]{1,0:T(8,128)(2,1)S(1)}, u32[]{:S(2)}, u32[]{:S(2)}) collective-permute-start(bf16[72,512]{1,0:T(8,128)(2,1)S(1)} %add_add_fusion.1), channel_id=1, source_target_pairs={{0,32},{32,0},{64,96},{96,64},{1,33},{33,1},{65,97},{97,65},{2,34}... | collective-permute-start | bytes 221192 | tf_op jit(solution)/shard_map/ppermute | solution.py:37
  268.0 8.0 %collective-permute-start.23 = (bf16[72,512]{1,0:T(8,128)(2,1)S(1)}, bf16[72,512]{1,0:T(8,128)(2,1)S(1)}, u32[]{:S(2)}, u32[]{:S(2)}) collective-permute-start(bf16[72,512]{1,0:T(8,128)(2,1)S(1)} %add_add_fusion.1), channel_id=1, source_target_pairs={{0,96},{32,64},{64,32},{96,0},{1,97},{33,65},{65,33},{97,1},{2,98}... | collective-permute-start | bytes 221192 | tf_op jit(solution)/shard_map/ppermute | solution.py:37
  273.0 1.6 copy-start.2
  276.1 12.4 %collective-permute-start.24 = (bf16[256,1024]{1,0:T(8,128)(2,1)S(1)}, bf16[256,1024]{1,0:T(8,128)(2,1)S(1)}, u32[]{:S(2)}, u32[]{:S(2)}) collective-permute-start(bf16[256,1024]{1,0:T(8,128)(2,1)S(1)} %get-tuple-element.126), channel_id=1, source_target_pairs={{0,32},{32,64},{64,96},{96,0},{1,33},{33,65},{65,97},{97,1},{2,34}... | collective-permute-start | bytes 1572872 | tf_op jit(solution)/shard_map/ppermute | solution.py:44
  277.5 10.9 %collective-permute-start.25 = (bf16[256,1024]{1,0:T(8,128)(2,1)S(1)}, bf16[256,1024]{1,0:T(8,128)(2,1)S(1)}, u32[]{:S(2)}, u32[]{:S(2)}) collective-permute-start(bf16[256,1024]{1,0:T(8,128)(2,1)S(1)} %get-tuple-element.127), channel_id=1, source_target_pairs={{0,96},{32,0},{64,32},{96,64},{1,97},{33,1},{65,33},{97,65},{2,98}... | collective-permute-start | bytes 1572872 | tf_op jit(solution)/shard_map/ppermute | solution.py:44
  279.4 11.7 %collective-permute-start.26 = (bf16[256,1024]{1,0:T(8,128)(2,1)S(1)}, bf16[256,1024]{1,0:T(8,128)(2,1)S(1)}, u32[]{:S(2)}, u32[]{:S(2)}) collective-permute-start(bf16[256,1024]{1,0:T(8,128)(2,1)S(1)} %get-tuple-element.131), channel_id=1, source_target_pairs={{0,8},{8,16},{16,24},{24,0},{1,9},{9,17},{17,25},{25,1},{2,10},{10... | collective-permute-start | bytes 1572872 | tf_op jit(solution)/shard_map/ppermute | solution.py:44
  279.6 12.4 %collective-permute-start.27 = (bf16[256,1024]{1,0:T(8,128)(2,1)S(1)}, bf16[256,1024]{1,0:T(8,128)(2,1)S(1)}, u32[]{:S(2)}, u32[]{:S(2)}) collective-permute-start(bf16[256,1024]{1,0:T(8,128)(2,1)S(1)} %get-tuple-element.133), channel_id=1, source_target_pairs={{0,24},{8,0},{16,8},{24,16},{1,25},{9,1},{17,9},{25,17},{2,26},{10... | collective-permute-start | bytes 1572872 | tf_op jit(solution)/shard_map/ppermute | solution.py:44
  288.4 3.6 %copy-start.15 = (bf16[256,1024]{1,0:T(8,128)(2,1)}, bf16[256,1024]{1,0:T(8,128)(2,1)S(1)}, u32[]{:S(2)}) copy-start(bf16[256,1024]{1,0:T(8,128)(2,1)S(1)} %collective-permute-done.24.refs_1_.refs_2_) | copy-start | bytes 1572868
  288.4 3.6 %copy-start.16 = (bf16[256,1024]{1,0:T(8,128)(2,1)}, bf16[256,1024]{1,0:T(8,128)(2,1)S(1)}, u32[]{:S(2)}) copy-start(bf16[256,1024]{1,0:T(8,128)(2,1)S(1)} %collective-permute-done.25.refs_3_) | copy-start | bytes 1572868
  291.1 0.9 copy-start.17
  292.0 0.8 copy-start.18
  294.5 8.5 %collective-permute-start.28 = (bf16[128,1024]{1,0:T(8,128)(2,1)S(1)}, bf16[128,1024]{1,0:T(8,128)(2,1)S(1)}, u32[]{:S(2)}, u32[]{:S(2)}) collective-permute-start(bf16[128,1024]{1,0:T(8,128)(2,1)S(1)} %get-tuple-element.134), channel_id=1, source_target_pairs={{0,32},{32,64},{64,96},{96,0},{1,33},{33,65},{65,97},{97,1},{2,34}... | collective-permute-start | bytes 786440 | tf_op jit(solution)/shard_map/ppermute | solution.py:44
  294.6 8.4 %collective-permute-start.29 = (bf16[128,1024]{1,0:T(8,128)(2,1)S(1)}, bf16[128,1024]{1,0:T(8,128)(2,1)S(1)}, u32[]{:S(2)}, u32[]{:S(2)}) collective-permute-start(bf16[128,1024]{1,0:T(8,128)(2,1)S(1)} %get-tuple-element.135), channel_id=1, source_target_pairs={{0,96},{32,0},{64,32},{96,64},{1,97},{33,1},{65,33},{97,65},{2,98}... | collective-permute-start | bytes 786440 | tf_op jit(solution)/shard_map/ppermute | solution.py:44
  297.8 7.6 %collective-permute-start.30 = (bf16[128,1024]{1,0:T(8,128)(2,1)S(1)}, bf16[128,1024]{1,0:T(8,128)(2,1)S(1)}, u32[]{:S(2)}, u32[]{:S(2)}) collective-permute-start(bf16[128,1024]{1,0:T(8,128)(2,1)S(1)} %get-tuple-element.138), channel_id=1, source_target_pairs={{0,8},{8,16},{16,24},{24,0},{1,9},{9,17},{17,25},{25,1},{2,10},{10... | collective-permute-start | bytes 786440 | tf_op jit(solution)/shard_map/ppermute | solution.py:44
  298.8 6.7 %collective-permute-start.31 = (bf16[128,1024]{1,0:T(8,128)(2,1)S(1)}, bf16[128,1024]{1,0:T(8,128)(2,1)S(1)}, u32[]{:S(2)}, u32[]{:S(2)}) collective-permute-start(bf16[128,1024]{1,0:T(8,128)(2,1)S(1)} %get-tuple-element.139), channel_id=1, source_target_pairs={{0,24},{8,0},{16,8},{24,16},{1,25},{9,1},{17,9},{25,17},{2,26},{10... | collective-permute-start | bytes 786440 | tf_op jit(solution)/shard_map/ppermute | solution.py:44
  303.0 2.4 copy-start.19
  303.0 2.4 copy-start.20
  305.4 0.7 copy-start.21
  305.4 0.8 copy-start.22
Sparse Core Ops, SparseCore 0:
  101.3 27.3 all-gather.2
  130.4 30.8 all-gather.4
